TPU v7x, 128 devices: a whole 4x4x4 slice. The times are simulated.
128 devices in a mesh: gx: 8 (over z, x_hi), gy: 16 (over x_lo, y, core).
Axes of the slice: x: 4 (x_hi: 2, x_lo: 2; x = x_hi * 2 + x_lo), y: 4, z: 4, core: 2. Of those that a mesh axis runs over, the one named last changes fastest.
Arguments:
- velocity: bfloat16 [3, 64, 1024, 576], P(None, 'gx', 'gy'), may hold values from -6 to 6
- viscosity: bfloat16 [64, 1024, 576], P('gx', 'gy'), may hold values from 0.019897461 to 0.19921875
- tap_cell: int32 [128, 320], P(('gx', 'gy')), may hold values from 0 to 294911
- tap_block: int32 [128, 320], P(('gx', 'gy')), may hold values from 0 to 511
- block_slot: int32 [512], replicated, may hold values from 0 to 511, each once
Outputs:
- new_velocity: bfloat16 [3, 64, 1024, 576], P(None, 'gx', 'gy')
- epoch_max: float32 [512], P(('gx', 'gy'))
Inputs may be any that keep to these rules, and one draw needn't show every extreme that they name: `tap_cell`: each index lies in the brick of 8 x 64 x 576 cells of the device that holds the row, flattened with x slowest and z fastest.
All inputs are finite; a program needn't handle non-finite values.
Results may differ from a plain program's by a relative error of at most 0.0078.
Values may be sent and summed in bfloat16 or wider, within the bound.
No kernel may reach another device: no remote copies, remote signals or barrier semaphores. Data moves between devices by JAX's collectives and lax.ppermute only.
A program may use at most 64 MiB of HBM per device.

v0:
```python
import jax
import jax.numpy as jnp
from jax import lax
from jax.sharding import PartitionSpec as P

step_size = 0.3


def padded_2(x, sides, width):
    for axis, dim in sides:
        peers, length = (lax.axis_size(axis), x.shape[dim])
        up = [(i, (i + 1) % peers) for i in range(peers)]
        down = [(j, i) for i, j in up]
        last = lax.slice_in_dim(x, length - width, length, axis=dim)
        leading = lax.slice_in_dim(x, 0, width, axis=dim)
        before = lax.ppermute(last, axis, up)
        after = lax.ppermute(leading, axis, down)
        x = jnp.concatenate([before, x, after], axis=dim)
    return x


def shifted(field, step_x, step_y, step_z):
    return field[
        ...,
        1 + step_x : field.shape[-3] - 1 + step_x,
        1 + step_y : field.shape[-2] - 1 + step_y,
        1 + step_z : field.shape[-1] - 1 + step_z,
    ]


def advance(flow_pad, visc_pad):
    flow = flow_pad.astype(jnp.float32)
    viscous = visc_pad.astype(jnp.float32)
    flow = jnp.concatenate([jnp.zeros_like(flow[..., :1]), flow, flow[..., -1:]], axis=-1)
    viscous = jnp.concatenate([viscous[..., :1], viscous, viscous[..., -1:]], axis=-1)
    offsets = ((1, 0, 0), (0, 1, 0), (0, 0, 1))
    centre_visc = shifted(viscous, 0, 0, 0)
    centre = shifted(flow, 0, 0, 0)
    results = []
    for channel in range(3):
        centre_val = centre[channel]
        change = jnp.zeros_like(centre_val)
        for axis_id, (step_x, step_y, step_z) in enumerate(offsets):
            above_cell = shifted(flow[channel], step_x, step_y, step_z)
            below_cell = shifted(flow[channel], -step_x, -step_y, -step_z)
            visc_above = shifted(viscous, step_x, step_y, step_z)
            visc_below = shifted(viscous, -step_x, -step_y, -step_z)
            change = change + 0.5 * (centre_visc + visc_above) * (above_cell - centre_val)
            change = change - 0.5 * (centre_visc + visc_below) * (centre_val - below_cell)
            change = change - 0.5 * centre[axis_id] * (above_cell - below_cell)
        results.append((centre_val + step_size * change).astype(jnp.bfloat16))
    return jnp.stack(results, 0)


def faces(field):
    return padded_2(field, (("gx", 1), ("gy", 2)), 1)


def tap_energy(state, cells):
    energy = jnp.sum(jnp.square(state.astype(jnp.float32)), axis=0).reshape(-1)
    return energy[cells]


def body(velocity, viscosity, tap_cell, tap_block, block_slot):
    stacked = jnp.concatenate([velocity, viscosity[None]], axis=0)
    padded = faces(stacked)
    first_state = advance(padded[:3], padded[3])
    second = faces(first_state)
    final_state = advance(second, padded[3])
    cells = tap_cell[0]
    peaks = jnp.maximum(tap_energy(first_state, cells), tap_energy(final_state, cells))
    block_count = block_slot.shape[0]
    block_ids = jnp.arange(block_count, dtype=jnp.int32)
    partial_value = jnp.max(
        jnp.where(tap_block[0][:, None] == block_ids[None, :], peaks[:, None], 0.0), axis=0
    )
    slotted = jnp.max(
        jnp.where(block_slot[:, None] == block_ids[None, :], partial_value[:, None], 0.0), axis=0
    )
    groups = lax.axis_size(("gx", "gy"))
    per_device = block_count // groups
    received = lax.all_to_all(
        slotted.reshape(groups, per_device), ("gx", "gy"), split_axis=0, concat_axis=0, tiled=True
    )
    epoch_max = jnp.max(received, axis=0)
    return (final_state, epoch_max)


def solution(mesh):
    placed = (
        P(None, "gx", "gy", None),
        P("gx", "gy", None),
        P(("gx", "gy"), None),
        P(("gx", "gy"), None),
        P(),
    )
    return jax.shard_map(
        body,
        mesh=mesh,
        in_specs=placed,
        out_specs=(P(None, "gx", "gy", None), P(("gx", "gy"))),
        check_vma=False,
    )
```

profile of v0, /device:TPU:1, one launch (start us, length us, event | category | flops | bytes accessed | tf_op | source)
XLA Modules:
  0.0 116.1 jit_solution(15687045521905380479)
XLA Ops:
  0.6 1.4 %pad_maximum_fusion.8 = (bf16[4,1,64,576]{3,2,1,0:T(8,128)(2,1)S(1)}, bf16[4,1,64,576]{3,2,1,0:T(8,128)(2,1)S(1)}) fusion(bf16[1,8,64,576]{3,2,1,0:T(8,128)(2,1)} %bitcast.142, bf16[3,8,64,576]{3,2,1,0:T(8,128)(2,1)} %param.5), kind=kLoop, calls=%fused_computation.62 | loop fusion | flops 294912 | bytes 2949120 | tf_op jit(solution)/shard_map/slice | solution.py:14
  2.0 3.6 %collective-permute-start = (bf16[4,1,64,576]{3,2,1,0:T(8,128)(2,1)S(1)}, bf16[4,1,64,576]{3,2,1,0:T(8,128)(2,1)S(1)}, u32[]{:S(2)}, u32[]{:S(2)}) collective-permute-start(bf16[4,1,64,576]{3,2,1,0:T(8,128)(2,1)S(1)} %get-tuple-element.19), channel_id=1, source_target_pairs={{0,16},{16,32},{32,48},{48,64},{64,80},{80,96},{96,112},{112,0},{1... | collective-permute-start | bytes 884744 | tf_op jit(solution)/shard_map/ppermute | solution.py:16
  5.7 3.6 %collective-permute-start.1 = (bf16[4,1,64,576]{3,2,1,0:T(8,128)(2,1)S(1)}, bf16[4,1,64,576]{3,2,1,0:T(8,128)(2,1)S(1)}, u32[]{:S(2)}, u32[]{:S(2)}) collective-permute-start(bf16[4,1,64,576]{3,2,1,0:T(8,128)(2,1)S(1)} %get-tuple-element.20), channel_id=1, source_target_pairs={{16,0},{32,16},{48,32},{64,48},{80,64},{96,80},{112,96},{0,112},{1... | collective-permute-start | bytes 884744 | tf_op jit(solution)/shard_map/ppermute | solution.py:17
  9.3 7.3 %collective-permute-done = bf16[4,1,64,576]{3,2,1,0:T(8,128)(2,1)S(1)} collective-permute-done((bf16[4,1,64,576]{3,2,1,0:T(8,128)(2,1)S(1)}, bf16[4,1,64,576]{3,2,1,0:T(8,128)(2,1)S(1)}, u32[]{:S(2)}, u32[]{:S(2)}) %collective-permute-start) | collective-permute-done | bytes 294944 | tf_op jit(solution)/shard_map/ppermute | solution.py:16
  16.6 4.8 %collective-permute-done.1 = bf16[4,1,64,576]{3,2,1,0:T(8,128)(2,1)S(1)} collective-permute-done((bf16[4,1,64,576]{3,2,1,0:T(8,128)(2,1)S(1)}, bf16[4,1,64,576]{3,2,1,0:T(8,128)(2,1)S(1)}, u32[]{:S(2)}, u32[]{:S(2)}) %collective-permute-start.1) | collective-permute-done | bytes 294944 | tf_op jit(solution)/shard_map/ppermute | solution.py:17
  21.4 0.8 pad_maximum_fusion.12
  22.3 2.7 %collective-permute-start.2 = (bf16[4,10,1,576]{3,2,1,0:T(2,128)(2,1)}, bf16[4,10,1,576]{3,2,1,0:T(2,128)(2,1)S(1)}, u32[]{:S(2)}, u32[]{:S(2)}) collective-permute-start(bf16[4,10,1,576]{3,2,1,0:T(2,128)(2,1)} %get-tuple-element.17), channel_id=1, source_target_pairs={{0,1},{1,2},{2,3},{3,4},{4,5},{5,6},{6,7},{7,8},{8,9},{9,10},{10,1... | collective-permute-start | bytes 138248 | tf_op jit(solution)/shard_map/ppermute | solution.py:16
  25.0 2.0 %collective-permute-done.2 = bf16[4,10,1,576]{3,2,1,0:T(2,128)(2,1)S(1)} collective-permute-done((bf16[4,10,1,576]{3,2,1,0:T(2,128)(2,1)}, bf16[4,10,1,576]{3,2,1,0:T(2,128)(2,1)S(1)}, u32[]{:S(2)}, u32[]{:S(2)}) %collective-permute-start.2) | collective-permute-done | bytes 46112 | tf_op jit(solution)/shard_map/ppermute | solution.py:16
  27.0 2.6 %collective-permute-done.3 = bf16[4,10,1,576]{3,2,1,0:T(2,128)(2,1)S(1)} collective-permute-done((bf16[4,10,1,576]{3,2,1,0:T(2,128)(2,1)}, bf16[4,10,1,576]{3,2,1,0:T(2,128)(2,1)S(1)}, u32[]{:S(2)}, u32[]{:S(2)}) %collective-permute-start.3) | collective-permute-done | bytes 46112 | tf_op jit(solution)/shard_map/ppermute | solution.py:17
  29.6 3.8 %pad_maximum_fusion.2 = bf16[4,10,66,576]{3,2,1,0:T(8,128)(2,1)S(1)} fusion(bf16[4,10,1,576]{3,2,1,0:T(2,128)(2,1)S(1)} %collective-permute-done.3, bf16[4,1,64,576]{3,2,1,0:T(8,128)(2,1)S(1)} %collective-permute-done.1, bf16[1,8,64,576]{3,2,1,0:T(8,128)(2,1)S(1)} %bitcast.144, bf16[3,8,64,576]{3,2,1,0:T(8,128)(2,1)S(1)} %copy-done.8, ...), kind=kLoop, calls=%fused_computation.6 | loop fusion | flops 18247680 | bytes 6082560 | tf_op jit(solution)/shard_map/concatenate | solution.py:18
  33.4 0.4 slice_convert_fusion
  33.8 0.3 slice.376
  34.1 1.8 %pad_maximum_fusion = f32[3,10,66,578]{3,2,1,0:T(8,128)S(1)} fusion(f32[3,10,66,1]{3,2,1,0:T(8,128)S(1)} %slice.376, f32[3,10,66,576]{3,2,1,0:T(8,128)S(1)} %slice_convert_fusion, f32[578]{0:T(1024)S(1)} %pad.25.clone), kind=kLoop, calls=%fused_computation.2 | loop fusion | flops 2288880 | bytes 9149912 | tf_op jit(solution)/shard_map/concatenate | solution.py:34
  35.9 0.4 slice_bitcast_fusion.4
  36.3 0.2 fusion.14
  36.7 5.1 %fusion.15 = (bf16[1,8,64,576]{3,2,1,0:T(8,128)(2,1)S(1)}, f32[8,64,576]{2,1,0:T(8,128)S(1)}, f32[8,64,576]{2,1,0:T(8,128)S(1)}, f32[8,64,576]{2,1,0:T(8,128)S(1...) fusion(f32[3,10,66,576]{3,2,1,0:T(8,128)S(1)} %slice_convert_fusion, ...), kind=kLoop, calls=%fused_computation.55 | loop fusion | flops 13565952 | bytes 28598272 | tf_op jit(solution)/shard_map/stack | solution.py:52
  41.9 2.9 %fusion.16 = bf16[1,8,64,576]{3,2,1,0:T(8,128)(2,1)S(1)} fusion(f32[3,10,66,576]{3,2,1,0:T(8,128)S(1)} %slice_convert_fusion, f32[8,64,576]{2,1,0:T(8,128)S(1)} %get-tuple-element.10, f32[10,66,578]{2,1,0:T(8,128)S(1)} %get-tuple-element.14, f32[8,64,576]{2,1,0:T(8,128)S(1)} %get-tuple-element.9, f32[8,64,576]{2,1,0:T(8,128)S(1)} %get-tuple-element.8, ...), kind=kLoop, calls=%fused_computation.56 | loop fusion | flops 9437184 | bytes 18284544 | tf_op jit(solution)/shard_map/stack | solution.py:52
  44.9 2.8 %fusion.17 = bf16[1,8,64,576]{3,2,1,0:T(8,128)(2,1)S(1)} fusion(f32[8,64,576]{2,1,0:T(8,128)S(1)} %get-tuple-element.10, f32[10,66,578]{2,1,0:T(8,128)S(1)} %get-tuple-element.15, f32[8,64,576]{2,1,0:T(8,128)S(1)} %get-tuple-element.9, f32[3,10,66,576]{3,2,1,0:T(8,128)S(1)} %slice_convert_fusion, f32[8,64,576]{2,1,0:T(8,128)S(1)} %get-tuple-element.8, ...), kind=kLoop, calls=%fused_computation.57 | loop fusion | flops 9437184 | bytes 18284544 | tf_op jit(solution)/shard_map/stack | solution.py:52
  47.7 0.4 pad_maximum_fusion.3
  48.1 2.8 %collective-permute-start.4 = (bf16[3,1,64,576]{3,2,1,0:T(8,128)(2,1)S(1)}, bf16[3,1,64,576]{3,2,1,0:T(8,128)(2,1)S(1)}, u32[]{:S(2)}, u32[]{:S(2)}) collective-permute-start(bf16[3,1,64,576]{3,2,1,0:T(8,128)(2,1)S(1)} %get-tuple-element.23), channel_id=1, source_target_pairs={{0,16},{16,32},{32,48},{48,64},{64,80},{80,96},{96,112},{112,0},{1... | collective-permute-start | bytes 663560 | tf_op jit(solution)/shard_map/ppermute | solution.py:16
  50.9 2.3 %collective-permute-start.5 = (bf16[3,1,64,576]{3,2,1,0:T(8,128)(2,1)S(1)}, bf16[3,1,64,576]{3,2,1,0:T(8,128)(2,1)S(1)}, u32[]{:S(2)}, u32[]{:S(2)}) collective-permute-start(bf16[3,1,64,576]{3,2,1,0:T(8,128)(2,1)S(1)} %get-tuple-element.24), channel_id=1, source_target_pairs={{16,0},{32,16},{48,32},{64,48},{80,64},{96,80},{112,96},{0,112},{1... | collective-permute-start | bytes 663560 | tf_op jit(solution)/shard_map/ppermute | solution.py:17
  53.3 5.3 %collective-permute-done.4 = bf16[3,1,64,576]{3,2,1,0:T(8,128)(2,1)S(1)} collective-permute-done((bf16[3,1,64,576]{3,2,1,0:T(8,128)(2,1)S(1)}, bf16[3,1,64,576]{3,2,1,0:T(8,128)(2,1)S(1)}, u32[]{:S(2)}, u32[]{:S(2)}) %collective-permute-start.4) | collective-permute-done | bytes 221216 | tf_op jit(solution)/shard_map/ppermute | solution.py:16
  58.6 4.5 %collective-permute-done.5 = bf16[3,1,64,576]{3,2,1,0:T(8,128)(2,1)S(1)} collective-permute-done((bf16[3,1,64,576]{3,2,1,0:T(8,128)(2,1)S(1)}, bf16[3,1,64,576]{3,2,1,0:T(8,128)(2,1)S(1)}, u32[]{:S(2)}, u32[]{:S(2)}) %collective-permute-start.5) | collective-permute-done | bytes 221216 | tf_op jit(solution)/shard_map/ppermute | solution.py:17
  63.1 0.7 copy-done.12
  63.9 0.8 pad_maximum_fusion.17
  64.7 1.0 collective-permute-start.6
  65.7 0.5 collective-permute-start.7
  66.2 1.5 %multiply_reduce_fusion.1 = f32[8,64,576]{2,1,0:T(8,128)} fusion(bf16[1,8,64,576]{3,2,1,0:T(8,128)(2,1)S(1)} %fusion.17, bf16[1,8,64,576]{3,2,1,0:T(8,128)(2,1)S(1)} %fusion.16, bf16[1,8,64,576]{3,2,1,0:T(8,128)(2,1)S(1)} %get-tuple-element.4), kind=kLoop, calls=%fused_computation.5 | loop fusion | flops 4128768 | bytes 2949120 | tf_op jit(solution)/shard_map/reduce_sum | solution.py:60
  67.7 2.8 %reshape.52 = f32[294912]{0:T(1024)} reshape(f32[8,64,576]{2,1,0:T(8,128)} %multiply_reduce_fusion.1) | data formatting | bytes 2359296 | tf_op jit(solution)/shard_map/reshape | solution.py:60
  70.5 4.5 %gather_fusion = f32[320]{0:T(512)S(1)} fusion(f32[294912]{0:T(1024)} %reshape.52, s32[1024]{0:T(1024)S(1)} %pad_clamp_fusion), kind=kCustom, calls=%fused_computation | custom fusion | bytes 3840 | tf_op jit(solution)/shard_map/gather | solution.py:61
  75.0 3.7 %maximum_convert_fusion = f32[3,10,66,576]{3,2,1,0:T(8,128)S(1)} fusion(bf16[3,10,1,576]{3,2,1,0:T(2,128)(2,1)} %collective-permute-done.7, bf16[3,1,64,576]{3,2,1,0:T(8,128)(2,1)} %copy-done.12, bf16[1,8,64,576]{3,2,1,0:T(8,128)(2,1)} %copy-done.9, bf16[1,8,64,576]{3,2,1,0:T(8,128)(2,1)S(1)} %fusion.16, bf16[1,8,64,576]{3,2,1,0:T(8,128)(2,1)} %copy-done.10, ...), kind=kLoop, calls=%fused_computation.8 | loop fusion | flops 15966720 | bytes 6842880 | tf_op jit(solution)/shard_map/convert_element_type | solution.py:32
  78.7 0.3 slice.408
  79.1 1.8 %pad_maximum_fusion.1 = f32[3,10,66,578]{3,2,1,0:T(8,128)S(1)} fusion(f32[3,10,66,1]{3,2,1,0:T(8,128)S(1)} %slice.408, f32[3,10,66,576]{3,2,1,0:T(8,128)S(1)} %maximum_convert_fusion, f32[578]{0:T(1024)S(1)} %pad.25.clone), kind=kLoop, calls=%fused_computation.3 | loop fusion | flops 2288880 | bytes 9149912 | tf_op jit(solution)/shard_map/concatenate | solution.py:34
  80.9 0.4 slice_bitcast_fusion.2
  81.3 0.9 copy-done.1
  82.2 0.4 copy-done.3
  82.6 0.4 copy-done.5
  83.0 0.4 copy-done.7
  83.4 2.9 %fusion.18 = bf16[1,8,64,576]{3,2,1,0:T(8,128)(2,1)S(1)} fusion(f32[3,10,66,576]{3,2,1,0:T(8,128)S(1)} %maximum_convert_fusion, f32[8,64,576]{2,1,0:T(8,128)S(1)} %copy-done.7, f32[10,66,578]{2,1,0:T(8,128)S(1)} %get-tuple-element.11, f32[8,64,576]{2,1,0:T(8,128)S(1)} %copy-done.5, f32[8,64,576]{2,1,0:T(8,128)S(1)} %copy-done.3, ...), kind=kLoop, calls=%fused_computation.58 | loop fusion | flops 9437184 | bytes 18284544 | tf_op jit(solution)/shard_map/stack | solution.py:52
  86.3 2.9 %fusion.19 = bf16[1,8,64,576]{3,2,1,0:T(8,128)(2,1)S(1)} fusion(f32[3,10,66,576]{3,2,1,0:T(8,128)S(1)} %maximum_convert_fusion, f32[8,64,576]{2,1,0:T(8,128)S(1)} %copy-done.7, f32[10,66,578]{2,1,0:T(8,128)S(1)} %get-tuple-element.13, f32[8,64,576]{2,1,0:T(8,128)S(1)} %copy-done.5, f32[8,64,576]{2,1,0:T(8,128)S(1)} %copy-done.3, ...), kind=kLoop, calls=%fused_computation.59 | loop fusion | flops 9437184 | bytes 18284544 | tf_op jit(solution)/shard_map/stack | solution.py:52
  89.2 2.8 %fusion.20 = bf16[1,8,64,576]{3,2,1,0:T(8,128)(2,1)S(1)} fusion(f32[8,64,576]{2,1,0:T(8,128)S(1)} %copy-done.7, f32[10,66,578]{2,1,0:T(8,128)S(1)} %get-tuple-element.12, f32[8,64,576]{2,1,0:T(8,128)S(1)} %copy-done.5, f32[3,10,66,576]{3,2,1,0:T(8,128)S(1)} %maximum_convert_fusion, f32[8,64,576]{2,1,0:T(8,128)S(1)} %copy-done.3, ...), kind=kLoop, calls=%fused_computation.60 | loop fusion | flops 9437184 | bytes 18284544 | tf_op jit(solution)/shard_map/stack | solution.py:52
  92.0 1.9 %multiply_reduce_fusion = (f32[8,64,576]{2,1,0:T(8,128)S(1)}, bf16[3,8,64,576]{3,2,1,0:T(8,128)(2,1)}) fusion(bf16[1,8,64,576]{3,2,1,0:T(8,128)(2,1)S(1)} %fusion.20, bf16[1,8,64,576]{3,2,1,0:T(8,128)(2,1)S(1)} %fusion.19, bf16[1,8,64,576]{3,2,1,0:T(8,128)(2,1)S(1)} %fusion.18), kind=kLoop, calls=%fused_computation.4 | loop fusion | flops 4128768 | bytes 4718592 | tf_op jit(solution)/shard_map/reduce_sum | solution.py:60
  93.9 0.6 reshape.53
  94.5 2.2 %gather_fusion.1 = f32[320]{0:T(512)S(1)} fusion(f32[294912]{0:T(1024)S(1)} %reshape.53, s32[1024]{0:T(1024)S(1)} %pad_clamp_fusion), kind=kCustom, calls=%fused_computation.1 | custom fusion | bytes 3840 | tf_op jit(solution)/shard_map/gather | solution.py:61
  96.7 0.2 select_reduce_fusion.1
  96.9 0.2 select_reduce_fusion
  97.2 18.2 %all_to_all.9 = f32[128,1,4]{2,1,0:T(1,128)S(1)} all-to-all(f32[128,1,4]{2,1,0:T(1,128)S(1)} %bitcast.146), channel_id=1, replica_groups=mesh['gx'=8,'gy'=16] {'gx','gy'}, dimensions={0} | all-to-all | bytes 4096 | tf_op jit(solution)/shard_map/all_to_all | solution.py:82
  115.4 0.7 reduce_max.29
  (38 shorter events, 0.4 us)
Async XLA Ops:
  0.6 20.8 %copy-start.8 = (bf16[3,8,64,576]{3,2,1,0:T(8,128)(2,1)S(1)}, bf16[3,8,64,576]{3,2,1,0:T(8,128)(2,1)}, u32[]{:S(2)}) copy-start(bf16[3,8,64,576]{3,2,1,0:T(8,128)(2,1)} %param.5) | copy-start | bytes 5308420
  0.6 20.8 %copy-start.11 = (bf16[8,64,576]{2,1,0:T(8,128)(2,1)S(1)}, bf16[8,64,576]{2,1,0:T(8,128)(2,1)}, u32[]{:S(2)}) copy-start(bf16[8,64,576]{2,1,0:T(8,128)(2,1)} %param.6) | copy-start | bytes 1769476
  2.0 14.6 %collective-permute-start = (bf16[4,1,64,576]{3,2,1,0:T(8,128)(2,1)S(1)}, bf16[4,1,64,576]{3,2,1,0:T(8,128)(2,1)S(1)}, u32[]{:S(2)}, u32[]{:S(2)}) collective-permute-start(bf16[4,1,64,576]{3,2,1,0:T(8,128)(2,1)S(1)} %get-tuple-element.19), channel_id=1, source_target_pairs={{0,16},{16,32},{32,48},{48,64},{64,80},{80,96},{96,112},{112,0},{1... | collective-permute-start | bytes 884744 | tf_op jit(solution)/shard_map/ppermute | solution.py:16
  5.7 19.3 %copy-start.15 = (s32[1,320]{1,0:T(1,128)S(1)}, s32[1,320]{1,0:T(1,128)}, u32[]{:S(2)}) copy-start(s32[1,320]{1,0:T(1,128)} %param.8) | copy-start | bytes 3844
  5.7 15.7 %collective-permute-start.1 = (bf16[4,1,64,576]{3,2,1,0:T(8,128)(2,1)S(1)}, bf16[4,1,64,576]{3,2,1,0:T(8,128)(2,1)S(1)}, u32[]{:S(2)}, u32[]{:S(2)}) collective-permute-start(bf16[4,1,64,576]{3,2,1,0:T(8,128)(2,1)S(1)} %get-tuple-element.20), channel_id=1, source_target_pairs={{16,0},{32,16},{48,32},{64,48},{80,64},{96,80},{112,96},{0,112},{1... | collective-permute-start | bytes 884744 | tf_op jit(solution)/shard_map/ppermute | solution.py:17
  22.3 4.7 %collective-permute-start.2 = (bf16[4,10,1,576]{3,2,1,0:T(2,128)(2,1)}, bf16[4,10,1,576]{3,2,1,0:T(2,128)(2,1)S(1)}, u32[]{:S(2)}, u32[]{:S(2)}) collective-permute-start(bf16[4,10,1,576]{3,2,1,0:T(2,128)(2,1)} %get-tuple-element.17), channel_id=1, source_target_pairs={{0,1},{1,2},{2,3},{3,4},{4,5},{5,6},{6,7},{7,8},{8,9},{9,10},{10,1... | collective-permute-start | bytes 138248 | tf_op jit(solution)/shard_map/ppermute | solution.py:16
  25.0 4.6 %collective-permute-start.3 = (bf16[4,10,1,576]{3,2,1,0:T(2,128)(2,1)}, bf16[4,10,1,576]{3,2,1,0:T(2,128)(2,1)S(1)}, u32[]{:S(2)}, u32[]{:S(2)}) collective-permute-start(bf16[4,10,1,576]{3,2,1,0:T(2,128)(2,1)} %get-tuple-element.18), channel_id=1, source_target_pairs={{1,0},{2,1},{3,2},{4,3},{5,4},{6,5},{7,6},{8,7},{9,8},{10,9},{11,1... | collective-permute-start | bytes 138248 | tf_op jit(solution)/shard_map/ppermute | solution.py:17
  41.8 3.0 %copy-start = (f32[8,64,576]{2,1,0:T(8,128)}, f32[8,64,576]{2,1,0:T(8,128)S(1)}, u32[]{:S(2)}) copy-start(f32[8,64,576]{2,1,0:T(8,128)S(1)} %get-tuple-element.7) | copy-start | bytes 3538948
  41.8 3.0 %copy-start.2 = (f32[8,64,576]{2,1,0:T(8,128)}, f32[8,64,576]{2,1,0:T(8,128)S(1)}, u32[]{:S(2)}) copy-start(f32[8,64,576]{2,1,0:T(8,128)S(1)} %get-tuple-element.8) | copy-start | bytes 3538948
  41.9 3.0 %copy-start.4 = (f32[8,64,576]{2,1,0:T(8,128)}, f32[8,64,576]{2,1,0:T(8,128)S(1)}, u32[]{:S(2)}) copy-start(f32[8,64,576]{2,1,0:T(8,128)S(1)} %get-tuple-element.9) | copy-start | bytes 3538948
  41.9 3.0 %copy-start.6 = (f32[8,64,576]{2,1,0:T(8,128)}, f32[8,64,576]{2,1,0:T(8,128)S(1)}, u32[]{:S(2)}) copy-start(f32[8,64,576]{2,1,0:T(8,128)S(1)} %get-tuple-element.10) | copy-start | bytes 3538948
  41.9 24.3 %copy-start.10 = (bf16[1,8,64,576]{3,2,1,0:T(8,128)(2,1)}, bf16[1,8,64,576]{3,2,1,0:T(8,128)(2,1)S(1)}, u32[]{:S(2)}) copy-start(bf16[1,8,64,576]{3,2,1,0:T(8,128)(2,1)S(1)} %get-tuple-element.4) | copy-start | bytes 1769476
  47.7 18.5 %copy-start.9 = (bf16[1,8,64,576]{3,2,1,0:T(8,128)(2,1)}, bf16[1,8,64,576]{3,2,1,0:T(8,128)(2,1)S(1)}, u32[]{:S(2)}) copy-start(bf16[1,8,64,576]{3,2,1,0:T(8,128)(2,1)S(1)} %fusion.17) | copy-start | bytes 1769476
  47.7 5.6 %copy-start.14 = (s32[1,320]{1,0:T(1,128)S(1)}, s32[1,320]{1,0:T(1,128)}, u32[]{:S(2)}) copy-start(s32[1,320]{1,0:T(1,128)} %param.7) | copy-start | bytes 3844
  48.1 10.5 %collective-permute-start.4 = (bf16[3,1,64,576]{3,2,1,0:T(8,128)(2,1)S(1)}, bf16[3,1,64,576]{3,2,1,0:T(8,128)(2,1)S(1)}, u32[]{:S(2)}, u32[]{:S(2)}) collective-permute-start(bf16[3,1,64,576]{3,2,1,0:T(8,128)(2,1)S(1)} %get-tuple-element.23), channel_id=1, source_target_pairs={{0,16},{16,32},{32,48},{48,64},{64,80},{80,96},{96,112},{112,0},{1... | collective-permute-start | bytes 663560 | tf_op jit(solution)/shard_map/ppermute | solution.py:16
  50.9 12.2 %collective-permute-start.5 = (bf16[3,1,64,576]{3,2,1,0:T(8,128)(2,1)S(1)}, bf16[3,1,64,576]{3,2,1,0:T(8,128)(2,1)S(1)}, u32[]{:S(2)}, u32[]{:S(2)}) collective-permute-start(bf16[3,1,64,576]{3,2,1,0:T(8,128)(2,1)S(1)} %get-tuple-element.24), channel_id=1, source_target_pairs={{16,0},{32,16},{48,32},{64,48},{80,64},{96,80},{112,96},{0,112},{1... | collective-permute-start | bytes 663560 | tf_op jit(solution)/shard_map/ppermute | solution.py:17
  63.1 0.7 copy-start.12
  64.7 10.3 %collective-permute-start.6 = (bf16[3,10,1,576]{3,2,1,0:T(2,128)(2,1)}, bf16[3,10,1,576]{3,2,1,0:T(2,128)(2,1)}, u32[]{:S(2)}, u32[]{:S(2)}) collective-permute-start(bf16[3,10,1,576]{3,2,1,0:T(2,128)(2,1)} %get-tuple-element.21), channel_id=1, source_target_pairs={{0,1},{1,2},{2,3},{3,4},{4,5},{5,6},{6,7},{7,8},{8,9},{9,10},{10,1... | collective-permute-start | bytes 103688 | tf_op jit(solution)/shard_map/ppermute | solution.py:16
  65.7 9.3 %collective-permute-start.7 = (bf16[3,10,1,576]{3,2,1,0:T(2,128)(2,1)}, bf16[3,10,1,576]{3,2,1,0:T(2,128)(2,1)}, u32[]{:S(2)}, u32[]{:S(2)}) collective-permute-start(bf16[3,10,1,576]{3,2,1,0:T(2,128)(2,1)} %get-tuple-element.22), channel_id=1, source_target_pairs={{1,0},{2,1},{3,2},{4,3},{5,4},{6,5},{7,6},{8,7},{9,8},{10,9},{11,1... | collective-permute-start | bytes 103688 | tf_op jit(solution)/shard_map/ppermute | solution.py:17
  80.9 1.3 %copy-start.1 = (f32[8,64,576]{2,1,0:T(8,128)S(1)}, f32[8,64,576]{2,1,0:T(8,128)}, u32[]{:S(2)}) copy-start(f32[8,64,576]{2,1,0:T(8,128)} %copy-done) | copy-start | bytes 3538948
  80.9 1.7 %copy-start.3 = (f32[8,64,576]{2,1,0:T(8,128)S(1)}, f32[8,64,576]{2,1,0:T(8,128)}, u32[]{:S(2)}) copy-start(f32[8,64,576]{2,1,0:T(8,128)} %copy-done.2) | copy-start | bytes 3538948
  80.9 2.1 %copy-start.5 = (f32[8,64,576]{2,1,0:T(8,128)S(1)}, f32[8,64,576]{2,1,0:T(8,128)}, u32[]{:S(2)}) copy-start(f32[8,64,576]{2,1,0:T(8,128)} %copy-done.4) | copy-start | bytes 3538948
  80.9 2.5 %copy-start.7 = (f32[8,64,576]{2,1,0:T(8,128)S(1)}, f32[8,64,576]{2,1,0:T(8,128)}, u32[]{:S(2)}) copy-start(f32[8,64,576]{2,1,0:T(8,128)} %copy-done.6) | copy-start | bytes 3538948
  94.5 2.4 %copy-start.13 = (s32[512]{0:T(512)S(1)}, s32[512]{0:T(512)}, u32[]{:S(2)}) copy-start(s32[512]{0:T(512)} %param.9) | copy-start | bytes 6148
where the time goes:
time: 116 us
  other arithmetic  39.1 us (34%)
  waiting for transfers between devices  26.6 us (23%)
  blocking collectives  18.2 us (16%)
  starting transfers between devices  16.6 us (14%)
  local copies, waits for them, and re-layouts  14.7 us (13%)
    another operation x7, other arithmetic, advance(): return jnp.stack(results, 0)  19.8 us
    all_to_all x1, blocking collectives, body(): lax.all_to_all(slotted.reshape(groups, per_device), ('gx', 'gy'), split_a...  18.2 us
    ppermute x4, waiting for transfers between devices, padded_2(): before = lax.ppermute(last, axis, up)  14.7 us
    ppermute x4, waiting for transfers between devices, padded_2(): after = lax.ppermute(leading, axis, down)  11.9 us
    ppermute x4, starting transfers between devices, padded_2(): before = lax.ppermute(last, axis, up)  10.2 us
    gather x2, local copies, waits for them, and re-layouts, tap_energy(): return energy[cells]  6.75 us
    ppermute x4, starting transfers between devices, padded_2(): after = lax.ppermute(leading, axis, down)  6.39 us
    convert_element_type x2, other arithmetic, advance(): flow = flow_pad.astype(jnp.float32)  4.07 us
  transfers between devices with their start and end apart: 8, of which 6 were waited for; matrix products, arithmetic and copies ran while one was open for 8% of the time, Pallas kernels for 0%

commit v1 on v0

v1 whole, which is shorter than its diff:
```python
import jax
import jax.numpy as jnp
from jax import lax
from jax.experimental import pallas as pl
from jax.experimental.pallas import tpu as pltpu
from jax.sharding import PartitionSpec as P

F32 = jnp.float32
BF16 = jnp.bfloat16
HALF = 0.15
TOP = 8
CHUNK = 16
PADDED = 640


def put(pad, field, x, row, value, low):
    rows, nz = value.shape
    pad[field, x, row : row + rows, :nz] = value
    lane = lax.broadcasted_iota(jnp.int32, (rows, PADDED - nz), 1)
    above = jnp.broadcast_to(value[:, nz - 1 : nz], lane.shape)
    below = jnp.broadcast_to(value[:, :1], lane.shape) if low else jnp.zeros(lane.shape, F32)
    pad[field, x, row : row + rows, nz:] = jnp.where(lane == PADDED - nz - 1, below, above)


def put_layer(pad, x, read_velocity, read_viscosity, ny):
    for k in range(0, ny, CHUNK):
        for c in range(3):
            put(pad, c, x, TOP + k, read_velocity(c, k).astype(F32), False)
        if read_viscosity is not None:
            put(pad, 3, x, TOP + k, read_viscosity(k).astype(F32) * HALF, True)


def update(pad, x, row):
    here = [pad[f, x, row : row + CHUNK, :] for f in range(4)]
    total = [here[0], here[1], here[2]]
    for d in range(3):
        drift = here[d] * HALF
        if d == 2:
            above = [pltpu.roll(v, PADDED - 1, 1) for v in here]
            high = above[3] + here[3]
            low = pltpu.roll(high, 1, 1)
            ups = [above[c] - here[c] for c in range(3)]
            downs = [pltpu.roll(u, 1, 1) for u in ups]
        else:
            if d == 0:
                above = [pad[f, x + 1, row : row + CHUNK, :] for f in range(4)]
                below = [pad[f, x - 1, row : row + CHUNK, :] for f in range(4)]
            else:
                above = [pad[f, x, row + 1 : row + 1 + CHUNK, :] for f in range(4)]
                below = [pad[f, x, row - 1 : row - 1 + CHUNK, :] for f in range(4)]
            high = above[3] + here[3]
            low = below[3] + here[3]
            ups = [above[c] - here[c] for c in range(3)]
            downs = [here[c] - below[c] for c in range(3)]
        plus = high - drift
        minus = low + drift
        for c in range(3):
            total[c] = total[c] + (plus * ups[c] - minus * downs[c])
    return total


def first_step(vel, visc, ylo, yhi, s1, edge_lo, edge_hi, part, rows, pad):
    _, nx, ny, nz = vel.shape

    def fill(x, _):
        put_layer(pad, x + 1, lambda c, k: vel[c, x, k : k + CHUNK, :], lambda k: visc[x, k : k + CHUNK, :], ny)
        return 0

    lax.fori_loop(0, nx, fill, 0)
    for ghost, row in ((ylo, TOP - 1), (yhi, TOP + ny)):
        for f in range(4):
            value = ghost[f].astype(F32) * (HALF if f == 3 else 1.0)
            for x in range(nx):
                put(pad, f, x + 1, row, value[x : x + 1], f == 3)
    pad[:, 0] = pad[:, 1]
    pad[:, nx + 1] = pad[:, nx]

    def layer(x, side):
        for k in range(0, ny, CHUNK):
            new = update(pad, x + 1, TOP + k)
            for c in range(3):
                value = new[c][:, :nz]
                s1[c, x, k : k + CHUNK, :] = value.astype(BF16)
                if side is not None:
                    (edge_lo, edge_hi)[side][c, k : k + CHUNK, :] = value.astype(BF16)
                    part[side, c, k : k + CHUNK, :] = value
                if k == 0:
                    rows[0, c, pl.ds(x, 1), :] = value[:1]
                if k == ny - CHUNK:
                    rows[1, c, pl.ds(x, 1), :] = value[CHUNK - 1 :]

    layer(0, 0)
    layer(nx - 1, 1)

    def middle(x, _):
        layer(x, None)
        return 0

    lax.fori_loop(1, nx - 1, middle, 0)


def first_edges(part, own_lo, own_hi, alo, ahi, rows, edges, extra, face_lo, face_hi):
    _, _, ny, nz = part.shape
    nx = rows.shape[2]
    faces = [[rows[i, c] for c in range(3)] for i in range(2)]
    line = lax.broadcasted_iota(jnp.int32, (nx, nz), 0)
    for side, (own, ghost) in enumerate(((own_lo, alo), (own_hi, ahi))):
        sign = 1.0 if side else -1.0
        for k in range(0, ny, CHUNK):
            mine = [own[f, k : k + CHUNK, :].astype(F32) for f in range(4)]
            far = [ghost[f, k : k + CHUNK, :].astype(F32) for f in range(4)]
            both = (mine[3] + far[3]) * HALF
            near_coef = both - sign * HALF * mine[0]
            far_coef = both + sign * HALF * far[0]
            for c in range(3):
                gap = far[c] - mine[c]
                value = part[side, c, k : k + CHUNK, :] + near_coef * gap
                edges[side, c, k : k + CHUNK, :] = value.astype(BF16)
                extra[side, c, k : k + CHUNK, :] = -far_coef * gap
                x = (nx - 1) * side
                if k == 0:
                    faces[0][c] = jnp.where(line == x, jnp.broadcast_to(value[:1], line.shape), faces[0][c])
                if k == ny - CHUNK:
                    faces[1][c] = jnp.where(line == x, jnp.broadcast_to(value[CHUNK - 1 :], line.shape), faces[1][c])
    for c in range(3):
        face_lo[c] = faces[0][c].astype(BF16)
        face_hi[c] = faces[1][c].astype(BF16)


def energies(hot, states, z, nz):
    total = None
    for state in states:
        value = jnp.dot(hot, state, preferred_element_type=F32)
        total = value * value if total is None else total + value * value
    lane = lax.broadcasted_iota(jnp.int32, total.shape, 1)
    return jnp.max(jnp.where(lane == z, total, 0.0), axis=1, keepdims=True)


def second_step(s1, edges, visc, alo, ahi, ylo, yhi, row_of, z_of, late_of, block_of, slots,
                s2, quasi, quasi_rows, blocks, coef_x, coef_y, hot_late, slot_of, peaks, pad, state):
    _, nx, ny, nz = s1.shape

    def fill(x, _):
        put_layer(pad, x + 1, lambda c, k: s1[c, x, k : k + CHUNK, :], lambda k: visc[x, k : k + CHUNK, :], ny)
        return 0

    lax.fori_loop(1, nx - 1, fill, 0)
    for side, ghost in enumerate((alo, ahi)):
        x = (nx - 1) * side
        put_layer(pad, x + 1, lambda c, k: edges[side, c, k : k + CHUNK, :], lambda k: visc[x, k : k + CHUNK, :], ny)
        outer = (nx + 1) * side
        pad[0:3, outer] = jnp.zeros((3,) + pad.shape[2:], F32)
        for k in range(0, ny, CHUNK):
            put(pad, 3, outer, TOP + k, ghost[3, k : k + CHUNK, :].astype(F32) * HALF, True)
    for ghost, row in ((ylo, TOP - 1), (yhi, TOP + ny)):
        value = ghost[3].astype(F32) * HALF
        for x in range(nx):
            put(pad, 3, x + 1, row, value[x : x + 1], True)
            for c in range(3):
                pad[c, x + 1, row : row + 1, :] = jnp.zeros((1, PADDED), F32)

    for side in range(2):
        sign = 1.0 if side else -1.0
        x, outer = 1 + (nx - 1) * side, (nx + 1) * side
        for k in range(TOP, TOP + ny, CHUNK):
            both = pad[3, x, k : k + CHUNK, :nz] + pad[3, outer, k : k + CHUNK, :nz]
            coef_x[side, k - TOP : k - TOP + CHUNK, :] = both - sign * HALF * pad[0, x, k : k + CHUNK, :nz]
        row, beyond = (TOP + ny - 1, TOP + ny) if side else (TOP, TOP - 1)
        for x in range(nx):
            both = pad[3, x + 1, row : row + 1, :nz] + pad[3, x + 1, beyond : beyond + 1, :nz]
            coef_y[side, x : x + 1, :] = both - sign * HALF * pad[1, x + 1, row : row + 1, :nz]

    def layer(x, side):
        for k in range(0, ny, CHUNK):
            new = update(pad, x + 1, TOP + k)
            for c in range(3):
                value = new[c][:, :nz]
                s2[c, x, k : k + CHUNK, :] = value.astype(BF16)
                if side is not None:
                    quasi[side, c, k : k + CHUNK, :] = value
                if k == 0:
                    quasi_rows[0, c, pl.ds(x, 1), :] = value[:1]
                    blocks[0, c, x] = value.astype(BF16)
                if k == ny - CHUNK:
                    quasi_rows[1, c, pl.ds(x, 1), :] = value[CHUNK - 1 :]
                    blocks[1, c, x] = value.astype(BF16)

    layer(0, 0)
    layer(nx - 1, 1)

    def middle(x, _):
        layer(x, None)
        return 0

    lax.fori_loop(1, nx - 1, middle, 0)

    taps = row_of.shape[0]
    rows = row_of[...]
    z = z_of[...]
    late = late_of[...]
    near = lax.broadcasted_iota(jnp.int32, (taps, nx * ny), 1)
    hot = jnp.where(near == rows, 1.0, 0.0).astype(BF16)
    middles = slice(ny, (nx - 1) * ny)
    for c in range(3):
        state[c, :ny, :] = edges[0, c]
        state[c, middles, :] = s1[c, 1 : nx - 1].reshape((nx - 2) * ny, nz)
        state[c, (nx - 1) * ny :, :] = edges[1, c]
    first = energies(hot, [state[c] for c in range(3)], z, nz)
    second = energies(hot, [s2[c].reshape(nx * ny, nz) for c in range(3)], z, nz)
    peaks[...] = jnp.maximum(first, jnp.where(late < 0, second, 0.0))
    column = lax.broadcasted_iota(jnp.int32, hot_late.shape, 1)
    hot_late[...] = jnp.where(column == late, 1.0, 0.0).astype(BF16)
    count = slots.shape[1]
    block = lax.broadcasted_iota(jnp.int32, (taps, count), 1)
    chosen = jnp.where(block == block_of[...], jnp.broadcast_to(slots[...], (taps, count)), 0.0)
    slot_of[...] = jnp.sum(chosen, axis=1, keepdims=True)


def second_edges(plo, phi, extra, quasi, coef_x, ylo, yhi, quasi_rows, coef_y, blocks, hot_late, z_of, slot_of, peaks, s2_in,
                 s2, best, layers, strips, late, sems):
    _, _, ny, nz = quasi.shape
    nx = quasi_rows.shape[2]
    ghosts_y = [[g[c].astype(F32) for c in range(3)] for g in (ylo, yhi)]
    copies = []
    added = [[coef_y[i] * ghosts_y[i][c] for c in range(3)] for i in range(2)]
    line = lax.broadcasted_iota(jnp.int32, (CHUNK, nz), 0)
    for side, ghost in enumerate((plo, phi)):
        x = (nx - 1) * side
        for c in range(3):
            for k in range(0, ny, CHUNK):
                part = slice(k, k + CHUNK)
                far = (ghost[c, part, :].astype(F32) + extra[side, c, part, :]).astype(BF16).astype(F32)
                value = quasi[side, c, part, :] + coef_x[side, part, :] * far
                if k == 0:
                    value = value + jnp.where(line == 0, jnp.broadcast_to(added[0][c][x : x + 1], line.shape), 0.0)
                if k == ny - CHUNK:
                    value = value + jnp.where(line == CHUNK - 1, jnp.broadcast_to(added[1][c][x : x + 1], line.shape), 0.0)
                value = value.astype(BF16)
                layers[side, c, part, :] = value
                late[c, side * ny + k : side * ny + k + CHUNK, :] = value
        copies.append(pltpu.make_async_copy(layers.at[side], s2.at[:, x], sems.at[side]))
        copies[-1].start()
    for c in range(3):
        fixed = [quasi_rows[i, c] + added[i][c] for i in range(2)]
        late[c, 2 * ny : 2 * ny + 2 * nx, :] = jnp.concatenate(fixed, axis=0).astype(BF16)
        for i in range(2):
            for x in range(1, nx - 1):
                fresh = jnp.broadcast_to(fixed[i][x : x + 1], line.shape)
                kept = blocks[i, c, x].astype(F32)
                strips[i, c, x - 1] = jnp.where(line == (CHUNK - 1) * i, fresh, kept).astype(BF16)
    for i in range(2):
        place = s2.at[:, 1 : nx - 1, (ny - CHUNK) * i : (ny - CHUNK) * i + CHUNK]
        copies.append(pltpu.make_async_copy(strips.at[i], place, sems.at[2 + i]))
        copies[-1].start()
    last = energies(hot_late[...], [late[c] for c in range(3)], z_of[...], nz)
    peak = jnp.maximum(peaks[...], last)
    slot = lax.broadcasted_iota(jnp.int32, (peak.shape[0], best.shape[1]), 1).astype(F32)
    best[...] = jnp.max(jnp.where(slot == slot_of[...], peak, 0.0), axis=0, keepdims=True)
    for copy in copies:
        copy.wait()


VM = pl.BlockSpec(memory_space=pltpu.VMEM)
HB = pl.BlockSpec(memory_space=pl.ANY)


def shape(dims, kind):
    return jax.ShapeDtypeStruct(dims, kind)


def body(velocity, viscosity, tap_cell, tap_block, block_slot):
    _, nx, ny, nz = velocity.shape
    taps = tap_cell.shape[1]
    count = block_slot.shape[0]
    padded = pltpu.VMEM((4, nx + 2, TOP + ny + 8, PADDED), F32)

    def perms(axis):
        peers = lax.axis_size(axis)
        up = [(i, (i + 1) % peers) for i in range(peers)]
        return up, [(j, i) for i, j in up]

    x_up, x_down = perms("gx")
    y_up, y_down = perms("gy")

    own_ylo = jnp.concatenate([velocity[:, :, 0], viscosity[None, :, 0]], axis=0)
    own_yhi = jnp.concatenate([velocity[:, :, ny - 1], viscosity[None, :, ny - 1]], axis=0)
    ylo = lax.ppermute(own_yhi, "gy", y_up)
    yhi = lax.ppermute(own_ylo, "gy", y_down)
    own_lo = jnp.concatenate([velocity[:, 0], viscosity[None, 0]], axis=0)
    own_hi = jnp.concatenate([velocity[:, nx - 1], viscosity[None, nx - 1]], axis=0)
    alo = lax.ppermute(own_hi, "gx", x_up)
    ahi = lax.ppermute(own_lo, "gx", x_down)

    cell = tap_cell[0]
    row_of = cell // nz
    z_of = (cell - row_of * nz)[:, None]
    tap_x, tap_y = row_of // ny, row_of % ny
    late_of = jnp.where(tap_y == 0, 2 * ny + tap_x, jnp.where(tap_y == ny - 1, 2 * ny + nx + tap_x, -1))
    late_of = jnp.where(tap_x == 0, tap_y, jnp.where(tap_x == nx - 1, ny + tap_y, late_of))[:, None]
    row_of = row_of[:, None]

    face = shape((3, ny, nz), BF16)
    s1, edge_lo, edge_hi, part, rows = pl.pallas_call(
        first_step,
        out_shape=(shape((3, nx, ny, nz), BF16), face, face, shape((2, 3, ny, nz), F32), shape((2, 3, nx, nz), F32)),
        in_specs=[VM] * 4,
        out_specs=[VM] * 5,
        scratch_shapes=[padded],
        compiler_params=pltpu.CompilerParams(vmem_limit_bytes=32 * 2**20),
        cost_estimate=pl.CostEstimate(flops=3 * 10**7, bytes_accessed=6 * 10**6, transcendentals=0),
        name="first_step",
    )(velocity, viscosity, ylo, yhi)
    plo = lax.ppermute(edge_hi, "gx", x_up)
    phi = lax.ppermute(edge_lo, "gx", x_down)

    yface = shape((3, nx, nz), BF16)
    edges, extra, face_lo, face_hi = pl.pallas_call(
        first_edges,
        out_shape=(shape((2, 3, ny, nz), BF16), shape((2, 3, ny, nz), F32), yface, yface),
        in_specs=[VM] * 6,
        out_specs=[VM] * 4,
        compiler_params=pltpu.CompilerParams(vmem_limit_bytes=16 * 2**20),
        cost_estimate=pl.CostEstimate(flops=3 * 10**6, bytes_accessed=3 * 10**6, transcendentals=0),
        name="first_edges",
    )(part, own_lo, own_hi, alo, ahi, rows)
    y2lo = lax.ppermute(face_hi, "gy", y_up)
    y2hi = lax.ppermute(face_lo, "gy", y_down)

    late_rows = 2 * ny + 2 * nx
    s2, quasi, quasi_rows, blocks, coef_x, coef_y, hot_late, slot_of, peaks = pl.pallas_call(
        second_step,
        out_shape=(
            shape((3, nx, ny, nz), BF16),
            shape((2, 3, ny, nz), F32),
            shape((2, 3, nx, nz), F32),
            shape((2, 3, nx, CHUNK, nz), BF16),
            shape((2, ny, nz), F32),
            shape((2, nx, nz), F32),
            shape((taps, late_rows), BF16),
            shape((taps, 1), F32),
            shape((taps, 1), F32),
        ),
        in_specs=[VM] * 12,
        out_specs=[VM] * 9,
        scratch_shapes=[padded, pltpu.VMEM((3, nx * ny, nz), BF16)],
        compiler_params=pltpu.CompilerParams(vmem_limit_bytes=32 * 2**20),
        cost_estimate=pl.CostEstimate(flops=3 * 10**7, bytes_accessed=8 * 10**6, transcendentals=0),
        name="second_step",
    )(s1, edges, viscosity, alo, ahi, ylo, yhi, row_of, z_of, late_of, tap_block[0][:, None], block_slot.astype(F32)[None])

    new_velocity, best = pl.pallas_call(
        second_edges,
        out_shape=(shape((3, nx, ny, nz), BF16), shape((1, count), F32)),
        in_specs=[VM] * 14 + [HB],
        out_specs=[HB, VM],
        scratch_shapes=[
            pltpu.VMEM((2, 3, ny, nz), BF16),
            pltpu.VMEM((2, 3, nx - 2, CHUNK, nz), BF16),
            pltpu.VMEM((3, late_rows, nz), BF16),
            pltpu.SemaphoreType.DMA((4,)),
        ],
        input_output_aliases={14: 0},
        compiler_params=pltpu.CompilerParams(vmem_limit_bytes=16 * 2**20),
        cost_estimate=pl.CostEstimate(flops=3 * 10**6, bytes_accessed=3 * 10**6, transcendentals=0),
        name="second_edges",
    )(plo, phi, extra, quasi, coef_x, y2lo, y2hi, quasi_rows, coef_y, blocks, hot_late, z_of, slot_of, peaks, s2)

    groups = lax.axis_size(("gx", "gy"))
    received = lax.all_to_all(best.reshape(groups, count // groups), ("gx", "gy"), split_axis=0, concat_axis=0, tiled=True)
    return new_velocity, jnp.max(received, axis=0)


def solution(mesh):
    placed = (
        P(None, "gx", "gy", None),
        P("gx", "gy", None),
        P(("gx", "gy"), None),
        P(("gx", "gy"), None),
        P(),
    )
    return jax.shard_map(
        body,
        mesh=mesh,
        in_specs=placed,
        out_specs=(P(None, "gx", "gy", None), P(("gx", "gy"))),
        check_vma=False,
    )
```

time: 116 us -> 84.7 us (0.73)
  other arithmetic: 39.1 us -> 5.23 us
  waiting for transfers between devices: 26.6 us -> 2.11 us
  Pallas kernels: 0 us -> 22.5 us
  starting transfers between devices: 16.6 us -> 21.2 us
    ppermute x8, waiting for transfers between devices: 26.6 us -> 2.11 us  [the longest x1 2.09 us: body(): yhi = lax.ppermute(own_ylo, 'gy', y_down)]
    pallas_call x0 -> x4, Pallas kernels: none -> 22.5 us  [the longest x1 10.5 us: body(): pl.pallas_call(second_step, out_shape=(shape((3, nx, ny, nz), BF16), shap...]
    another operation x7 -> x0, other arithmetic: 19.8 us -> none  [advance(): return jnp.stack(results, 0)]
    gather x2 -> x0, local copies, waits for them, and re-layouts: 6.75 us -> none  [tap_energy(): return energy[cells]]
    concatenate x3 -> x4, other arithmetic: 7.38 us -> 2.18 us  [the longest x1 0.77 us: body(): jnp.concatenate([velocity[:, nx - 1], viscosity[None, nx - 1]], axis=0)]
    ppermute x8, starting transfers between devices: 16.6 us -> 21.2 us  [the longest x1 6.87 us: body(): y2hi = lax.ppermute(face_lo, 'gy', y_down)]
    unnamed x32, local copies, waits for them, and re-layouts: 2.87 us -> 6.86 us
    convert_element_type x3 -> x1, other arithmetic: 4.32 us -> 0.68 us  [body(): block_slot.astype(F32)[None]]
  transfers between devices with their start and end apart: 8 -> 8, of which waited for: 6 -> 1; matrix products, arithmetic and copies ran while one was open for 8% -> 10% of each run, Pallas kernels for 0% -> 24%
where the time goes in v1:
time: 84.7 us; the launch traced here: 84.2 us
  Pallas kernels  22.5 us (27%)
  starting transfers between devices  21.2 us (25%)
  blocking collectives  17.5 us (21%)
  local copies, waits for them, and re-layouts  14.9 us (18%)
  other arithmetic  5.23 us (6%)
  waiting for transfers between devices  2.11 us (2%)
    all_to_all x1, blocking collectives, body(): lax.all_to_all(best.reshape(groups, count // groups), ('gx', 'gy'), split...  17.5 us
    pallas_call x1, Pallas kernels, body(): pl.pallas_call(second_step, out_shape=(shape((3, nx, ny, nz), BF16), shap...  10.5 us
    pallas_call x1, Pallas kernels, body(): pl.pallas_call(first_step, out_shape=(shape((3, nx, ny, nz), BF16), face,...  7.91 us
    ppermute x1, starting transfers between devices, body(): y2hi = lax.ppermute(face_lo, 'gy', y_down)  6.87 us
    unnamed x32, local copies, waits for them, and re-layouts  6.86 us
    ppermute x1, starting transfers between devices, body(): phi = lax.ppermute(edge_lo, 'gx', x_down)  5.08 us
    ppermute x1, starting transfers between devices, body(): ahi = lax.ppermute(own_lo, 'gx', x_down)  3.48 us
    ppermute x1, starting transfers between devices, body(): alo = lax.ppermute(own_hi, 'gx', x_up)  2.74 us
  transfers between devices with their start and end apart: 8, of which 1 were waited for; matrix products, arithmetic and copies ran while one was open for 10% of the time, Pallas kernels for 24%

profile of v1, /device:TPU:1, one launch (start us, length us, event | category | flops | bytes accessed | tf_op | source)
XLA Modules:
  0.0 84.2 jit_solution(1854540101848434864)
XLA Ops:
  0.6 0.0 copy-start
  0.6 0.0 copy-start.1
  0.7 1.1 %fusion.4 = (bf16[8,1,576]{2,1,0:T(2,128)(2,1)S(1)}, bf16[8,1,576]{2,1,0:T(2,128)(2,1)S(1)}) fusion(bf16[8,64,576]{2,1,0:T(8,128)(2,1)} %visc.3), kind=kLoop, calls=%fused_computation.25 | loop fusion | bytes 36864 | tf_op jit(solution)/shard_map/slice | solution.py:285
  1.8 1.2 %fusion.2 = (bf16[3,8,1,576]{3,2,1,0:T(2,128)(2,1)S(1)}, bf16[3,8,1,576]{3,2,1,0:T(2,128)(2,1)S(1)}) fusion(bf16[3,8,64,576]{3,2,1,0:T(8,128)(2,1)} %vel.1), kind=kLoop, calls=%fused_computation.23 | loop fusion | bytes 110592 | tf_op jit(solution)/shard_map/slice | solution.py:285
  3.0 0.6 pad_maximum_fusion.2
  3.6 2.7 %collective-permute-start = (bf16[4,8,576]{2,1,0:T(8,128)(2,1)}, bf16[4,8,576]{2,1,0:T(8,128)(2,1)S(1)}, u32[]{:S(2)}, u32[]{:S(2)}) collective-permute-start(bf16[4,8,576]{2,1,0:T(8,128)(2,1)} %pad_maximum_fusion.2), channel_id=1, source_target_pairs={{0,1},{1,2},{2,3},{3,4},{4,5},{5,6},{6,7},{7,8},{8,9},{9,10},{10,1... | collective-permute-start | bytes 110600 | tf_op jit(solution)/shard_map/ppermute | solution.py:287
  6.3 0.9 %fusion.3 = (bf16[1,64,576]{2,1,0:T(8,128)(2,1)S(1)}, bf16[1,64,576]{2,1,0:T(8,128)(2,1)S(1)}) fusion(bf16[8,64,576]{2,1,0:T(8,128)(2,1)} %visc.3), kind=kLoop, calls=%fused_computation.24 | loop fusion | bytes 294912 | tf_op jit(solution)/shard_map/slice | solution.py:290
  7.2 1.1 %slice_bitcast_fusion = (bf16[3,64,576]{2,1,0:T(8,128)(2,1)S(1)}, bf16[3,64,576]{2,1,0:T(8,128)(2,1)S(1)}) fusion(bf16[3,8,64,576]{3,2,1,0:T(8,128)(2,1)} %vel.1), kind=kLoop, calls=%fused_computation.8 | loop fusion | bytes 884736 | tf_op jit(solution)/shard_map/squeeze | solution.py:290
  8.4 0.8 pad_maximum_fusion.1.own_hi
  9.1 2.7 %collective-permute-start.4 = (bf16[4,64,576]{2,1,0:T(8,128)(2,1)}, bf16[4,64,576]{2,1,0:T(8,128)(2,1)S(1)}, u32[]{:S(2)}, u32[]{:S(2)}) collective-permute-start(bf16[4,64,576]{2,1,0:T(8,128)(2,1)} %pad_maximum_fusion.1.own_hi), channel_id=1, source_target_pairs={{0,16},{16,32},{32,48},{48,64},{64,80},{80,96},{96,112},{112,0},{1... | collective-permute-start | bytes 884744 | tf_op jit(solution)/shard_map/ppermute | solution.py:291
  11.9 0.8 pad_maximum_fusion.own_lo
  12.6 3.5 %collective-permute-start.5 = (bf16[4,64,576]{2,1,0:T(8,128)(2,1)}, bf16[4,64,576]{2,1,0:T(8,128)(2,1)S(1)}, u32[]{:S(2)}, u32[]{:S(2)}) collective-permute-start(bf16[4,64,576]{2,1,0:T(8,128)(2,1)} %pad_maximum_fusion.own_lo), channel_id=1, source_target_pairs={{16,0},{32,16},{48,32},{64,48},{80,64},{96,80},{112,96},{0,112},{1... | collective-permute-start | bytes 884744 | tf_op jit(solution)/shard_map/ppermute | solution.py:292
  16.2 0.1 collective-permute-start.1
  16.3 0.8 copy.44
  17.1 0.8 copy.45
  17.9 0.0 collective-permute-done.ylo
  17.9 2.1 %collective-permute-done.1.yhi = bf16[4,8,576]{2,1,0:T(8,128)(2,1)S(1)} collective-permute-done((bf16[4,8,576]{2,1,0:T(8,128)(2,1)S(1)}, bf16[4,8,576]{2,1,0:T(8,128)(2,1)S(1)}, u32[]{:S(2)}, u32[]{:S(2)}) %collective-permute-start.1) | collective-permute-done | bytes 36896 | tf_op jit(solution)/shard_map/ppermute | solution.py:288
  19.9 0.0 copy-done
  20.0 7.9 %first_step.1 = (bf16[3,8,64,576]{3,2,1,0:T(8,128)(2,1)S(1)}, bf16[3,64,576]{2,1,0:T(8,128)(2,1)}, bf16[3,64,576]{2,1,0:T(8,128)(2,1)}, f32[2,3,64,576]{3,2,1,0:T(8,128)S(1)}, f32[2,3,8,576]{3,2,1,0:T(8,128)S(1)}) custom-call(bf16[3,8,64,576]{3,2,1,0:T(8,128)(2,1)S(1)} %copy-done.1, bf16[8,64,576]{2,1,0:T(8,128)(2,1)S(1)} %copy-done, ...), custom_call_target="tpu_custom_call" | custom-call | flops 30000000 | bytes 6000000 | tf_op jit(solution)/shard_map/first_step/pallas_call | solution.py:303
  27.9 1.3 %copy-done.2 = bf16[3,8,64,576]{3,2,1,0:T(8,128)(2,1)} copy-done((bf16[3,8,64,576]{3,2,1,0:T(8,128)(2,1)}, bf16[3,8,64,576]{3,2,1,0:T(8,128)(2,1)S(1)}, u32[]{:S(2)}) %copy-start.2) | copy-done | bytes 1769496
  29.1 0.0 collective-permute-start.2
  29.1 5.1 %collective-permute-start.3 = (bf16[3,64,576]{2,1,0:T(8,128)(2,1)}, bf16[3,64,576]{2,1,0:T(8,128)(2,1)}, u32[]{:S(2)}, u32[]{:S(2)}) collective-permute-start(bf16[3,64,576]{2,1,0:T(8,128)(2,1)} %get-tuple-element.23), channel_id=1, source_target_pairs={{16,0},{32,16},{48,32},{64,48},{80,64},{96,80},{112,96},{0,112},{1... | collective-permute-start | bytes 663560 | tf_op jit(solution)/shard_map/ppermute | solution.py:314
  34.2 0.0 collective-permute-done.4.alo
  34.2 0.0 collective-permute-done.5.ahi
  34.2 1.8 %first_edges.1 = (bf16[2,3,64,576]{3,2,1,0:T(8,128)(2,1)S(1)}, f32[2,3,64,576]{3,2,1,0:T(8,128)S(1)}, bf16[3,8,576]{2,1,0:T(8,128)(2,1)}, bf16[3,8,576]{2,1,0:T(8,128)(2,1)}) custom-call(f32[2,3,64,576]{3,2,1,0:T(8,128)S(1)} %get-tuple-element.24.part, bf16[4,64,576]{2,1,0:T(8,128)(2,1)} %pad_maximum_fusion.own_lo, ...), custom_call_target="tpu_custom_call" | custom-call | flops 3000000 | bytes 3000000 | tf_op jit(solution)/shard_map/first_edges/pallas_call | solution.py:317
  36.0 1.0 %copy-done.4 = f32[2,3,64,576]{3,2,1,0:T(8,128)} copy-done((f32[2,3,64,576]{3,2,1,0:T(8,128)}, f32[2,3,64,576]{3,2,1,0:T(8,128)S(1)}, u32[]{:S(2)}) %copy-start.4) | copy-done | bytes 884760
  37.0 0.8 copy-done.9
  37.7 0.3 collective-permute-start.6
  38.0 6.9 %collective-permute-start.7 = (bf16[3,8,576]{2,1,0:T(8,128)(2,1)}, bf16[3,8,576]{2,1,0:T(8,128)(2,1)}, u32[]{:S(2)}, u32[]{:S(2)}) collective-permute-start(bf16[3,8,576]{2,1,0:T(8,128)(2,1)} %get-tuple-element.32), channel_id=1, source_target_pairs={{1,0},{2,1},{3,2},{4,3},{5,4},{6,5},{7,6},{8,7},{9,8},{10,9},{11,1... | collective-permute-start | bytes 82952 | tf_op jit(solution)/shard_map/ppermute | solution.py:327
  44.9 0.0 copy-done.11
  44.9 1.0 %select_select_fusion = (s32[320,1]{1,0:T(8,128)}, s32[320,1]{1,0:T(8,128)}, s32[320,1]{1,0:T(8,128)S(1)}) fusion(s32[320,1]{1,0:T(8,128)S(1)} %copy-done.11, pred[320,1]{1,0:T(8,128)(4,1)S(1)} %copy-done.12), kind=kLoop, calls=%fused_computation.10 | loop fusion | flops 12160 | bytes 5440 | tf_op jit(solution)/shard_map/jit(_where)/select_n | solution.py:299
  45.9 1.5 %copy.48.block_of = s32[320,1]{1,0:T(8,128)} copy(s32[320,1]{0,1:T(1,128)} %bitcast.32) | data formatting | bytes 2560 | tf_op jit(solution)/shard_map/broadcast_in_dim;squeeze | solution.py:349
  47.4 0.7 convert_element_type.3
  48.1 0.9 %copy-done.6 = s32[320,1]{1,0:T(8,128)S(1)} copy-done((s32[320,1]{1,0:T(8,128)S(1)}, s32[320,1]{1,0:T(8,128)}, u32[]{:S(2)}) %copy-start.6) | copy-done | bytes 1304
  49.0 0.9 %copy-done.7 = s32[320,1]{1,0:T(8,128)S(1)} copy-done((s32[320,1]{1,0:T(8,128)S(1)}, s32[320,1]{1,0:T(8,128)}, u32[]{:S(2)}) %copy-start.7) | copy-done | bytes 1304
  49.9 0.9 %copy-done.8 = s32[320,1]{1,0:T(8,128)S(1)} copy-done((s32[320,1]{1,0:T(8,128)S(1)}, s32[320,1]{1,0:T(8,128)}, u32[]{:S(2)}) %copy-start.8) | copy-done | bytes 1304
  50.8 1.0 %copy-done.10 = bf16[2,3,64,576]{3,2,1,0:T(8,128)(2,1)S(1)} copy-done((bf16[2,3,64,576]{3,2,1,0:T(8,128)(2,1)S(1)}, bf16[2,3,64,576]{3,2,1,0:T(8,128)(2,1)}, u32[]{:S(2)}) %copy-start.10) | copy-done | bytes 442392
  51.9 10.5 %second_step.1 = (bf16[3,8,64,576]{3,2,1,0:T(8,128)(2,1)}, f32[2,3,64,576]{3,2,1,0:T(8,128)S(1)}, f32[2,3,8,576]{3,2,1,0:T(8,128)S(1)}, bf16[2,3,8,16,576]{4,3,2...) custom-call(bf16[3,8,64,576]{3,2,1,0:T(8,128)(2,1)S(1)} %copy-done.3, ...), custom_call_target="tpu_custom_call" | custom-call | flops 30000000 | bytes 8000000 | tf_op jit(solution)/shard_map/second_step/pallas_call | solution.py:330
  62.3 0.0 collective-permute-done.2.plo
  62.4 0.0 collective-permute-done.3.phi
  62.4 0.0 collective-permute-done.6.ylo
  62.4 0.0 collective-permute-done.7.yhi
  62.4 2.4 %second_edges.1 = (bf16[3,8,64,576]{3,2,1,0:T(8,128)(2,1)}, f32[1,512]{1,0:T(1,128)S(1)}) custom-call(bf16[3,64,576]{2,1,0:T(8,128)(2,1)} %collective-permute-done.2.plo, bf16[3,64,576]{2,1,0:T(8,128)(2,1)} %collective-permute-done.3.phi, f32[2,3,64,576]{3,2,1,0:T(8,128)S(1)} %copy-done.5, ...), custom_call_target="tpu_custom_call", output_to_operand_aliasing={{0}: (14, {})} | custom-call | flops 3000000 | bytes 3000000 | tf_op jit(solution)/shard_map/second_edges/pallas_call | solution.py:351
  64.8 0.5 broadcast.217
  65.3 0.7 reduce.4
  65.9 0.1 all_to_all.6
  66.0 17.5 %all_to_all.9 = f32[128,1,4]{2,1,0:T(1,128)S(1)} all-to-all(f32[128,1,4]{2,1,0:T(1,128)S(1)} %bitcast.26), channel_id=1, replica_groups=mesh['gx'=8,'gy'=16] {'gx','gy'}, dimensions={0} | all-to-all | bytes 4096 | tf_op jit(solution)/shard_map/all_to_all | solution.py:369
  83.6 0.7 reduce_max.9
  (23 shorter events, 0.1 us)
Async XLA Ops:
  0.6 19.3 %copy-start = (bf16[8,64,576]{2,1,0:T(8,128)(2,1)S(1)}, bf16[8,64,576]{2,1,0:T(8,128)(2,1)}, u32[]{:S(2)}) copy-start(bf16[8,64,576]{2,1,0:T(8,128)(2,1)} %visc.3) | copy-start | bytes 1769476
  0.6 19.3 %copy-start.1 = (bf16[3,8,64,576]{3,2,1,0:T(8,128)(2,1)S(1)}, bf16[3,8,64,576]{3,2,1,0:T(8,128)(2,1)}, u32[]{:S(2)}) copy-start(bf16[3,8,64,576]{3,2,1,0:T(8,128)(2,1)} %vel.1) | copy-start | bytes 5308420
  0.7 15.6 %copy-start.13 = (s32[1,320]{1,0:T(1,128)S(1)}, s32[1,320]{1,0:T(1,128)}, u32[]{:S(2)}) copy-start(s32[1,320]{1,0:T(1,128)} %param.7) | copy-start | bytes 3844
  3.6 14.2 %collective-permute-start = (bf16[4,8,576]{2,1,0:T(8,128)(2,1)}, bf16[4,8,576]{2,1,0:T(8,128)(2,1)S(1)}, u32[]{:S(2)}, u32[]{:S(2)}) collective-permute-start(bf16[4,8,576]{2,1,0:T(8,128)(2,1)} %pad_maximum_fusion.2), channel_id=1, source_target_pairs={{0,1},{1,2},{2,3},{3,4},{4,5},{5,6},{6,7},{7,8},{8,9},{9,10},{10,1... | collective-permute-start | bytes 110600 | tf_op jit(solution)/shard_map/ppermute | solution.py:287
  9.1 25.1 %collective-permute-start.4 = (bf16[4,64,576]{2,1,0:T(8,128)(2,1)}, bf16[4,64,576]{2,1,0:T(8,128)(2,1)S(1)}, u32[]{:S(2)}, u32[]{:S(2)}) collective-permute-start(bf16[4,64,576]{2,1,0:T(8,128)(2,1)} %pad_maximum_fusion.1.own_hi), channel_id=1, source_target_pairs={{0,16},{16,32},{32,48},{48,64},{64,80},{80,96},{96,112},{112,0},{1... | collective-permute-start | bytes 884744 | tf_op jit(solution)/shard_map/ppermute | solution.py:291
  12.6 21.6 %collective-permute-start.5 = (bf16[4,64,576]{2,1,0:T(8,128)(2,1)}, bf16[4,64,576]{2,1,0:T(8,128)(2,1)S(1)}, u32[]{:S(2)}, u32[]{:S(2)}) collective-permute-start(bf16[4,64,576]{2,1,0:T(8,128)(2,1)} %pad_maximum_fusion.own_lo), channel_id=1, source_target_pairs={{16,0},{32,16},{48,32},{64,48},{80,64},{96,80},{112,96},{0,112},{1... | collective-permute-start | bytes 884744 | tf_op jit(solution)/shard_map/ppermute | solution.py:292
  16.2 3.8 %collective-permute-start.1 = (bf16[4,8,576]{2,1,0:T(8,128)(2,1)S(1)}, bf16[4,8,576]{2,1,0:T(8,128)(2,1)S(1)}, u32[]{:S(2)}, u32[]{:S(2)}) collective-permute-start(bf16[4,8,576]{2,1,0:T(8,128)(2,1)S(1)} %pad_maximum_fusion.3), channel_id=1, source_target_pairs={{1,0},{2,1},{3,2},{4,3},{5,4},{6,5},{7,6},{8,7},{9,8},{10,9},{11,1... | collective-permute-start | bytes 110600 | tf_op jit(solution)/shard_map/ppermute | solution.py:288
  17.8 27.0 %copy-start.11 = (s32[320,1]{1,0:T(8,128)S(1)}, s32[320,1]{1,0:T(8,128)}, u32[]{:S(2)}) copy-start(s32[320,1]{1,0:T(8,128)} %copy.44) | copy-start | bytes 3844
  17.9 27.0 %copy-start.12 = (pred[320,1]{1,0:T(8,128)(4,1)S(1)}, pred[320,1]{1,0:T(8,128)(4,1)}, u32[]{:S(2)}) copy-start(pred[320,1]{1,0:T(8,128)(4,1)} %copy.45) | copy-start | bytes 964
  27.9 1.3 %copy-start.2 = (bf16[3,8,64,576]{3,2,1,0:T(8,128)(2,1)}, bf16[3,8,64,576]{3,2,1,0:T(8,128)(2,1)S(1)}, u32[]{:S(2)}) copy-start(bf16[3,8,64,576]{3,2,1,0:T(8,128)(2,1)S(1)} %get-tuple-element.27.s1) | copy-start | bytes 5308420
  29.1 19.0 %copy-start.3 = (bf16[3,8,64,576]{3,2,1,0:T(8,128)(2,1)S(1)}, bf16[3,8,64,576]{3,2,1,0:T(8,128)(2,1)}, u32[]{:S(2)}) copy-start(bf16[3,8,64,576]{3,2,1,0:T(8,128)(2,1)} %copy-done.2) | copy-start | bytes 5308420
  29.1 33.2 %collective-permute-start.2 = (bf16[3,64,576]{2,1,0:T(8,128)(2,1)}, bf16[3,64,576]{2,1,0:T(8,128)(2,1)}, u32[]{:S(2)}, u32[]{:S(2)}) collective-permute-start(bf16[3,64,576]{2,1,0:T(8,128)(2,1)} %get-tuple-element.22), channel_id=1, source_target_pairs={{0,16},{16,32},{32,48},{48,64},{64,80},{80,96},{96,112},{112,0},{1... | collective-permute-start | bytes 663560 | tf_op jit(solution)/shard_map/ppermute | solution.py:313
  29.1 33.2 %collective-permute-start.3 = (bf16[3,64,576]{2,1,0:T(8,128)(2,1)}, bf16[3,64,576]{2,1,0:T(8,128)(2,1)}, u32[]{:S(2)}, u32[]{:S(2)}) collective-permute-start(bf16[3,64,576]{2,1,0:T(8,128)(2,1)} %get-tuple-element.23), channel_id=1, source_target_pairs={{16,0},{32,16},{48,32},{64,48},{80,64},{96,80},{112,96},{0,112},{1... | collective-permute-start | bytes 663560 | tf_op jit(solution)/shard_map/ppermute | solution.py:314
  36.0 1.0 %copy-start.4 = (f32[2,3,64,576]{3,2,1,0:T(8,128)}, f32[2,3,64,576]{3,2,1,0:T(8,128)S(1)}, u32[]{:S(2)}) copy-start(f32[2,3,64,576]{3,2,1,0:T(8,128)S(1)} %get-tuple-element.26.extra) | copy-start | bytes 2654212
  37.0 0.8 copy-start.9
  37.7 24.6 %collective-permute-start.6 = (bf16[3,8,576]{2,1,0:T(8,128)(2,1)}, bf16[3,8,576]{2,1,0:T(8,128)(2,1)S(1)}, u32[]{:S(2)}, u32[]{:S(2)}) collective-permute-start(bf16[3,8,576]{2,1,0:T(8,128)(2,1)} %get-tuple-element.31), channel_id=1, source_target_pairs={{0,1},{1,2},{2,3},{3,4},{4,5},{5,6},{6,7},{7,8},{8,9},{9,10},{10,1... | collective-permute-start | bytes 82952 | tf_op jit(solution)/shard_map/ppermute | solution.py:326
  38.0 24.4 %collective-permute-start.7 = (bf16[3,8,576]{2,1,0:T(8,128)(2,1)}, bf16[3,8,576]{2,1,0:T(8,128)(2,1)}, u32[]{:S(2)}, u32[]{:S(2)}) collective-permute-start(bf16[3,8,576]{2,1,0:T(8,128)(2,1)} %get-tuple-element.32), channel_id=1, source_target_pairs={{1,0},{2,1},{3,2},{4,3},{5,4},{6,5},{7,6},{8,7},{9,8},{10,9},{11,1... | collective-permute-start | bytes 82952 | tf_op jit(solution)/shard_map/ppermute | solution.py:327
  48.1 0.9 %copy-start.6 = (s32[320,1]{1,0:T(8,128)S(1)}, s32[320,1]{1,0:T(8,128)}, u32[]{:S(2)}) copy-start(s32[320,1]{1,0:T(8,128)} %copy.48.block_of) | copy-start | bytes 3844
  49.0 0.9 %copy-start.7 = (s32[320,1]{1,0:T(8,128)S(1)}, s32[320,1]{1,0:T(8,128)}, u32[]{:S(2)}) copy-start(s32[320,1]{1,0:T(8,128)} %get-tuple-element.50.late_of) | copy-start | bytes 3844
  49.9 0.9 %copy-start.8 = (s32[320,1]{1,0:T(8,128)S(1)}, s32[320,1]{1,0:T(8,128)}, u32[]{:S(2)}) copy-start(s32[320,1]{1,0:T(8,128)} %get-tuple-element.51.row_of) | copy-start | bytes 3844
  50.8 1.0 %copy-start.10 = (bf16[2,3,64,576]{3,2,1,0:T(8,128)(2,1)S(1)}, bf16[2,3,64,576]{3,2,1,0:T(8,128)(2,1)}, u32[]{:S(2)}) copy-start(bf16[2,3,64,576]{3,2,1,0:T(8,128)(2,1)} %copy-done.9) | copy-start | bytes 1327108
  51.9 10.5 %copy-start.5 = (f32[2,3,64,576]{3,2,1,0:T(8,128)S(1)}, f32[2,3,64,576]{3,2,1,0:T(8,128)}, u32[]{:S(2)}) copy-start(f32[2,3,64,576]{3,2,1,0:T(8,128)} %copy-done.4) | copy-start | bytes 2654212

commit v2 on v1

--- a/solution.py
+++ b/solution.py
@@ -59,7 +59,43 @@
     return total
 
 
-def first_step(vel, visc, ylo, yhi, s1, edge_lo, edge_hi, part, rows, pad):
+def y_faces(vel, visc, ylo, yhi, block_v, block_n, sems):
+    _, nx, ny, nz = vel.shape
+    copies = []
+    for i in range(2):
+        rows = slice((ny - CHUNK) * i, (ny - CHUNK) * i + CHUNK)
+        copies.append(pltpu.make_async_copy(vel.at[:, :, rows], block_v.at[i], sems.at[2 * i]))
+        copies.append(pltpu.make_async_copy(visc.at[:, rows], block_n.at[i], sems.at[2 * i + 1]))
+    for copy in copies:
+        copy.start()
+    line = lax.broadcasted_iota(jnp.int32, (nx, nz), 0)
+    for i, out in enumerate((ylo, yhi)):
+        copies[2 * i].wait()
+        copies[2 * i + 1].wait()
+        row = (CHUNK - 1) * i
+        for f in range(4):
+            total = jnp.zeros((nx, nz), F32)
+            for x in range(nx):
+                block = block_n[i, x] if f == 3 else block_v[i, f, x]
+                one = block.astype(F32)[row : row + 1]
+                total = jnp.where(line == x, jnp.broadcast_to(one, line.shape), total)
+            out[f] = total.astype(BF16)
+
+
+def x_faces(vel, visc, after, lo, hi, sems):
+    nx = vel.shape[1]
+    copies = []
+    for i, out in enumerate((lo, hi)):
+        x = (nx - 1) * i
+        copies.append(pltpu.make_async_copy(vel.at[:, x], out.at[0:3], sems.at[2 * i]))
+        copies.append(pltpu.make_async_copy(visc.at[x], out.at[3], sems.at[2 * i + 1]))
+    for copy in copies:
+        copy.start()
+    for copy in copies:
+        copy.wait()
+
+
+def first_step(vel, visc, ylo, yhi, s1, part, edge_lo, edge_hi, rows, pad, inner, outer, sems):
     _, nx, ny, nz = vel.shape
 
     def fill(x, _):
@@ -80,10 +116,11 @@
             new = update(pad, x + 1, TOP + k)
             for c in range(3):
                 value = new[c][:, :nz]
-                s1[c, x, k : k + CHUNK, :] = value.astype(BF16)
-                if side is not None:
+                if side is None:
+                    inner[c, x - 1, k : k + CHUNK, :] = value.astype(BF16)
+                else:
                     (edge_lo, edge_hi)[side][c, k : k + CHUNK, :] = value.astype(BF16)
-                    part[side, c, k : k + CHUNK, :] = value
+                    outer[side, c, k : k + CHUNK, :] = value
                 if k == 0:
                     rows[0, c, pl.ds(x, 1), :] = value[:1]
                 if k == ny - CHUNK:
@@ -91,40 +128,51 @@
 
     layer(0, 0)
     layer(nx - 1, 1)
+    edges_out = pltpu.make_async_copy(outer, part, sems.at[0])
+    edges_out.start()
+
+    def send(x):
+        return pltpu.make_async_copy(inner.at[:, x - 1], s1.at[:, x - 1], sems.at[x])
 
     def middle(x, _):
         layer(x, None)
+        send(x).start()
+        return 0
+
+    def finish(x, _):
+        send(x).wait()
         return 0
 
     lax.fori_loop(1, nx - 1, middle, 0)
-
-
-def first_edges(part, own_lo, own_hi, alo, ahi, rows, edges, extra, face_lo, face_hi):
-    _, _, ny, nz = part.shape
-    nx = rows.shape[2]
-    faces = [[rows[i, c] for c in range(3)] for i in range(2)]
+    lax.fori_loop(1, nx - 1, finish, 0)
+    edges_out.wait()
+
+
+def missing_terms(mine, far, sign):
+    both = (mine[3] + far[3]) * HALF
+    near_coef = both - sign * HALF * mine[0]
+    far_coef = both + sign * HALF * far[0]
+    gaps = [far[c] - mine[c] for c in range(3)]
+    return [near_coef * g for g in gaps], [-far_coef * g for g in gaps]
+
+
+def first_faces(rows, own_ylo, own_yhi, alo, ahi, face_lo, face_hi):
+    _, _, nx, nz = rows.shape
+    ny = alo.shape[1]
     line = lax.broadcasted_iota(jnp.int32, (nx, nz), 0)
-    for side, (own, ghost) in enumerate(((own_lo, alo), (own_hi, ahi))):
-        sign = 1.0 if side else -1.0
-        for k in range(0, ny, CHUNK):
-            mine = [own[f, k : k + CHUNK, :].astype(F32) for f in range(4)]
-            far = [ghost[f, k : k + CHUNK, :].astype(F32) for f in range(4)]
-            both = (mine[3] + far[3]) * HALF
-            near_coef = both - sign * HALF * mine[0]
-            far_coef = both + sign * HALF * far[0]
+    for i, (own, out) in enumerate(((own_ylo, face_lo), (own_yhi, face_hi))):
+        values = [rows[i, c] for c in range(3)]
+        for side, ghost in enumerate((alo, ahi)):
+            x = (nx - 1) * side
+            k = (ny - CHUNK) * i
+            row = (CHUNK - 1) * i
+            mine = [own[f].astype(F32)[x : x + 1] for f in range(4)]
+            far = [ghost[f, k : k + CHUNK, :].astype(F32)[row : row + 1] for f in range(4)]
+            terms, _ = missing_terms(mine, far, 1.0 if side else -1.0)
             for c in range(3):
-                gap = far[c] - mine[c]
-                value = part[side, c, k : k + CHUNK, :] + near_coef * gap
-                edges[side, c, k : k + CHUNK, :] = value.astype(BF16)
-                extra[side, c, k : k + CHUNK, :] = -far_coef * gap
-                x = (nx - 1) * side
-                if k == 0:
-                    faces[0][c] = jnp.where(line == x, jnp.broadcast_to(value[:1], line.shape), faces[0][c])
-                if k == ny - CHUNK:
-                    faces[1][c] = jnp.where(line == x, jnp.broadcast_to(value[CHUNK - 1 :], line.shape), faces[1][c])
-    for c in range(3):
-        face_lo[c] = faces[0][c].astype(BF16)
-        face_hi[c] = faces[1][c].astype(BF16)
+                values[c] = values[c] + jnp.where(line == x, jnp.broadcast_to(terms[c], line.shape), 0.0)
+        for c in range(3):
+            out[c] = values[c].astype(BF16)
 
 
 def energies(hot, states, z, nz):
@@ -136,22 +184,45 @@
     return jnp.max(jnp.where(lane == z, total, 0.0), axis=1, keepdims=True)
 
 
-def second_step(s1, edges, visc, alo, ahi, ylo, yhi, row_of, z_of, late_of, block_of, slots,
-                s2, quasi, quasi_rows, blocks, coef_x, coef_y, hot_late, slot_of, peaks, pad, state):
-    _, nx, ny, nz = s1.shape
+def second_step(s1, part, own_lo, own_hi, visc, alo, ahi, ylo, yhi, cells, tap_blocks, slots,
+                s2, quasi, extra, quasi_rows, blocks, coef_x, coef_y, hot_late, z_of, slot_of, peaks, pad, state, outer, sems):
+    _, nx, ny, nz = s2.shape
+    edges_in = pltpu.make_async_copy(part, outer, sems.at[0])
+    edges_in.start()
+
+    def fetch(x):
+        return pltpu.make_async_copy(s1.at[:, x - 1], state.at[:, x], sems.at[x])
+
+    def begin(x, _):
+        fetch(x).start()
+        return 0
+
+    lax.fori_loop(1, nx - 1, begin, 0)
+    edges_in.wait()
+    for side, (own, ghost) in enumerate(((own_lo, alo), (own_hi, ahi))):
+        x = (nx - 1) * side
+        beyond = (nx + 1) * side
+        pad[0:3, beyond] = jnp.zeros((3,) + pad.shape[2:], F32)
+        for k in range(0, ny, CHUNK):
+            mine = [own[f, k : k + CHUNK, :].astype(F32) for f in range(4)]
+            far = [ghost[f, k : k + CHUNK, :].astype(F32) for f in range(4)]
+            terms, far_terms = missing_terms(mine, far, 1.0 if side else -1.0)
+            put(pad, 3, beyond, TOP + k, far[3] * HALF, True)
+            for c in range(3):
+                state[c, x, k : k + CHUNK, :] = (outer[side, c, k : k + CHUNK, :] + terms[c]).astype(BF16)
+                extra[side, c, k : k + CHUNK, :] = far_terms[c]
 
     def fill(x, _):
-        put_layer(pad, x + 1, lambda c, k: s1[c, x, k : k + CHUNK, :], lambda k: visc[x, k : k + CHUNK, :], ny)
-        return 0
-
-    lax.fori_loop(1, nx - 1, fill, 0)
-    for side, ghost in enumerate((alo, ahi)):
-        x = (nx - 1) * side
-        put_layer(pad, x + 1, lambda c, k: edges[side, c, k : k + CHUNK, :], lambda k: visc[x, k : k + CHUNK, :], ny)
-        outer = (nx + 1) * side
-        pad[0:3, outer] = jnp.zeros((3,) + pad.shape[2:], F32)
-        for k in range(0, ny, CHUNK):
-            put(pad, 3, outer, TOP + k, ghost[3, k : k + CHUNK, :].astype(F32) * HALF, True)
+        put_layer(pad, x + 1, lambda c, k: state[c, x, k : k + CHUNK, :], lambda k: visc[x, k : k + CHUNK, :], ny)
+        return 0
+
+    def fetch_fill(x, _):
+        fetch(x).wait()
+        return fill(x, 0)
+
+    fill(0, 0)
+    fill(nx - 1, 0)
+    lax.fori_loop(1, nx - 1, fetch_fill, 0)
     for ghost, row in ((ylo, TOP - 1), (yhi, TOP + ny)):
         value = ghost[3].astype(F32) * HALF
         for x in range(nx):
@@ -194,25 +265,33 @@
 
     lax.fori_loop(1, nx - 1, middle, 0)
 
-    taps = row_of.shape[0]
-    rows = row_of[...]
-    z = z_of[...]
-    late = late_of[...]
+    taps = cells.shape[1]
+    same = lax.broadcasted_iota(jnp.int32, (taps, taps), 0) == lax.broadcasted_iota(jnp.int32, (taps, taps), 1)
+
+    def column_of(line):
+        return jnp.sum(jnp.where(same, jnp.broadcast_to(line, same.shape), 0.0), axis=1, keepdims=True)
+
+    cell = cells[...].astype(F32)
+    line_rows = jnp.floor((cell + 0.5) * (1.0 / nz))
+    line_x = jnp.floor((line_rows + 0.5) * (1.0 / ny))
+    line_y = line_rows - line_x * ny
+    line_late = jnp.where(line_y == 0, 2 * ny + line_x, jnp.where(line_y == ny - 1, 2 * ny + nx + line_x, -1.0))
+    line_late = jnp.where(line_x == 0, line_y, jnp.where(line_x == nx - 1, ny + line_y, line_late))
+    rows = column_of(line_rows).astype(jnp.int32)
+    z = column_of(cell - line_rows * nz).astype(jnp.int32)
+    late = column_of(line_late).astype(jnp.int32)
+    z_of[...] = z
     near = lax.broadcasted_iota(jnp.int32, (taps, nx * ny), 1)
     hot = jnp.where(near == rows, 1.0, 0.0).astype(BF16)
-    middles = slice(ny, (nx - 1) * ny)
-    for c in range(3):
-        state[c, :ny, :] = edges[0, c]
-        state[c, middles, :] = s1[c, 1 : nx - 1].reshape((nx - 2) * ny, nz)
-        state[c, (nx - 1) * ny :, :] = edges[1, c]
-    first = energies(hot, [state[c] for c in range(3)], z, nz)
+    first = energies(hot, [state[c].reshape(nx * ny, nz) for c in range(3)], z, nz)
     second = energies(hot, [s2[c].reshape(nx * ny, nz) for c in range(3)], z, nz)
     peaks[...] = jnp.maximum(first, jnp.where(late < 0, second, 0.0))
     column = lax.broadcasted_iota(jnp.int32, hot_late.shape, 1)
     hot_late[...] = jnp.where(column == late, 1.0, 0.0).astype(BF16)
     count = slots.shape[1]
     block = lax.broadcasted_iota(jnp.int32, (taps, count), 1)
-    chosen = jnp.where(block == block_of[...], jnp.broadcast_to(slots[...], (taps, count)), 0.0)
+    wanted = column_of(tap_blocks[...].astype(F32)).astype(jnp.int32)
+    chosen = jnp.where(block == wanted, jnp.broadcast_to(slots[...].astype(F32), (taps, count)), 0.0)
     slot_of[...] = jnp.sum(chosen, axis=1, keepdims=True)
 
 
@@ -254,14 +333,20 @@
         copies[-1].start()
     last = energies(hot_late[...], [late[c] for c in range(3)], z_of[...], nz)
     peak = jnp.maximum(peaks[...], last)
-    slot = lax.broadcasted_iota(jnp.int32, (peak.shape[0], best.shape[1]), 1).astype(F32)
-    best[...] = jnp.max(jnp.where(slot == slot_of[...], peak, 0.0), axis=0, keepdims=True)
+    slot = lax.broadcasted_iota(jnp.int32, (peak.shape[0], best.shape[0] * best.shape[1]), 1).astype(F32)
+    flat = jnp.max(jnp.where(slot == slot_of[...], peak, 0.0), axis=0, keepdims=True)
+    owners, each = best.shape
+    place = lax.broadcasted_iota(jnp.int32, (owners, owners * each), 1)
+    first = each * lax.broadcasted_iota(jnp.int32, (owners, owners * each), 0)
+    spread = jnp.broadcast_to(flat, place.shape)
+    for j in range(each):
+        best[:, j : j + 1] = jnp.max(jnp.where(place == first + j, spread, 0.0), axis=1, keepdims=True)
     for copy in copies:
         copy.wait()
 
 
 VM = pl.BlockSpec(memory_space=pltpu.VMEM)
-HB = pl.BlockSpec(memory_space=pl.ANY)
+HB = pl.BlockSpec(memory_space=pltpu.HBM)
 
 
 def shape(dims, kind):
@@ -271,7 +356,6 @@
 def body(velocity, viscosity, tap_cell, tap_block, block_slot):
     _, nx, ny, nz = velocity.shape
     taps = tap_cell.shape[1]
-    count = block_slot.shape[0]
     padded = pltpu.VMEM((4, nx + 2, TOP + ny + 8, PADDED), F32)
 
     def perms(axis):
@@ -282,75 +366,98 @@
     x_up, x_down = perms("gx")
     y_up, y_down = perms("gy")
 
-    own_ylo = jnp.concatenate([velocity[:, :, 0], viscosity[None, :, 0]], axis=0)
-    own_yhi = jnp.concatenate([velocity[:, :, ny - 1], viscosity[None, :, ny - 1]], axis=0)
+    own_ylo, own_yhi = pl.pallas_call(
+        y_faces,
+        out_shape=(shape((4, nx, nz), BF16),) * 2,
+        in_specs=[HB] * 2,
+        out_specs=[VM] * 2,
+        scratch_shapes=[
+            pltpu.VMEM((2, 3, nx, CHUNK, nz), BF16),
+            pltpu.VMEM((2, nx, CHUNK, nz), BF16),
+            pltpu.SemaphoreType.DMA((4,)),
+        ],
+        compiler_params=pltpu.CompilerParams(vmem_limit_bytes=60 * 2**20),
+        name="y_faces",
+    )(velocity, viscosity)
     ylo = lax.ppermute(own_yhi, "gy", y_up)
     yhi = lax.ppermute(own_ylo, "gy", y_down)
-    own_lo = jnp.concatenate([velocity[:, 0], viscosity[None, 0]], axis=0)
-    own_hi = jnp.concatenate([velocity[:, nx - 1], viscosity[None, nx - 1]], axis=0)
+    own_lo, own_hi = pl.pallas_call(
+        x_faces,
+        out_shape=(shape((4, ny, nz), BF16),) * 2,
+        in_specs=[HB] * 3,
+        out_specs=[VM] * 2,
+        scratch_shapes=[pltpu.SemaphoreType.DMA((4,))],
+        compiler_params=pltpu.CompilerParams(vmem_limit_bytes=60 * 2**20),
+        name="x_faces",
+    )(velocity, viscosity, own_ylo)
     alo = lax.ppermute(own_hi, "gx", x_up)
     ahi = lax.ppermute(own_lo, "gx", x_down)
 
-    cell = tap_cell[0]
-    row_of = cell // nz
-    z_of = (cell - row_of * nz)[:, None]
-    tap_x, tap_y = row_of // ny, row_of % ny
-    late_of = jnp.where(tap_y == 0, 2 * ny + tap_x, jnp.where(tap_y == ny - 1, 2 * ny + nx + tap_x, -1))
-    late_of = jnp.where(tap_x == 0, tap_y, jnp.where(tap_x == nx - 1, ny + tap_y, late_of))[:, None]
-    row_of = row_of[:, None]
-
     face = shape((3, ny, nz), BF16)
-    s1, edge_lo, edge_hi, part, rows = pl.pallas_call(
+    s1, part, edge_lo, edge_hi, rows = pl.pallas_call(
         first_step,
-        out_shape=(shape((3, nx, ny, nz), BF16), face, face, shape((2, 3, ny, nz), F32), shape((2, 3, nx, nz), F32)),
+        out_shape=(shape((3, nx - 2, ny, nz), BF16), shape((2, 3, ny, nz), F32), face, face, shape((2, 3, nx, nz), F32)),
         in_specs=[VM] * 4,
-        out_specs=[VM] * 5,
-        scratch_shapes=[padded],
-        compiler_params=pltpu.CompilerParams(vmem_limit_bytes=32 * 2**20),
-        cost_estimate=pl.CostEstimate(flops=3 * 10**7, bytes_accessed=6 * 10**6, transcendentals=0),
+        out_specs=[HB, HB, VM, VM, VM],
+        scratch_shapes=[
+            padded,
+            pltpu.VMEM((3, nx - 2, ny, nz), BF16),
+            pltpu.VMEM((2, 3, ny, nz), F32),
+            pltpu.SemaphoreType.DMA((nx - 1,)),
+        ],
+        compiler_params=pltpu.CompilerParams(vmem_limit_bytes=28 * 2**20),
+        cost_estimate=pl.CostEstimate(flops=10**10, bytes_accessed=6 * 10**6, transcendentals=0),
         name="first_step",
     )(velocity, viscosity, ylo, yhi)
     plo = lax.ppermute(edge_hi, "gx", x_up)
     phi = lax.ppermute(edge_lo, "gx", x_down)
 
     yface = shape((3, nx, nz), BF16)
-    edges, extra, face_lo, face_hi = pl.pallas_call(
-        first_edges,
-        out_shape=(shape((2, 3, ny, nz), BF16), shape((2, 3, ny, nz), F32), yface, yface),
-        in_specs=[VM] * 6,
-        out_specs=[VM] * 4,
-        compiler_params=pltpu.CompilerParams(vmem_limit_bytes=16 * 2**20),
-        cost_estimate=pl.CostEstimate(flops=3 * 10**6, bytes_accessed=3 * 10**6, transcendentals=0),
-        name="first_edges",
-    )(part, own_lo, own_hi, alo, ahi, rows)
+    face_lo, face_hi = pl.pallas_call(
+        first_faces,
+        out_shape=(yface, yface),
+        in_specs=[VM] * 5,
+        out_specs=[VM] * 2,
+        cost_estimate=pl.CostEstimate(flops=10**6, bytes_accessed=10**6, transcendentals=0),
+        name="first_faces",
+    )(rows, own_ylo, own_yhi, alo, ahi)
     y2lo = lax.ppermute(face_hi, "gy", y_up)
     y2hi = lax.ppermute(face_lo, "gy", y_down)
 
+    groups = lax.axis_size(("gx", "gy"))
+    each = block_slot.shape[0] // groups
     late_rows = 2 * ny + 2 * nx
-    s2, quasi, quasi_rows, blocks, coef_x, coef_y, hot_late, slot_of, peaks = pl.pallas_call(
+    s2, quasi, extra, quasi_rows, blocks, coef_x, coef_y, hot_late, z_of, slot_of, peaks = pl.pallas_call(
         second_step,
         out_shape=(
             shape((3, nx, ny, nz), BF16),
+            shape((2, 3, ny, nz), F32),
             shape((2, 3, ny, nz), F32),
             shape((2, 3, nx, nz), F32),
             shape((2, 3, nx, CHUNK, nz), BF16),
             shape((2, ny, nz), F32),
             shape((2, nx, nz), F32),
             shape((taps, late_rows), BF16),
+            shape((taps, 1), jnp.int32),
             shape((taps, 1), F32),
             shape((taps, 1), F32),
         ),
-        in_specs=[VM] * 12,
-        out_specs=[VM] * 9,
-        scratch_shapes=[padded, pltpu.VMEM((3, nx * ny, nz), BF16)],
+        in_specs=[HB, HB] + [VM] * 10,
+        out_specs=[VM] * 11,
+        scratch_shapes=[
+            padded,
+            pltpu.VMEM((3, nx, ny, nz), BF16),
+            pltpu.VMEM((2, 3, ny, nz), F32),
+            pltpu.SemaphoreType.DMA((nx - 1,)),
+        ],
         compiler_params=pltpu.CompilerParams(vmem_limit_bytes=32 * 2**20),
         cost_estimate=pl.CostEstimate(flops=3 * 10**7, bytes_accessed=8 * 10**6, transcendentals=0),
         name="second_step",
-    )(s1, edges, viscosity, alo, ahi, ylo, yhi, row_of, z_of, late_of, tap_block[0][:, None], block_slot.astype(F32)[None])
+    )(s1, part, own_lo, own_hi, viscosity, alo, ahi, ylo, yhi, tap_cell, tap_block, block_slot[None])
 
     new_velocity, best = pl.pallas_call(
         second_edges,
-        out_shape=(shape((3, nx, ny, nz), BF16), shape((1, count), F32)),
+        out_shape=(shape((3, nx, ny, nz), BF16), shape((groups, each), F32)),
         in_specs=[VM] * 14 + [HB],
         out_specs=[HB, VM],
         scratch_shapes=[
@@ -365,8 +472,7 @@
         name="second_edges",
     )(plo, phi, extra, quasi, coef_x, y2lo, y2hi, quasi_rows, coef_y, blocks, hot_late, z_of, slot_of, peaks, s2)
 
-    groups = lax.axis_size(("gx", "gy"))
-    received = lax.all_to_all(best.reshape(groups, count // groups), ("gx", "gy"), split_axis=0, concat_axis=0, tiled=True)
+    received = lax.all_to_all(best, ("gx", "gy"), split_axis=0, concat_axis=0, tiled=True)
     return new_velocity, jnp.max(received, axis=0)
 
 

time: 84.7 us -> 76.5 us (0.903)
  Pallas kernels: 22.5 us -> 30.1 us
  local copies, waits for them, and re-layouts: 14.9 us -> 9.1 us
  other arithmetic: 5.23 us -> 0.66 us
  starting transfers between devices: 21.2 us -> 17.6 us
  waiting for transfers between devices: 2.11 us -> 0.02 us
    ppermute x1, starting transfers between devices: 6.87 us -> 0.93 us  [body(): y2hi = lax.ppermute(face_lo, 'gy', y_down)]
    pallas_call x2 -> x4, Pallas kernels: 9.67 us -> 15.6 us  [the longest x1 9.66 us: body(): pl.pallas_call(first_step, out_shape=(shape((3, nx - 2, ny, nz), BF16), s...]
    slice x3 -> x0, local copies, waits for them, and re-layouts: 3.22 us -> none  [the longest x1 1.16 us: body(): velocity[:, :, 0]]
    ppermute x1, starting transfers between devices: 3.48 us -> 6.29 us  [body(): ahi = lax.ppermute(own_lo, 'gx', x_down)]
    ppermute x1, starting transfers between devices: 2.74 us -> 0.01 us  [body(): alo = lax.ppermute(own_hi, 'gx', x_up)]
    pallas_call x1, Pallas kernels: 10.5 us -> 13 us  [body(): pl.pallas_call(second_step, out_shape=(shape((3, nx, ny, nz), BF16), shap...]
    ppermute x1, starting transfers between devices: 0.26 us -> 2.58 us  [body(): y2lo = lax.ppermute(face_hi, 'gy', y_up)]
    unnamed x32, local copies, waits for them, and re-layouts: 6.86 us -> 9.1 us
  transfers between devices with their start and end apart: 8 -> 8, of which waited for: 1 -> 0; matrix products, arithmetic and copies ran while one was open for 10% -> 0% of each run, Pallas kernels for 24% -> 35%
where the time goes in v2:
time: 76.5 us; the launch traced here: 75.9 us
  Pallas kernels  30.1 us (39%)
  blocking collectives  17.7 us (23%)
  starting transfers between devices  17.6 us (23%)
  local copies, waits for them, and re-layouts  9.1 us (12%)
    all_to_all x1, blocking collectives, body(): lax.all_to_all(best, ('gx', 'gy'), split_axis=0, concat_axis=0, tiled=True)  17.7 us
    pallas_call x1, Pallas kernels, body(): pl.pallas_call(second_step, out_shape=(shape((3, nx, ny, nz), BF16), shap...  13 us
    pallas_call x1, Pallas kernels, body(): pl.pallas_call(first_step, out_shape=(shape((3, nx - 2, ny, nz), BF16), s...  9.66 us
    unnamed x32, local copies, waits for them, and re-layouts  9.1 us
    ppermute x1, starting transfers between devices, body(): ahi = lax.ppermute(own_lo, 'gx', x_down)  6.29 us
    ppermute x1, starting transfers between devices, body(): phi = lax.ppermute(edge_lo, 'gx', x_down)  4.69 us
    ppermute x1, starting transfers between devices, body(): ylo = lax.ppermute(own_yhi, 'gy', y_up)  2.76 us
    ppermute x1, starting transfers between devices, body(): y2lo = lax.ppermute(face_hi, 'gy', y_up)  2.58 us
  transfers between devices with their start and end apart: 8, of which 0 were waited for; matrix products, arithmetic and copies ran while one was open for 0% of the time, Pallas kernels for 35%

profile of v2, /device:TPU:1, one launch (start us, length us, event | category | flops | bytes accessed | tf_op | source)
XLA Modules:
  0.0 75.9 jit_solution(10695805261442511126)
XLA Ops:
  0.6 2.0 %y_faces.1 = (bf16[4,8,576]{2,1,0:T(8,128)(2,1)}, bf16[4,8,576]{2,1,0:T(8,128)(2,1)}) custom-call(bf16[3,8,64,576]{3,2,1,0:T(8,128)(2,1)} %vel.5, bf16[8,64,576]{2,1,0:T(8,128)(2,1)} %visc.7), custom_call_target="tpu_custom_call" | custom-call | tf_op jit(solution)/shard_map/y_faces/pallas_call | solution.py:369
  2.6 0.0 copy-start
  2.7 0.0 copy-start.1
  2.7 2.8 %collective-permute-start = (bf16[4,8,576]{2,1,0:T(8,128)(2,1)}, bf16[4,8,576]{2,1,0:T(8,128)(2,1)S(1)}, u32[]{:S(2)}, u32[]{:S(2)}) collective-permute-start(bf16[4,8,576]{2,1,0:T(8,128)(2,1)} %get-tuple-element.26.own_yhi), channel_id=1, source_target_pairs={{0,1},{1,2},{2,3},{3,4},{4,5},{5,6},{6,7},{7,8},{8,9},{9,10},{10,1... | collective-permute-start | bytes 110600 | tf_op jit(solution)/shard_map/ppermute | solution.py:382
  5.4 0.0 collective-permute-start.1
  5.4 2.1 %x_faces.1 = (bf16[4,64,576]{2,1,0:T(8,128)(2,1)}, bf16[4,64,576]{2,1,0:T(8,128)(2,1)}) custom-call(bf16[3,8,64,576]{3,2,1,0:T(8,128)(2,1)} %vel.5, bf16[8,64,576]{2,1,0:T(8,128)(2,1)} %visc.7, bf16[4,8,576]{2,1,0:T(8,128)(2,1)} %get-tuple-element.27.after.own_ylo), custom_call_target="tpu_custom_call" | custom-call | tf_op jit(solution)/shard_map/x_faces/pallas_call | solution.py:384
  7.5 6.3 %collective-permute-start.5 = (bf16[4,64,576]{2,1,0:T(8,128)(2,1)}, bf16[4,64,576]{2,1,0:T(8,128)(2,1)}, u32[]{:S(2)}, u32[]{:S(2)}) collective-permute-start(bf16[4,64,576]{2,1,0:T(8,128)(2,1)} %get-tuple-element.32.own_lo), channel_id=1, source_target_pairs={{16,0},{32,16},{48,32},{64,48},{80,64},{96,80},{112,96},{0,112},{1... | collective-permute-start | bytes 884744 | tf_op jit(solution)/shard_map/ppermute | solution.py:394
  13.8 0.0 copy-start.14
  13.8 0.0 collective-permute-start.4
  13.8 0.0 collective-permute-done.ylo
  13.8 0.0 copy-start.7
  13.8 0.6 copy-done.7
  14.4 0.0 collective-permute-done.1.yhi
  14.4 0.0 copy-start.10
  14.4 0.6 copy-done.10
  15.0 0.0 copy-done
  15.0 0.0 copy-done.1
  15.1 0.0 copy-start.8
  15.1 0.8 %copy-done.8 = bf16[4,8,576]{2,1,0:T(8,128)(2,1)S(1)} copy-done((bf16[4,8,576]{2,1,0:T(8,128)(2,1)S(1)}, bf16[4,8,576]{2,1,0:T(8,128)(2,1)}, u32[]{:S(2)}) %copy-start.8) | copy-done | bytes 36888
  15.8 0.0 copy-start.11
  15.8 0.8 %copy-done.11 = bf16[4,8,576]{2,1,0:T(8,128)(2,1)S(1)} copy-done((bf16[4,8,576]{2,1,0:T(8,128)(2,1)S(1)}, bf16[4,8,576]{2,1,0:T(8,128)(2,1)}, u32[]{:S(2)}) %copy-start.11) | copy-done | bytes 36888
  16.6 9.7 %first_step.1 = (bf16[3,6,64,576]{3,2,1,0:T(8,128)(2,1)S(1)}, f32[2,3,64,576]{3,2,1,0:T(8,128)S(1)}, bf16[3,64,576]{2,1,0:T(8,128)(2,1)}, bf16[3,64,576]{2,1,0:T(8,128)(2,1)}, f32[2,3,8,576]{3,2,1,0:T(8,128)S(1)}) custom-call(bf16[3,8,64,576]{3,2,1,0:T(8,128)(2,1)S(1)} %copy-done, bf16[8,64,576]{2,1,0:T(8,128)(2,1)S(1)} %copy-done.1, ...), custom_call_target="tpu_custom_call" | custom-call | flops 10000000000 | bytes 6000000 | tf_op jit(solution)/shard_map/first_step/pallas_call | solution.py:397
  26.3 0.0 copy-start.2
  26.3 0.9 %copy-done.2 = f32[2,3,64,576]{3,2,1,0:T(8,128)} copy-done((f32[2,3,64,576]{3,2,1,0:T(8,128)}, f32[2,3,64,576]{3,2,1,0:T(8,128)S(1)}, u32[]{:S(2)}) %copy-start.2) | copy-done | bytes 884760
  27.2 0.7 copy-done.6
  27.9 0.4 collective-permute-start.2
  28.3 4.7 %collective-permute-start.3 = (bf16[3,64,576]{2,1,0:T(8,128)(2,1)}, bf16[3,64,576]{2,1,0:T(8,128)(2,1)S(1)}, u32[]{:S(2)}, u32[]{:S(2)}) collective-permute-start(bf16[3,64,576]{2,1,0:T(8,128)(2,1)} %get-tuple-element.29), channel_id=1, source_target_pairs={{16,0},{32,16},{48,32},{64,48},{80,64},{96,80},{112,96},{0,112},{1... | collective-permute-start | bytes 663560 | tf_op jit(solution)/shard_map/ppermute | solution.py:413
  33.0 0.0 collective-permute-done.5.ahi
  33.0 0.0 collective-permute-done.4.alo
  33.0 1.9 %first_faces.1 = (bf16[3,8,576]{2,1,0:T(8,128)(2,1)}, bf16[3,8,576]{2,1,0:T(8,128)(2,1)}) custom-call(f32[2,3,8,576]{3,2,1,0:T(8,128)} %copy-done.6, bf16[4,8,576]{2,1,0:T(8,128)(2,1)} %get-tuple-element.27.after.own_ylo, bf16[4,8,576]{2,1,0:T(8,128)(2,1)} %get-tuple-element.26.own_yhi, bf16[4,64,576]{2,1,0:T(8,128)(2,1)} %collective-permute-done.4.alo, ...), custom_call_target="tpu_custom_call" | custom-call | flops 1000000 | bytes 1000000 | tf_op jit(solution)/shard_map/first_faces/pallas_call | solution.py:416
  34.8 2.6 %collective-permute-start.6 = (bf16[3,8,576]{2,1,0:T(8,128)(2,1)}, bf16[3,8,576]{2,1,0:T(8,128)(2,1)S(1)}, u32[]{:S(2)}, u32[]{:S(2)}) collective-permute-start(bf16[3,8,576]{2,1,0:T(8,128)(2,1)} %get-tuple-element.38), channel_id=1, source_target_pairs={{0,1},{1,2},{2,3},{3,4},{4,5},{5,6},{6,7},{7,8},{8,9},{9,10},{10,1... | collective-permute-start | bytes 82952 | tf_op jit(solution)/shard_map/ppermute | solution.py:424
  37.4 0.9 %collective-permute-start.7 = (bf16[3,8,576]{2,1,0:T(8,128)(2,1)}, bf16[3,8,576]{2,1,0:T(8,128)(2,1)S(1)}, u32[]{:S(2)}, u32[]{:S(2)}) collective-permute-start(bf16[3,8,576]{2,1,0:T(8,128)(2,1)} %get-tuple-element.39), channel_id=1, source_target_pairs={{1,0},{2,1},{3,2},{4,3},{5,4},{6,5},{7,6},{8,7},{9,8},{10,9},{11,1... | collective-permute-start | bytes 82952 | tf_op jit(solution)/shard_map/ppermute | solution.py:425
  38.4 0.0 copy-done.14
  38.4 0.0 copy-done.13
  38.4 0.0 copy-done.15
  38.4 1.2 %copy-done.3 = f32[2,3,64,576]{3,2,1,0:T(8,128)S(1)} copy-done((f32[2,3,64,576]{3,2,1,0:T(8,128)S(1)}, f32[2,3,64,576]{3,2,1,0:T(8,128)}, u32[]{:S(2)}) %copy-start.3) | copy-done | bytes 884760
  39.6 1.0 %copy-done.4 = bf16[4,64,576]{2,1,0:T(8,128)(2,1)S(1)} copy-done((bf16[4,64,576]{2,1,0:T(8,128)(2,1)S(1)}, bf16[4,64,576]{2,1,0:T(8,128)(2,1)}, u32[]{:S(2)}) %copy-start.4) | copy-done | bytes 294936
  40.5 1.0 %copy-done.5 = bf16[4,64,576]{2,1,0:T(8,128)(2,1)S(1)} copy-done((bf16[4,64,576]{2,1,0:T(8,128)(2,1)S(1)}, bf16[4,64,576]{2,1,0:T(8,128)(2,1)}, u32[]{:S(2)}) %copy-start.5) | copy-done | bytes 294936
  41.5 0.8 %copy-done.9 = bf16[4,8,576]{2,1,0:T(8,128)(2,1)S(1)} copy-done((bf16[4,8,576]{2,1,0:T(8,128)(2,1)S(1)}, bf16[4,8,576]{2,1,0:T(8,128)(2,1)}, u32[]{:S(2)}) %copy-start.9) | copy-done | bytes 36888
  42.3 0.8 %copy-done.12 = bf16[4,8,576]{2,1,0:T(8,128)(2,1)S(1)} copy-done((bf16[4,8,576]{2,1,0:T(8,128)(2,1)S(1)}, bf16[4,8,576]{2,1,0:T(8,128)(2,1)}, u32[]{:S(2)}) %copy-start.12) | copy-done | bytes 36888
  43.1 13.0 %second_step.1 = (bf16[3,8,64,576]{3,2,1,0:T(8,128)(2,1)}, f32[2,3,64,576]{3,2,1,0:T(8,128)S(1)}, f32[2,3,64,576]{3,2,1,0:T(8,128)S(1)}, f32[2,3,8,576]{3,2,1,0:...) custom-call(bf16[3,6,64,576]{3,2,1,0:T(8,128)(2,1)S(1)} %get-tuple-e, ...), custom_call_target="tpu_custom_call" | custom-call | flops 30000000 | bytes 8000000 | tf_op jit(solution)/shard_map/second_step/pallas_call | solution.py:430
  56.1 0.0 collective-permute-done.2.plo
  56.1 0.0 collective-permute-done.3.phi
  56.1 0.0 collective-permute-done.6.ylo
  56.1 0.0 collective-permute-done.7.yhi
  56.2 1.5 %second_edges.1 = (bf16[3,8,64,576]{3,2,1,0:T(8,128)(2,1)}, f32[128,4]{1,0:T(8,128)S(1)}) custom-call(bf16[3,64,576]{2,1,0:T(8,128)(2,1)S(1)} %collective-permute-done.2.plo, bf16[3,64,576]{2,1,0:T(8,128)(2,1)S(1)} %collective-permute-done.3.phi, f32[2,3,64,576]{3,2,1,0:T(8,128)S(1)} %get-tuple-element.34.extra, ...), custom_call_target="tpu_custom_call", output_to_operand_aliasing={{0}: (14, {})} | custom-call | flops 3000000 | bytes 3000000 | tf_op jit(solution)/shard_map/second_edges/pallas_call | solution.py:458
  57.6 17.7 %all_to_all.9 = f32[128,1,4]{2,1,0:T(1,128)S(1)} all-to-all(f32[128,1,4]{2,1,0:T(1,128)S(1)} %bitcast.4), channel_id=1, replica_groups=mesh['gx'=8,'gy'=16] {'gx','gy'}, dimensions={0} | all-to-all | bytes 4096 | tf_op jit(solution)/shard_map/all_to_all | solution.py:475
  75.3 0.7 reduce_max.9
  (8 shorter events, 0.0 us)
Async XLA Ops:
  2.6 12.4 %copy-start = (bf16[3,8,64,576]{3,2,1,0:T(8,128)(2,1)S(1)}, bf16[3,8,64,576]{3,2,1,0:T(8,128)(2,1)}, u32[]{:S(2)}) copy-start(bf16[3,8,64,576]{3,2,1,0:T(8,128)(2,1)} %vel.5) | copy-start | bytes 5308420
  2.7 12.4 %copy-start.1 = (bf16[8,64,576]{2,1,0:T(8,128)(2,1)S(1)}, bf16[8,64,576]{2,1,0:T(8,128)(2,1)}, u32[]{:S(2)}) copy-start(bf16[8,64,576]{2,1,0:T(8,128)(2,1)} %visc.7) | copy-start | bytes 1769476
  2.7 11.1 %collective-permute-start = (bf16[4,8,576]{2,1,0:T(8,128)(2,1)}, bf16[4,8,576]{2,1,0:T(8,128)(2,1)S(1)}, u32[]{:S(2)}, u32[]{:S(2)}) collective-permute-start(bf16[4,8,576]{2,1,0:T(8,128)(2,1)} %get-tuple-element.26.own_yhi), channel_id=1, source_target_pairs={{0,1},{1,2},{2,3},{3,4},{4,5},{5,6},{6,7},{7,8},{8,9},{9,10},{10,1... | collective-permute-start | bytes 110600 | tf_op jit(solution)/shard_map/ppermute | solution.py:382
  5.4 9.0 %collective-permute-start.1 = (bf16[4,8,576]{2,1,0:T(8,128)(2,1)}, bf16[4,8,576]{2,1,0:T(8,128)(2,1)S(1)}, u32[]{:S(2)}, u32[]{:S(2)}) collective-permute-start(bf16[4,8,576]{2,1,0:T(8,128)(2,1)} %get-tuple-element.27.after.own_ylo), channel_id=1, source_target_pairs={{1,0},{2,1},{3,2},{4,3},{5,4},{6,5},{7,6},{8,7},{9,8},{10,9},{11,1... | collective-permute-start | bytes 110600 | tf_op jit(solution)/shard_map/ppermute | solution.py:383
  7.5 25.5 %collective-permute-start.5 = (bf16[4,64,576]{2,1,0:T(8,128)(2,1)}, bf16[4,64,576]{2,1,0:T(8,128)(2,1)}, u32[]{:S(2)}, u32[]{:S(2)}) collective-permute-start(bf16[4,64,576]{2,1,0:T(8,128)(2,1)} %get-tuple-element.32.own_lo), channel_id=1, source_target_pairs={{16,0},{32,16},{48,32},{64,48},{80,64},{96,80},{112,96},{0,112},{1... | collective-permute-start | bytes 884744 | tf_op jit(solution)/shard_map/ppermute | solution.py:394
  13.8 24.6 %copy-start.14 = (s32[1,320]{1,0:T(1,128)S(1)}, s32[1,320]{1,0:T(1,128)}, u32[]{:S(2)}) copy-start(s32[1,320]{1,0:T(1,128)} %cells.1) | copy-start | bytes 3844
  13.8 19.2 %collective-permute-start.4 = (bf16[4,64,576]{2,1,0:T(8,128)(2,1)}, bf16[4,64,576]{2,1,0:T(8,128)(2,1)}, u32[]{:S(2)}, u32[]{:S(2)}) collective-permute-start(bf16[4,64,576]{2,1,0:T(8,128)(2,1)} %get-tuple-element.33.own_hi), channel_id=1, source_target_pairs={{0,16},{16,32},{32,48},{48,64},{64,80},{80,96},{96,112},{112,0},{1... | collective-permute-start | bytes 884744 | tf_op jit(solution)/shard_map/ppermute | solution.py:393
  13.8 0.6 copy-start.7
  14.4 0.6 copy-start.10
  15.1 0.8 %copy-start.8 = (bf16[4,8,576]{2,1,0:T(8,128)(2,1)S(1)}, bf16[4,8,576]{2,1,0:T(8,128)(2,1)}, u32[]{:S(2)}) copy-start(bf16[4,8,576]{2,1,0:T(8,128)(2,1)} %copy-done.7) | copy-start | bytes 110596
  15.8 0.8 %copy-start.11 = (bf16[4,8,576]{2,1,0:T(8,128)(2,1)S(1)}, bf16[4,8,576]{2,1,0:T(8,128)(2,1)}, u32[]{:S(2)}) copy-start(bf16[4,8,576]{2,1,0:T(8,128)(2,1)} %copy-done.10) | copy-start | bytes 110596
  16.6 21.8 %copy-start.13 = (s32[512]{0:T(512)S(1)}, s32[512]{0:T(512)}, u32[]{:S(2)}) copy-start(s32[512]{0:T(512)} %param.9) | copy-start | bytes 6148
  16.6 21.8 %copy-start.15 = (s32[1,320]{1,0:T(1,128)S(1)}, s32[1,320]{1,0:T(1,128)}, u32[]{:S(2)}) copy-start(s32[1,320]{1,0:T(1,128)} %tap_blocks.1) | copy-start | bytes 3844
  26.3 0.9 %copy-start.2 = (f32[2,3,64,576]{3,2,1,0:T(8,128)}, f32[2,3,64,576]{3,2,1,0:T(8,128)S(1)}, u32[]{:S(2)}) copy-start(f32[2,3,64,576]{3,2,1,0:T(8,128)S(1)} %get-tuple-element.31.part) | copy-start | bytes 2654212
  27.2 0.7 copy-start.6
  27.9 28.2 %collective-permute-start.2 = (bf16[3,64,576]{2,1,0:T(8,128)(2,1)}, bf16[3,64,576]{2,1,0:T(8,128)(2,1)S(1)}, u32[]{:S(2)}, u32[]{:S(2)}) collective-permute-start(bf16[3,64,576]{2,1,0:T(8,128)(2,1)} %get-tuple-element.28), channel_id=1, source_target_pairs={{0,16},{16,32},{32,48},{48,64},{64,80},{80,96},{96,112},{112,0},{1... | collective-permute-start | bytes 663560 | tf_op jit(solution)/shard_map/ppermute | solution.py:412
  28.3 27.8 %collective-permute-start.3 = (bf16[3,64,576]{2,1,0:T(8,128)(2,1)}, bf16[3,64,576]{2,1,0:T(8,128)(2,1)S(1)}, u32[]{:S(2)}, u32[]{:S(2)}) collective-permute-start(bf16[3,64,576]{2,1,0:T(8,128)(2,1)} %get-tuple-element.29), channel_id=1, source_target_pairs={{16,0},{32,16},{48,32},{64,48},{80,64},{96,80},{112,96},{0,112},{1... | collective-permute-start | bytes 663560 | tf_op jit(solution)/shard_map/ppermute | solution.py:413
  34.8 21.3 %collective-permute-start.6 = (bf16[3,8,576]{2,1,0:T(8,128)(2,1)}, bf16[3,8,576]{2,1,0:T(8,128)(2,1)S(1)}, u32[]{:S(2)}, u32[]{:S(2)}) collective-permute-start(bf16[3,8,576]{2,1,0:T(8,128)(2,1)} %get-tuple-element.38), channel_id=1, source_target_pairs={{0,1},{1,2},{2,3},{3,4},{4,5},{5,6},{6,7},{7,8},{8,9},{9,10},{10,1... | collective-permute-start | bytes 82952 | tf_op jit(solution)/shard_map/ppermute | solution.py:424
  37.4 18.7 %collective-permute-start.7 = (bf16[3,8,576]{2,1,0:T(8,128)(2,1)}, bf16[3,8,576]{2,1,0:T(8,128)(2,1)S(1)}, u32[]{:S(2)}, u32[]{:S(2)}) collective-permute-start(bf16[3,8,576]{2,1,0:T(8,128)(2,1)} %get-tuple-element.39), channel_id=1, source_target_pairs={{1,0},{2,1},{3,2},{4,3},{5,4},{6,5},{7,6},{8,7},{9,8},{10,9},{11,1... | collective-permute-start | bytes 82952 | tf_op jit(solution)/shard_map/ppermute | solution.py:425
  38.4 1.2 %copy-start.3 = (f32[2,3,64,576]{3,2,1,0:T(8,128)S(1)}, f32[2,3,64,576]{3,2,1,0:T(8,128)}, u32[]{:S(2)}) copy-start(f32[2,3,64,576]{3,2,1,0:T(8,128)} %copy-done.2) | copy-start | bytes 2654212
  39.6 1.0 %copy-start.4 = (bf16[4,64,576]{2,1,0:T(8,128)(2,1)S(1)}, bf16[4,64,576]{2,1,0:T(8,128)(2,1)}, u32[]{:S(2)}) copy-start(bf16[4,64,576]{2,1,0:T(8,128)(2,1)} %get-tuple-element.32.own_lo) | copy-start | bytes 884740
  40.5 1.0 %copy-start.5 = (bf16[4,64,576]{2,1,0:T(8,128)(2,1)S(1)}, bf16[4,64,576]{2,1,0:T(8,128)(2,1)}, u32[]{:S(2)}) copy-start(bf16[4,64,576]{2,1,0:T(8,128)(2,1)} %get-tuple-element.33.own_hi) | copy-start | bytes 884740
  41.5 0.8 %copy-start.9 = (bf16[4,8,576]{2,1,0:T(8,128)(2,1)S(1)}, bf16[4,8,576]{2,1,0:T(8,128)(2,1)}, u32[]{:S(2)}) copy-start(bf16[4,8,576]{2,1,0:T(8,128)(2,1)} %copy-done.7) | copy-start | bytes 110596
  42.3 0.8 %copy-start.12 = (bf16[4,8,576]{2,1,0:T(8,128)(2,1)S(1)}, bf16[4,8,576]{2,1,0:T(8,128)(2,1)}, u32[]{:S(2)}) copy-start(bf16[4,8,576]{2,1,0:T(8,128)(2,1)} %copy-done.10) | copy-start | bytes 110596

commit v3 on v2

--- a/solution.py
+++ b/solution.py
@@ -10,53 +10,75 @@
 HALF = 0.15
 TOP = 8
 CHUNK = 16
-PADDED = 640
-
-
-def put(pad, field, x, row, value, low):
+LANES = 128
+
+
+def tiles_of(nz):
+    return [(t, min(LANES, nz - t * LANES)) for t in range(-(-nz // LANES))]
+
+
+def put(pad, field, x, row, value):
     rows, nz = value.shape
-    pad[field, x, row : row + rows, :nz] = value
-    lane = lax.broadcasted_iota(jnp.int32, (rows, PADDED - nz), 1)
-    above = jnp.broadcast_to(value[:, nz - 1 : nz], lane.shape)
-    below = jnp.broadcast_to(value[:, :1], lane.shape) if low else jnp.zeros(lane.shape, F32)
-    pad[field, x, row : row + rows, nz:] = jnp.where(lane == PADDED - nz - 1, below, above)
+    for t, width in tiles_of(nz):
+        piece = value[:, t * LANES : t * LANES + width]
+        if width == LANES:
+            pad[field, x, t, row : row + rows, :] = piece
+        else:
+            pad[field, x, t, row : row + rows, :width] = piece
+            pad[field, x, t, row : row + rows, width:] = jnp.broadcast_to(piece[:, width - 1 :], (rows, LANES - width))
 
 
 def put_layer(pad, x, read_velocity, read_viscosity, ny):
     for k in range(0, ny, CHUNK):
         for c in range(3):
-            put(pad, c, x, TOP + k, read_velocity(c, k).astype(F32), False)
-        if read_viscosity is not None:
-            put(pad, 3, x, TOP + k, read_viscosity(k).astype(F32) * HALF, True)
-
-
-def update(pad, x, row):
-    here = [pad[f, x, row : row + CHUNK, :] for f in range(4)]
-    total = [here[0], here[1], here[2]]
-    for d in range(3):
-        drift = here[d] * HALF
-        if d == 2:
-            above = [pltpu.roll(v, PADDED - 1, 1) for v in here]
-            high = above[3] + here[3]
-            low = pltpu.roll(high, 1, 1)
-            ups = [above[c] - here[c] for c in range(3)]
-            downs = [pltpu.roll(u, 1, 1) for u in ups]
+            put(pad, c, x, TOP + k, read_velocity(c, k).astype(F32))
+        put(pad, 3, x, TOP + k, read_viscosity(k).astype(F32) * HALF)
+
+
+def update(pad, x, row, side, ghosts):
+    tiles = pad.shape[2]
+    lane = lax.broadcasted_iota(jnp.int32, (CHUNK, LANES), 1)
+
+    def load(f, t, dx=0, dy=0):
+        return pad[f, x + dx, t, row + dy : row + dy + CHUNK, :]
+
+    result = []
+    ahead = [pltpu.roll(load(f, 0), LANES - 1, 1) for f in range(4)]
+    behind = None
+    for t in range(tiles):
+        here = [load(f, t) for f in range(4)]
+        total = [here[0], here[1], here[2]]
+        current = ahead
+        if t + 1 < tiles:
+            ahead = [pltpu.roll(load(f, t + 1), LANES - 1, 1) for f in range(4)]
+            above_z = [jnp.where(lane == LANES - 1, ahead[f], current[f]) for f in range(4)]
         else:
-            if d == 0:
-                above = [pad[f, x + 1, row : row + CHUNK, :] for f in range(4)]
-                below = [pad[f, x - 1, row : row + CHUNK, :] for f in range(4)]
-            else:
-                above = [pad[f, x, row + 1 : row + 1 + CHUNK, :] for f in range(4)]
-                below = [pad[f, x, row - 1 : row - 1 + CHUNK, :] for f in range(4)]
-            high = above[3] + here[3]
-            low = below[3] + here[3]
-            ups = [above[c] - here[c] for c in range(3)]
-            downs = [here[c] - below[c] for c in range(3)]
-        plus = high - drift
-        minus = low + drift
-        for c in range(3):
-            total[c] = total[c] + (plus * ups[c] - minus * downs[c])
-    return total
+            above_z = current
+        turned = [pltpu.roll(here[f], 1, 1) for f in range(4)]
+        if t:
+            below_z = [jnp.where(lane == 0, behind[f], turned[f]) for f in range(4)]
+        else:
+            below_z = [jnp.where(lane == 0, here[f] if f == 3 else 0.0, turned[f]) for f in range(4)]
+        behind = turned
+        for d in range(3):
+            drift = here[d] * HALF
+            for up in (True, False):
+                missing = d == 0 and side == (1 if up else 0)
+                if missing and not ghosts:
+                    continue
+                if d == 2:
+                    far = above_z if up else below_z
+                else:
+                    step = 1 if up else -1
+                    dx, dy = (step, 0) if d == 0 else (0, step)
+                    far = [None if missing and f < 3 else load(f, t, dx, dy) for f in range(4)]
+                both = far[3] + here[3]
+                coef = both - drift if up else both + drift
+                for c in range(3):
+                    gap = here[c] if far[c] is None else (here[c] - far[c])
+                    total[c] = total[c] - coef * gap
+        result.append((here, total))
+    return result
 
 
 def y_faces(vel, visc, ylo, yhi, block_v, block_n, sems):
@@ -95,7 +117,7 @@
         copy.wait()
 
 
-def first_step(vel, visc, ylo, yhi, s1, part, edge_lo, edge_hi, rows, pad, inner, outer, sems):
+def first_step(vel, visc, ylo, yhi, s1, part, edge_lo, edge_hi, rows, pad, inner, outer, lines, sems):
     _, nx, ny, nz = vel.shape
 
     def fill(x, _):
@@ -107,24 +129,24 @@
         for f in range(4):
             value = ghost[f].astype(F32) * (HALF if f == 3 else 1.0)
             for x in range(nx):
-                put(pad, f, x + 1, row, value[x : x + 1], f == 3)
-    pad[:, 0] = pad[:, 1]
-    pad[:, nx + 1] = pad[:, nx]
+                put(pad, f, x + 1, row, value[x : x + 1])
 
     def layer(x, side):
         for k in range(0, ny, CHUNK):
-            new = update(pad, x + 1, TOP + k)
-            for c in range(3):
-                value = new[c][:, :nz]
-                if side is None:
-                    inner[c, x - 1, k : k + CHUNK, :] = value.astype(BF16)
-                else:
-                    (edge_lo, edge_hi)[side][c, k : k + CHUNK, :] = value.astype(BF16)
-                    outer[side, c, k : k + CHUNK, :] = value
-                if k == 0:
-                    rows[0, c, pl.ds(x, 1), :] = value[:1]
-                if k == ny - CHUNK:
-                    rows[1, c, pl.ds(x, 1), :] = value[CHUNK - 1 :]
+            new = update(pad, x + 1, TOP + k, side, False)
+            for t, width in tiles_of(nz):
+                part = pl.ds(t * LANES, width)
+                for c in range(3):
+                    value = new[t][1][c][:, :width]
+                    if side is None:
+                        inner[c, x - 1, k : k + CHUNK, part] = value.astype(BF16)
+                    else:
+                        (edge_lo, edge_hi)[side][c, k : k + CHUNK, part] = value.astype(BF16)
+                        outer[side, c, k : k + CHUNK, part] = value
+                    if k == 0:
+                        lines[0, c, x, :, part] = value[:1]
+                    if k == ny - CHUNK:
+                        lines[1, c, x, :, part] = value[CHUNK - 1 :]
 
     layer(0, 0)
     layer(nx - 1, 1)
@@ -144,6 +166,10 @@
         return 0
 
     lax.fori_loop(1, nx - 1, middle, 0)
+    for i in range(2):
+        for c in range(3):
+            for x in range(nx):
+                rows[i, c, x : x + 1, :] = lines[i, c, x]
     lax.fori_loop(1, nx - 1, finish, 0)
     edges_out.wait()
 
@@ -185,7 +211,7 @@
 
 
 def second_step(s1, part, own_lo, own_hi, visc, alo, ahi, ylo, yhi, cells, tap_blocks, slots,
-                s2, quasi, extra, quasi_rows, blocks, coef_x, coef_y, hot_late, z_of, slot_of, peaks, pad, state, outer, sems):
+                s2, quasi, extra, quasi_rows, blocks, coef_x, coef_y, hot_late, z_of, slot_of, peaks, pad, state, outer, strength, lines, sems):
     _, nx, ny, nz = s2.shape
     edges_in = pltpu.make_async_copy(part, outer, sems.at[0])
     edges_in.start()
@@ -202,12 +228,11 @@
     for side, (own, ghost) in enumerate(((own_lo, alo), (own_hi, ahi))):
         x = (nx - 1) * side
         beyond = (nx + 1) * side
-        pad[0:3, beyond] = jnp.zeros((3,) + pad.shape[2:], F32)
         for k in range(0, ny, CHUNK):
             mine = [own[f, k : k + CHUNK, :].astype(F32) for f in range(4)]
             far = [ghost[f, k : k + CHUNK, :].astype(F32) for f in range(4)]
             terms, far_terms = missing_terms(mine, far, 1.0 if side else -1.0)
-            put(pad, 3, beyond, TOP + k, far[3] * HALF, True)
+            put(pad, 3, beyond, TOP + k, far[3] * HALF)
             for c in range(3):
                 state[c, x, k : k + CHUNK, :] = (outer[side, c, k : k + CHUNK, :] + terms[c]).astype(BF16)
                 extra[side, c, k : k + CHUNK, :] = far_terms[c]
@@ -223,38 +248,57 @@
     fill(0, 0)
     fill(nx - 1, 0)
     lax.fori_loop(1, nx - 1, fetch_fill, 0)
+    for row in (0, TOP + ny):
+        pad[0:3, 1 : nx + 1, :, row : row + TOP, :] = jnp.zeros((3, nx, pad.shape[2], TOP, LANES), F32)
     for ghost, row in ((ylo, TOP - 1), (yhi, TOP + ny)):
         value = ghost[3].astype(F32) * HALF
         for x in range(nx):
-            put(pad, 3, x + 1, row, value[x : x + 1], True)
-            for c in range(3):
-                pad[c, x + 1, row : row + 1, :] = jnp.zeros((1, PADDED), F32)
+            put(pad, 3, x + 1, row, value[x : x + 1])
 
     for side in range(2):
         sign = 1.0 if side else -1.0
-        x, outer = 1 + (nx - 1) * side, (nx + 1) * side
-        for k in range(TOP, TOP + ny, CHUNK):
-            both = pad[3, x, k : k + CHUNK, :nz] + pad[3, outer, k : k + CHUNK, :nz]
-            coef_x[side, k - TOP : k - TOP + CHUNK, :] = both - sign * HALF * pad[0, x, k : k + CHUNK, :nz]
-        row, beyond = (TOP + ny - 1, TOP + ny) if side else (TOP, TOP - 1)
-        for x in range(nx):
-            both = pad[3, x + 1, row : row + 1, :nz] + pad[3, x + 1, beyond : beyond + 1, :nz]
-            coef_y[side, x : x + 1, :] = both - sign * HALF * pad[1, x + 1, row : row + 1, :nz]
+        x, beyond = 1 + (nx - 1) * side, (nx + 1) * side
+        row, ghost_row = (TOP + ny - 1, TOP + ny) if side else (TOP, TOP - 1)
+        for t, width in tiles_of(nz):
+            part = pl.ds(t * LANES, width)
+            for k in range(0, ny, CHUNK):
+                rows = slice(TOP + k, TOP + k + CHUNK)
+                both = pad[3, x, t, rows, :width] + pad[3, beyond, t, rows, :width]
+                coef_x[side, k : k + CHUNK, part] = both - sign * HALF * pad[0, x, t, rows, :width]
+            for y in range(nx):
+                both = pad[3, y + 1, t, row : row + 1, :width] + pad[3, y + 1, t, ghost_row : ghost_row + 1, :width]
+                coef_y[side, y : y + 1, part] = both - sign * HALF * pad[1, y + 1, t, row : row + 1, :width]
+
+    line = lax.broadcasted_iota(jnp.int32, (CHUNK, LANES), 0)
 
     def layer(x, side):
         for k in range(0, ny, CHUNK):
-            new = update(pad, x + 1, TOP + k)
-            for c in range(3):
-                value = new[c][:, :nz]
-                s2[c, x, k : k + CHUNK, :] = value.astype(BF16)
-                if side is not None:
-                    quasi[side, c, k : k + CHUNK, :] = value
-                if k == 0:
-                    quasi_rows[0, c, pl.ds(x, 1), :] = value[:1]
-                    blocks[0, c, x] = value.astype(BF16)
-                if k == ny - CHUNK:
-                    quasi_rows[1, c, pl.ds(x, 1), :] = value[CHUNK - 1 :]
-                    blocks[1, c, x] = value.astype(BF16)
+            new = update(pad, x + 1, TOP + k, side, True)
+            for t, width in tiles_of(nz):
+                part = pl.ds(t * LANES, width)
+                here, fresh = new[t]
+                rounded = [v.astype(BF16) for v in fresh]
+                energy = here[0] * here[0] + here[1] * here[1] + here[2] * here[2]
+                if side is None:
+                    again = [v.astype(F32) for v in rounded]
+                    again = again[0] * again[0] + again[1] * again[1] + again[2] * again[2]
+                    if k == 0:
+                        again = jnp.where(line == 0, 0.0, again)
+                    if k == ny - CHUNK:
+                        again = jnp.where(line == CHUNK - 1, 0.0, again)
+                    energy = jnp.maximum(energy, again)
+                strength[pl.ds(x * ny + k, CHUNK), part] = energy[:, :width].astype(BF16)
+                for c in range(3):
+                    value = fresh[c][:, :width]
+                    s2[c, x, k : k + CHUNK, part] = rounded[c][:, :width]
+                    if side is not None:
+                        quasi[side, c, k : k + CHUNK, part] = value
+                    if k == 0:
+                        lines[0, c, x, :, part] = value[:1]
+                        blocks[0, c, x, :, part] = rounded[c][:, :width]
+                    if k == ny - CHUNK:
+                        lines[1, c, x, :, part] = value[CHUNK - 1 :]
+                        blocks[1, c, x, :, part] = rounded[c][:, :width]
 
     layer(0, 0)
     layer(nx - 1, 1)
@@ -264,6 +308,11 @@
         return 0
 
     lax.fori_loop(1, nx - 1, middle, 0)
+
+    for i in range(2):
+        for c in range(3):
+            for x in range(nx):
+                quasi_rows[i, c, x : x + 1, :] = lines[i, c, x]
 
     taps = cells.shape[1]
     same = lax.broadcasted_iota(jnp.int32, (taps, taps), 0) == lax.broadcasted_iota(jnp.int32, (taps, taps), 1)
@@ -283,9 +332,9 @@
     z_of[...] = z
     near = lax.broadcasted_iota(jnp.int32, (taps, nx * ny), 1)
     hot = jnp.where(near == rows, 1.0, 0.0).astype(BF16)
-    first = energies(hot, [state[c].reshape(nx * ny, nz) for c in range(3)], z, nz)
-    second = energies(hot, [s2[c].reshape(nx * ny, nz) for c in range(3)], z, nz)
-    peaks[...] = jnp.maximum(first, jnp.where(late < 0, second, 0.0))
+    picked = jnp.dot(hot, strength[...], preferred_element_type=F32)
+    lane = lax.broadcasted_iota(jnp.int32, picked.shape, 1)
+    peaks[...] = jnp.max(jnp.where(lane == z, picked, 0.0), axis=1, keepdims=True)
     column = lax.broadcasted_iota(jnp.int32, hot_late.shape, 1)
     hot_late[...] = jnp.where(column == late, 1.0, 0.0).astype(BF16)
     count = slots.shape[1]
@@ -356,7 +405,7 @@
 def body(velocity, viscosity, tap_cell, tap_block, block_slot):
     _, nx, ny, nz = velocity.shape
     taps = tap_cell.shape[1]
-    padded = pltpu.VMEM((4, nx + 2, TOP + ny + 8, PADDED), F32)
+    padded = pltpu.VMEM((4, nx + 2, len(tiles_of(nz)), TOP + ny + 8, LANES), F32)
 
     def perms(axis):
         peers = lax.axis_size(axis)
@@ -403,6 +452,7 @@
             padded,
             pltpu.VMEM((3, nx - 2, ny, nz), BF16),
             pltpu.VMEM((2, 3, ny, nz), F32),
+            pltpu.VMEM((2, 3, nx, 1, nz), F32),
             pltpu.SemaphoreType.DMA((nx - 1,)),
         ],
         compiler_params=pltpu.CompilerParams(vmem_limit_bytes=28 * 2**20),
@@ -418,6 +468,7 @@
         out_shape=(yface, yface),
         in_specs=[VM] * 5,
         out_specs=[VM] * 2,
+        compiler_params=pltpu.CompilerParams(vmem_limit_bytes=4 * 2**20),
         cost_estimate=pl.CostEstimate(flops=10**6, bytes_accessed=10**6, transcendentals=0),
         name="first_faces",
     )(rows, own_ylo, own_yhi, alo, ahi)
@@ -448,6 +499,8 @@
             padded,
             pltpu.VMEM((3, nx, ny, nz), BF16),
             pltpu.VMEM((2, 3, ny, nz), F32),
+            pltpu.VMEM((nx * ny, nz), BF16),
+            pltpu.VMEM((2, 3, nx, 1, nz), F32),
             pltpu.SemaphoreType.DMA((nx - 1,)),
         ],
         compiler_params=pltpu.CompilerParams(vmem_limit_bytes=32 * 2**20),

time: 76.5 us -> 61.1 us (0.80)
  Pallas kernels: 30.1 us -> 19.9 us
  local copies, waits for them, and re-layouts: 9.1 us -> 0.05 us
  waiting for transfers between devices: 0.02 us -> 2.38 us
  starting transfers between devices: 17.6 us -> 19.7 us
    unnamed x32 -> x18, local copies, waits for them, and re-layouts: 9.1 us -> 0.05 us
    pallas_call x1, Pallas kernels: 13 us -> 8.32 us  [body(): pl.pallas_call(second_step, out_shape=(shape((3, nx, ny, nz), BF16), shap...]
    pallas_call x1, Pallas kernels: 9.66 us -> 5.99 us  [body(): pl.pallas_call(first_step, out_shape=(shape((3, nx - 2, ny, nz), BF16), s...]
    ppermute x1, waiting for transfers between devices: 0.01 us -> 2.36 us  [body(): alo = lax.ppermute(own_hi, 'gx', x_up)]
    ppermute x1, starting transfers between devices: 2.58 us -> 4.66 us  [body(): y2lo = lax.ppermute(face_hi, 'gy', y_up)]
    pallas_call x1, Pallas kernels: 1.86 us -> 0.09 us  [body(): pl.pallas_call(first_faces, out_shape=(yface, yface), in_specs=[VM] * 5,...]
  transfers between devices with their start and end apart: 8 -> 8, of which waited for: 0 -> 1; matrix products, arithmetic and copies ran while one was open for 0% -> 0% of each run, Pallas kernels for 35% -> 27%
where the time goes in v3:
time: 61.1 us; the launch traced here: 60.9 us
  Pallas kernels  19.9 us (33%)
  starting transfers between devices  19.7 us (32%)
  blocking collectives  17.4 us (28%)
  waiting for transfers between devices  2.38 us (4%)
  between operations  0.81 us (1%)
  other arithmetic  0.66 us (1%)
    all_to_all x1, blocking collectives, body(): lax.all_to_all(best, ('gx', 'gy'), split_axis=0, concat_axis=0, tiled=True)  17.4 us
    pallas_call x1, Pallas kernels, body(): pl.pallas_call(second_step, out_shape=(shape((3, nx, ny, nz), BF16), shap...  8.32 us
    ppermute x1, starting transfers between devices, body(): ahi = lax.ppermute(own_lo, 'gx', x_down)  6.29 us
    pallas_call x1, Pallas kernels, body(): pl.pallas_call(first_step, out_shape=(shape((3, nx - 2, ny, nz), BF16), s...  5.99 us
    ppermute x1, starting transfers between devices, body(): phi = lax.ppermute(edge_lo, 'gx', x_down)  4.76 us
    ppermute x1, starting transfers between devices, body(): y2lo = lax.ppermute(face_hi, 'gy', y_up)  4.66 us
    ppermute x1, starting transfers between devices, body(): ylo = lax.ppermute(own_yhi, 'gy', y_up)  2.76 us
    ppermute x1, waiting for transfers between devices, body(): alo = lax.ppermute(own_hi, 'gx', x_up)  2.36 us
  transfers between devices with their start and end apart: 8, of which 1 were waited for; matrix products, arithmetic and copies ran while one was open for 0% of the time, Pallas kernels for 27%

profile of v3, /device:TPU:1, one launch (start us, length us, event | category | flops | bytes accessed | tf_op | source)
XLA Modules:
  0.0 60.9 jit_solution(5662935183037109515)
XLA Ops:
  0.6 2.0 %y_faces.1 = (bf16[4,8,576]{2,1,0:T(8,128)(2,1)}, bf16[4,8,576]{2,1,0:T(8,128)(2,1)}) custom-call(bf16[3,8,64,576]{3,2,1,0:T(8,128)(2,1)} %vel.5, bf16[8,64,576]{2,1,0:T(8,128)(2,1)} %visc.7), custom_call_target="tpu_custom_call" | custom-call | tf_op jit(solution)/shard_map/y_faces/pallas_call | solution.py:418
  2.6 0.0 copy-start
  2.6 0.0 copy-start.1
  2.7 2.8 %collective-permute-start = (bf16[4,8,576]{2,1,0:T(8,128)(2,1)}, bf16[4,8,576]{2,1,0:T(8,128)(2,1)S(1)}, u32[]{:S(2)}, u32[]{:S(2)}) collective-permute-start(bf16[4,8,576]{2,1,0:T(8,128)(2,1)} %get-tuple-element.26.own_yhi), channel_id=1, source_target_pairs={{0,1},{1,2},{2,3},{3,4},{4,5},{5,6},{6,7},{7,8},{8,9},{9,10},{10,1... | collective-permute-start | bytes 110600 | tf_op jit(solution)/shard_map/ppermute | solution.py:431
  5.4 0.0 collective-permute-start.1
  5.4 2.0 %x_faces.1 = (bf16[4,64,576]{2,1,0:T(8,128)(2,1)}, bf16[4,64,576]{2,1,0:T(8,128)(2,1)}) custom-call(bf16[3,8,64,576]{3,2,1,0:T(8,128)(2,1)} %vel.5, bf16[8,64,576]{2,1,0:T(8,128)(2,1)} %visc.7, bf16[4,8,576]{2,1,0:T(8,128)(2,1)} %get-tuple-element.27.after.own_ylo), custom_call_target="tpu_custom_call" | custom-call | tf_op jit(solution)/shard_map/x_faces/pallas_call | solution.py:433
  7.5 6.3 %collective-permute-start.5 = (bf16[4,64,576]{2,1,0:T(8,128)(2,1)}, bf16[4,64,576]{2,1,0:T(8,128)(2,1)S(1)}, u32[]{:S(2)}, u32[]{:S(2)}) collective-permute-start(bf16[4,64,576]{2,1,0:T(8,128)(2,1)} %get-tuple-element.32.own_lo), channel_id=1, source_target_pairs={{16,0},{32,16},{48,32},{64,48},{80,64},{96,80},{112,96},{0,112},{1... | collective-permute-start | bytes 884744 | tf_op jit(solution)/shard_map/ppermute | solution.py:443
  13.8 0.0 copy-start.4
  13.8 0.0 copy-start.5
  13.8 0.0 copy-start.2
  13.8 0.0 copy-start.3
  13.8 0.0 copy-start.6
  13.8 0.0 copy-start.7
  13.8 0.0 copy-start.8
  13.8 0.1 collective-permute-start.4
  13.9 0.0 collective-permute-done.ylo
  13.9 0.0 collective-permute-done.1.yhi
  13.9 0.0 copy-done
  13.9 0.0 copy-done.1
  13.9 6.0 %first_step.1 = (bf16[3,6,64,576]{3,2,1,0:T(8,128)(2,1)S(1)}, f32[2,3,64,576]{3,2,1,0:T(8,128)S(1)}, bf16[3,64,576]{2,1,0:T(8,128)(2,1)S(1)}, bf16[3,64,576]{2,1,0:T(8,128)(2,1)S(1)}, f32[2,3,8,576]{3,2,1,0:T(8,128)S(1)}) custom-call(bf16[3,8,64,576]{3,2,1,0:T(8,128)(2,1)S(1)} %copy-done, bf16[8,64,576]{2,1,0:T(8,128)(2,1)S(1)} %copy-done.1, ...), custom_call_target="tpu_custom_call" | custom-call | flops 10000000000 | bytes 6000000 | tf_op jit(solution)/shard_map/first_step/pallas_call | solution.py:446
  19.9 0.4 collective-permute-start.2
  20.4 4.8 %collective-permute-start.3 = (bf16[3,64,576]{2,1,0:T(8,128)(2,1)S(1)}, bf16[3,64,576]{2,1,0:T(8,128)(2,1)S(1)}, u32[]{:S(2)}, u32[]{:S(2)}) collective-permute-start(bf16[3,64,576]{2,1,0:T(8,128)(2,1)S(1)} %get-tuple-element.29), channel_id=1, source_target_pairs={{16,0},{32,16},{48,32},{64,48},{80,64},{96,80},{112,96},{0,112},{1... | collective-permute-start | bytes 663560 | tf_op jit(solution)/shard_map/ppermute | solution.py:463
  25.1 0.0 collective-permute-done.5.ahi
  25.1 2.4 %collective-permute-done.4.alo = bf16[4,64,576]{2,1,0:T(8,128)(2,1)S(1)} collective-permute-done((bf16[4,64,576]{2,1,0:T(8,128)(2,1)}, bf16[4,64,576]{2,1,0:T(8,128)(2,1)S(1)}, u32[]{:S(2)}, u32[]{:S(2)}) %collective-permute-start.4) | collective-permute-done | bytes 294944 | tf_op jit(solution)/shard_map/ppermute | solution.py:442
  27.5 0.0 copy-done.4
  27.5 0.0 copy-done.5
  27.5 0.1 first_faces.1
  27.6 4.7 %collective-permute-start.6 = (bf16[3,8,576]{2,1,0:T(8,128)(2,1)S(1)}, bf16[3,8,576]{2,1,0:T(8,128)(2,1)S(1)}, u32[]{:S(2)}, u32[]{:S(2)}) collective-permute-start(bf16[3,8,576]{2,1,0:T(8,128)(2,1)S(1)} %get-tuple-element.38), channel_id=1, source_target_pairs={{0,1},{1,2},{2,3},{3,4},{4,5},{5,6},{6,7},{7,8},{8,9},{9,10},{10,1... | collective-permute-start | bytes 82952 | tf_op jit(solution)/shard_map/ppermute | solution.py:475
  32.2 0.7 %collective-permute-start.7 = (bf16[3,8,576]{2,1,0:T(8,128)(2,1)S(1)}, bf16[3,8,576]{2,1,0:T(8,128)(2,1)S(1)}, u32[]{:S(2)}, u32[]{:S(2)}) collective-permute-start(bf16[3,8,576]{2,1,0:T(8,128)(2,1)S(1)} %get-tuple-element.39), channel_id=1, source_target_pairs={{1,0},{2,1},{3,2},{4,3},{5,4},{6,5},{7,6},{8,7},{9,8},{10,9},{11,1... | collective-permute-start | bytes 82952 | tf_op jit(solution)/shard_map/ppermute | solution.py:476
  33.0 0.0 copy-done.2
  33.0 0.0 copy-done.3
  33.0 0.0 copy-done.6
  33.0 0.0 copy-done.7
  33.0 0.0 copy-done.8
  33.0 8.3 %second_step.1 = (bf16[3,8,64,576]{3,2,1,0:T(8,128)(2,1)}, f32[2,3,64,576]{3,2,1,0:T(8,128)S(1)}, f32[2,3,64,576]{3,2,1,0:T(8,128)S(1)}, f32[2,3,8,576]{3,2,1,0:...) custom-call(bf16[3,6,64,576]{3,2,1,0:T(8,128)(2,1)S(1)} %get-tuple-e, ...), custom_call_target="tpu_custom_call" | custom-call | flops 30000000 | bytes 8000000 | tf_op jit(solution)/shard_map/second_step/pallas_call | solution.py:481
  41.3 0.0 collective-permute-done.2.plo
  41.4 0.0 collective-permute-done.3.phi
  41.4 0.0 collective-permute-done.6.ylo
  41.4 0.0 collective-permute-done.7.yhi
  41.4 1.5 %second_edges.1 = (bf16[3,8,64,576]{3,2,1,0:T(8,128)(2,1)}, f32[128,4]{1,0:T(8,128)S(1)}) custom-call(bf16[3,64,576]{2,1,0:T(8,128)(2,1)S(1)} %collective-permute-done.2.plo, bf16[3,64,576]{2,1,0:T(8,128)(2,1)S(1)} %collective-permute-done.3.phi, f32[2,3,64,576]{3,2,1,0:T(8,128)S(1)} %get-tuple-element.34.extra, ...), custom_call_target="tpu_custom_call", output_to_operand_aliasing={{0}: (14, {})} | custom-call | flops 3000000 | bytes 3000000 | tf_op jit(solution)/shard_map/second_edges/pallas_call | solution.py:511
  42.9 17.4 %all_to_all.9 = f32[128,1,4]{2,1,0:T(1,128)S(1)} all-to-all(f32[128,1,4]{2,1,0:T(1,128)S(1)} %bitcast.4), channel_id=1, replica_groups=mesh['gx'=8,'gy'=16] {'gx','gy'}, dimensions={0} | all-to-all | bytes 4096 | tf_op jit(solution)/shard_map/all_to_all | solution.py:528
  60.3 0.7 %reduce_max.9 = f32[4]{0:T(128)} reduce(f32[128,1,4]{2,1,0:T(1,128)S(1)} %all_to_all.9, f32[]{:T(128)} %constant.0.clone.1), dimensions={0,1}, to_apply=%region_0.0 | reduce | flops 508 | bytes 2068 | tf_op jit(solution)/shard_map/reduce_max | solution.py:529
Async XLA Ops:
  2.6 11.3 %copy-start = (bf16[3,8,64,576]{3,2,1,0:T(8,128)(2,1)S(1)}, bf16[3,8,64,576]{3,2,1,0:T(8,128)(2,1)}, u32[]{:S(2)}) copy-start(bf16[3,8,64,576]{3,2,1,0:T(8,128)(2,1)} %vel.5) | copy-start | bytes 5308420
  2.6 11.3 %copy-start.1 = (bf16[8,64,576]{2,1,0:T(8,128)(2,1)S(1)}, bf16[8,64,576]{2,1,0:T(8,128)(2,1)}, u32[]{:S(2)}) copy-start(bf16[8,64,576]{2,1,0:T(8,128)(2,1)} %visc.7) | copy-start | bytes 1769476
  2.7 11.2 %collective-permute-start = (bf16[4,8,576]{2,1,0:T(8,128)(2,1)}, bf16[4,8,576]{2,1,0:T(8,128)(2,1)S(1)}, u32[]{:S(2)}, u32[]{:S(2)}) collective-permute-start(bf16[4,8,576]{2,1,0:T(8,128)(2,1)} %get-tuple-element.26.own_yhi), channel_id=1, source_target_pairs={{0,1},{1,2},{2,3},{3,4},{4,5},{5,6},{6,7},{7,8},{8,9},{9,10},{10,1... | collective-permute-start | bytes 110600 | tf_op jit(solution)/shard_map/ppermute | solution.py:431
  5.4 8.5 %collective-permute-start.1 = (bf16[4,8,576]{2,1,0:T(8,128)(2,1)}, bf16[4,8,576]{2,1,0:T(8,128)(2,1)S(1)}, u32[]{:S(2)}, u32[]{:S(2)}) collective-permute-start(bf16[4,8,576]{2,1,0:T(8,128)(2,1)} %get-tuple-element.27.after.own_ylo), channel_id=1, source_target_pairs={{1,0},{2,1},{3,2},{4,3},{5,4},{6,5},{7,6},{8,7},{9,8},{10,9},{11,1... | collective-permute-start | bytes 110600 | tf_op jit(solution)/shard_map/ppermute | solution.py:432
  7.5 17.7 %collective-permute-start.5 = (bf16[4,64,576]{2,1,0:T(8,128)(2,1)}, bf16[4,64,576]{2,1,0:T(8,128)(2,1)S(1)}, u32[]{:S(2)}, u32[]{:S(2)}) collective-permute-start(bf16[4,64,576]{2,1,0:T(8,128)(2,1)} %get-tuple-element.32.own_lo), channel_id=1, source_target_pairs={{16,0},{32,16},{48,32},{64,48},{80,64},{96,80},{112,96},{0,112},{1... | collective-permute-start | bytes 884744 | tf_op jit(solution)/shard_map/ppermute | solution.py:443
  13.8 13.7 %copy-start.4 = (bf16[4,8,576]{2,1,0:T(8,128)(2,1)S(1)}, bf16[4,8,576]{2,1,0:T(8,128)(2,1)}, u32[]{:S(2)}) copy-start(bf16[4,8,576]{2,1,0:T(8,128)(2,1)} %get-tuple-element.27.after.own_ylo) | copy-start | bytes 110596
  13.8 13.7 %copy-start.5 = (bf16[4,8,576]{2,1,0:T(8,128)(2,1)S(1)}, bf16[4,8,576]{2,1,0:T(8,128)(2,1)}, u32[]{:S(2)}) copy-start(bf16[4,8,576]{2,1,0:T(8,128)(2,1)} %get-tuple-element.26.own_yhi) | copy-start | bytes 110596
  13.8 19.2 %copy-start.2 = (bf16[4,64,576]{2,1,0:T(8,128)(2,1)S(1)}, bf16[4,64,576]{2,1,0:T(8,128)(2,1)}, u32[]{:S(2)}) copy-start(bf16[4,64,576]{2,1,0:T(8,128)(2,1)} %get-tuple-element.32.own_lo) | copy-start | bytes 884740
  13.8 19.2 %copy-start.3 = (bf16[4,64,576]{2,1,0:T(8,128)(2,1)S(1)}, bf16[4,64,576]{2,1,0:T(8,128)(2,1)}, u32[]{:S(2)}) copy-start(bf16[4,64,576]{2,1,0:T(8,128)(2,1)} %get-tuple-element.33.own_hi) | copy-start | bytes 884740
  13.8 19.2 %copy-start.6 = (s32[512]{0:T(512)S(1)}, s32[512]{0:T(512)}, u32[]{:S(2)}) copy-start(s32[512]{0:T(512)} %param.9) | copy-start | bytes 6148
  13.8 19.2 %copy-start.7 = (s32[1,320]{1,0:T(1,128)S(1)}, s32[1,320]{1,0:T(1,128)}, u32[]{:S(2)}) copy-start(s32[1,320]{1,0:T(1,128)} %cells.1) | copy-start | bytes 3844
  13.8 19.2 %copy-start.8 = (s32[1,320]{1,0:T(1,128)S(1)}, s32[1,320]{1,0:T(1,128)}, u32[]{:S(2)}) copy-start(s32[1,320]{1,0:T(1,128)} %tap_blocks.1) | copy-start | bytes 3844
  13.8 13.7 %collective-permute-start.4 = (bf16[4,64,576]{2,1,0:T(8,128)(2,1)}, bf16[4,64,576]{2,1,0:T(8,128)(2,1)S(1)}, u32[]{:S(2)}, u32[]{:S(2)}) collective-permute-start(bf16[4,64,576]{2,1,0:T(8,128)(2,1)} %get-tuple-element.33.own_hi), channel_id=1, source_target_pairs={{0,16},{16,32},{32,48},{48,64},{64,80},{80,96},{96,112},{112,0},{1... | collective-permute-start | bytes 884744 | tf_op jit(solution)/shard_map/ppermute | solution.py:442
  19.9 21.4 %collective-permute-start.2 = (bf16[3,64,576]{2,1,0:T(8,128)(2,1)S(1)}, bf16[3,64,576]{2,1,0:T(8,128)(2,1)S(1)}, u32[]{:S(2)}, u32[]{:S(2)}) collective-permute-start(bf16[3,64,576]{2,1,0:T(8,128)(2,1)S(1)} %get-tuple-element.28), channel_id=1, source_target_pairs={{0,16},{16,32},{32,48},{48,64},{64,80},{80,96},{96,112},{112,0},{1... | collective-permute-start | bytes 663560 | tf_op jit(solution)/shard_map/ppermute | solution.py:462
  20.4 21.0 %collective-permute-start.3 = (bf16[3,64,576]{2,1,0:T(8,128)(2,1)S(1)}, bf16[3,64,576]{2,1,0:T(8,128)(2,1)S(1)}, u32[]{:S(2)}, u32[]{:S(2)}) collective-permute-start(bf16[3,64,576]{2,1,0:T(8,128)(2,1)S(1)} %get-tuple-element.29), channel_id=1, source_target_pairs={{16,0},{32,16},{48,32},{64,48},{80,64},{96,80},{112,96},{0,112},{1... | collective-permute-start | bytes 663560 | tf_op jit(solution)/shard_map/ppermute | solution.py:463
  27.6 13.8 %collective-permute-start.6 = (bf16[3,8,576]{2,1,0:T(8,128)(2,1)S(1)}, bf16[3,8,576]{2,1,0:T(8,128)(2,1)S(1)}, u32[]{:S(2)}, u32[]{:S(2)}) collective-permute-start(bf16[3,8,576]{2,1,0:T(8,128)(2,1)S(1)} %get-tuple-element.38), channel_id=1, source_target_pairs={{0,1},{1,2},{2,3},{3,4},{4,5},{5,6},{6,7},{7,8},{8,9},{9,10},{10,1... | collective-permute-start | bytes 82952 | tf_op jit(solution)/shard_map/ppermute | solution.py:475
  32.2 9.1 %collective-permute-start.7 = (bf16[3,8,576]{2,1,0:T(8,128)(2,1)S(1)}, bf16[3,8,576]{2,1,0:T(8,128)(2,1)S(1)}, u32[]{:S(2)}, u32[]{:S(2)}) collective-permute-start(bf16[3,8,576]{2,1,0:T(8,128)(2,1)S(1)} %get-tuple-element.39), channel_id=1, source_target_pairs={{1,0},{2,1},{3,2},{4,3},{5,4},{6,5},{7,6},{8,7},{9,8},{10,9},{11,1... | collective-permute-start | bytes 82952 | tf_op jit(solution)/shard_map/ppermute | solution.py:476

commit v4 on v0

v4 whole, which is shorter than its diff:
```python
import jax
import jax.numpy as jnp
from jax import lax
from jax.experimental import pallas as pl
from jax.experimental.pallas import tpu as pltpu
from jax.sharding import PartitionSpec as P

F32 = jnp.float32
BF16 = jnp.bfloat16
HALF = 0.15
TOP = 8
CHUNK = 16
LANES = 128


def tiles_of(nz):
    return [(t, min(LANES, nz - t * LANES)) for t in range(-(-nz // LANES))]


def put(pad, index, row, value):
    rows, nz = value.shape
    for t, width in tiles_of(nz):
        pad[(*index, t, slice(row, row + rows), slice(0, width))] = value[:, t * LANES : t * LANES + width]


def update(load, packed, side, ghosts, nz):
    lane = lax.broadcasted_iota(jnp.int32, (CHUNK, LANES), 1)

    def tile(t, width):
        values = [packed(f, pl.ds(t * LANES, width)) for f in range(4)]
        if width < LANES:
            values = [jnp.concatenate([v, jnp.zeros((CHUNK, LANES - width), BF16)], axis=1) for v in values]
        return values

    def wide(values):
        return [v.astype(F32) * HALF if f == 3 else v.astype(F32) for f, v in enumerate(values)]

    spans = tiles_of(nz)
    result = []
    own = tile(*spans[0])
    ahead = [pltpu.roll(v, LANES - 1, 1) for v in own]
    behind = None
    for t, width in spans:
        here = [load(f, t, 0, 0) for f in range(4)]
        current, now = ahead, own
        if t + 1 < len(spans):
            own = tile(*spans[t + 1])
            ahead = [pltpu.roll(v, LANES - 1, 1) for v in own]
            beyond = ahead
        else:
            beyond = now
        above_z = wide([jnp.where(lane == width - 1, beyond[f], current[f]) for f in range(4)])
        turned = [pltpu.roll(v, 1, 1) for v in now]
        if t:
            before = behind
        else:
            before = [jnp.zeros((CHUNK, LANES), BF16)] * 3 + [now[3]]
        below_z = wide([jnp.where(lane == 0, before[f], turned[f]) for f in range(4)])
        behind = turned
        weight = None
        terms = [[], [], []]
        for d in range(3):
            drift = here[d] * HALF
            for up in (True, False):
                missing = d == 0 and side == (1 if up else 0)
                if missing and not ghosts:
                    weight = drift if up else weight - drift
                    continue
                if d == 2:
                    far = above_z if up else below_z
                else:
                    step = 1 if up else -1
                    dx, dy = (step, 0) if d == 0 else (0, step)
                    far = [None if missing and f < 3 else load(f, t, dx, dy) for f in range(4)]
                both = far[3] + here[3]
                weight = both if weight is None else weight + both
                if far[0] is not None:
                    coef = both - drift if up else both + drift
                    for c in range(3):
                        terms[c].append(coef * far[c])
        weight = 1.0 - weight
        total = [here[c] * weight for c in range(3)]
        for c in range(3):
            for term in terms[c]:
                total[c] = total[c] + term
        result.append((here, total))
    return result


def x_face(vel, visc, lo, sems):
    copies = [pltpu.make_async_copy(vel.at[:, 0], lo.at[0:3], sems.at[0]), pltpu.make_async_copy(visc.at[0], lo.at[3], sems.at[1])]
    for copy in copies:
        copy.start()
    for copy in copies:
        copy.wait()


def other_faces(vel, visc, after, ylo, yhi, hi):
    _, nx, ny, nz = vel.shape
    hi[0:3] = vel[:, nx - 1]
    hi[3] = visc[nx - 1]
    line = lax.broadcasted_iota(jnp.int32, (nx, nz), 0)
    for i, out in enumerate((ylo, yhi)):
        rows = slice((ny - CHUNK) * i, (ny - CHUNK) * i + CHUNK)
        row = (CHUNK - 1) * i
        for f in range(4):
            total = jnp.zeros((nx, nz), F32)
            for x in range(nx):
                block = visc[x, rows] if f == 3 else vel[f, x, rows]
                one = block.astype(F32)[row : row + 1]
                total = jnp.where(line == x, jnp.broadcast_to(one, line.shape), total)
            out[f] = total.astype(BF16)


def first_step(vel, visc, ylo, yhi, next_pad, nu_pad, packed, edge_lo, edge_hi, rows, pad, lines):
    _, nx, ny, nz = vel.shape
    tiles = len(tiles_of(nz))

    def fill(x, _):
        for k in range(0, ny, CHUNK):
            for c in range(3):
                put(pad, (c, x), TOP + k, vel[c, x, k : k + CHUNK, :].astype(F32))
            put(nu_pad, (x,), TOP + k, visc[x, k : k + CHUNK, :].astype(F32) * HALF)
        return 0

    lax.fori_loop(0, nx, fill, 0)
    for ghost, row in ((ylo, TOP - 1), (yhi, TOP + ny)):
        for f in range(4):
            value = ghost[f].astype(F32) * (HALF if f == 3 else 1.0)
            for x in range(nx):
                if f == 3:
                    put(nu_pad, (x,), row, value[x : x + 1])
                else:
                    put(pad, (f, x), row, value[x : x + 1])
    for row in (0, TOP + ny):
        next_pad[:, :, :, row : row + TOP, :] = jnp.zeros((3, nx, tiles, TOP, LANES), F32)

    def layer(x, side):
        for k in range(0, ny, CHUNK):

            def load(f, t, dx, dy):
                window = pl.ds(TOP + k + dy, CHUNK)
                return nu_pad[x + dx, t, window, :] if f == 3 else pad[f, x + dx, t, window, :]

            def bits(f, part):
                return visc[x, k : k + CHUNK, part] if f == 3 else vel[f, x, k : k + CHUNK, part]

            new = update(load, bits, side, False, nz)
            for t, width in tiles_of(nz):
                part = pl.ds(t * LANES, width)
                for c in range(3):
                    value = new[t][1][c]
                    rounded = value.astype(BF16)
                    if k == 0:
                        lines[0, c, x, :, part] = value[:1, :width]
                    if k == ny - CHUNK:
                        lines[1, c, x, :, part] = value[CHUNK - 1 :, :width]
                    if side is not None:
                        (edge_lo, edge_hi)[side][c, k : k + CHUNK, part] = rounded[:, :width]
                    else:
                        value = rounded.astype(F32)
                        packed[c, x - 1, k : k + CHUNK, part] = rounded[:, :width]
                    next_pad[c, x, t, TOP + k : TOP + k + CHUNK, :] = value

    layer(0, 0)
    layer(nx - 1, 1)

    def middle(x, _):
        layer(x, None)
        return 0

    lax.fori_loop(1, nx - 1, middle, 0)
    for i in range(2):
        for c in range(3):
            for x in range(nx):
                rows[i, c, x : x + 1, :] = lines[i, c, x]


def missing_terms(mine, far, sign):
    both = (mine[3] + far[3]) * HALF
    near_coef = both - sign * HALF * mine[0]
    far_coef = both + sign * HALF * far[0]
    gaps = [far[c] - mine[c] for c in range(3)]
    return [near_coef * g for g in gaps], [-far_coef * g for g in gaps]


def first_faces(rows, own_ylo, own_yhi, alo, ahi, after, face_lo, face_hi):
    _, _, nx, nz = rows.shape
    ny = alo.shape[1]
    line = lax.broadcasted_iota(jnp.int32, (nx, nz), 0)
    for i, (own, out) in enumerate(((own_ylo, face_lo), (own_yhi, face_hi))):
        values = [rows[i, c] for c in range(3)]
        for side, ghost in enumerate((alo, ahi)):
            x = (nx - 1) * side
            k = (ny - CHUNK) * i
            row = (CHUNK - 1) * i
            mine = [own[f].astype(F32)[x : x + 1] for f in range(4)]
            far = [ghost[f, k : k + CHUNK, :].astype(F32)[row : row + 1] for f in range(4)]
            terms, _ = missing_terms(mine, far, 1.0 if side else -1.0)
            for c in range(3):
                values[c] = values[c] + jnp.where(line == x, jnp.broadcast_to(terms[c], line.shape), 0.0)
        for c in range(3):
            out[c] = values[c].astype(BF16)


def emit(new, nz, k, ny, store, strength, strength_row, blocks, lines, both_steps):
    line = lax.broadcasted_iota(jnp.int32, (CHUNK, LANES), 0)
    for t, width in tiles_of(nz):
        part = pl.ds(t * LANES, width)
        here, fresh = new[t]
        rounded = [v.astype(BF16) for v in fresh]
        energy = here[0] * here[0] + here[1] * here[1] + here[2] * here[2]
        if both_steps:
            again = [v.astype(F32) for v in rounded]
            again = again[0] * again[0] + again[1] * again[1] + again[2] * again[2]
            if k == 0:
                again = jnp.where(line == 0, 0.0, again)
            if k == ny - CHUNK:
                again = jnp.where(line == CHUNK - 1, 0.0, again)
            energy = jnp.maximum(energy, again)
        strength[pl.ds(strength_row, CHUNK), part] = energy[:, :width].astype(BF16)
        for c in range(3):
            store(c, part, fresh[c][:, :width], rounded[c][:, :width])
            if k == 0:
                lines(0, c, part, fresh[c][:1, :width])
                blocks(0, c, part, rounded[c][:, :width])
            if k == ny - CHUNK:
                lines(1, c, part, fresh[c][CHUNK - 1 :, :width])
                blocks(1, c, part, rounded[c][:, :width])


def gather(hot, states, z):
    total = None
    for state in states:
        value = jnp.dot(hot, state, preferred_element_type=F32)
        if len(states) > 1:
            value = value * value
        total = value if total is None else total + value
    lane = lax.broadcasted_iota(jnp.int32, total.shape, 1)
    return jnp.max(jnp.where(lane == z, total, 0.0), axis=1, keepdims=True)


def second_middle(pad, nu_pad, packed, visc, after, cells, tap_blocks, slots,
                  s2, blocks, rows, hot_outer, hot_late, z_of, slot_of, peaks, inner, strength, lines, sem):
    _, nx, tiles, _, _ = pad.shape
    ny, nz = inner.shape[2:]

    def layer(x, _):
        for k in range(0, ny, CHUNK):

            def load(f, t, dx, dy):
                window = pl.ds(TOP + k + dy, CHUNK)
                return nu_pad[x + dx, t, window, :] if f == 3 else pad[f, x + dx, t, window, :]

            def store(c, part, value, rounded):
                inner[c, x - 2, k : k + CHUNK, part] = rounded

            def put_block(i, c, part, rounded):
                blocks[i, c, x - 2, :, part] = rounded

            def put_line(i, c, part, value):
                lines[i, c, x - 2, :, part] = value

            def bits(f, part):
                return visc[x, k : k + CHUNK, part] if f == 3 else packed[f, x - 1, k : k + CHUNK, part]

            new = update(load, bits, None, True, nz)
            emit(new, nz, k, ny, store, strength, (x - 2) * ny + k, put_block, put_line, True)
        return 0

    lax.fori_loop(2, nx - 2, layer, 0)
    copy = pltpu.make_async_copy(inner, s2.at[:, 2 : nx - 2], sem)
    copy.start()
    for i in range(2):
        for c in range(3):
            for x in range(nx - 4):
                rows[i, c, x : x + 1, :] = lines[i, c, x]

    taps = cells.shape[1]
    same = lax.broadcasted_iota(jnp.int32, (taps, taps), 0) == lax.broadcasted_iota(jnp.int32, (taps, taps), 1)

    def column_of(line):
        return jnp.sum(jnp.where(same, jnp.broadcast_to(line, same.shape), 0.0), axis=1, keepdims=True)

    def one_hot(column, width):
        position = lax.broadcasted_iota(jnp.int32, (taps, width), 1)
        return jnp.where(position == column.astype(jnp.int32), 1.0, 0.0).astype(BF16)

    cell = cells[...].astype(F32)
    line_rows = jnp.floor((cell + 0.5) * (1.0 / nz))
    line_x = jnp.floor((line_rows + 0.5) * (1.0 / ny))
    line_y = line_rows - line_x * ny
    line_late = jnp.where(line_y == 0, 2 * ny + line_x, jnp.where(line_y == ny - 1, 2 * ny + nx + line_x, -1.0))
    line_late = jnp.where(line_x == 0, line_y, jnp.where(line_x == nx - 1, ny + line_y, line_late))
    row = column_of(line_rows)
    middle = row - 2 * ny
    outer = jnp.where(row < 2 * ny, row, jnp.where(row < (nx - 2) * ny, -1.0, row - (nx - 4) * ny))
    z = column_of(cell - line_rows * nz).astype(jnp.int32)
    z_of[...] = z
    hot_outer[...] = one_hot(outer, hot_outer.shape[1])
    hot_late[...] = one_hot(column_of(line_late), hot_late.shape[1])
    peaks[...] = gather(one_hot(middle, (nx - 4) * ny), [strength[...]], z)
    count = slots.shape[1]
    block = lax.broadcasted_iota(jnp.int32, (taps, count), 1)
    wanted = column_of(tap_blocks[...].astype(F32)).astype(jnp.int32)
    chosen = jnp.where(block == wanted, jnp.broadcast_to(slots[...].astype(F32), (taps, count)), 0.0)
    slot_of[...] = jnp.sum(chosen, axis=1, keepdims=True)
    copy.wait()


def second_outer(pad, nu_pad, packed, visc, own_lo, own_hi, alo, ahi, hot_outer, z_of, peaks_in, s2_in,
                 s2, quasi, extra, rows, blocks, coef_x, coef_y, peaks, edge, edge_bits, ghost_nu, inner, strength, lines, sems):
    _, nx, tiles, _, _ = pad.shape
    ny, nz = inner.shape[3:]
    for side, (own, ghost) in enumerate(((own_lo, alo), (own_hi, ahi))):
        x = (nx - 1) * side
        for k in range(0, ny, CHUNK):
            mine = [own[f, k : k + CHUNK, :].astype(F32) for f in range(4)]
            far = [ghost[f, k : k + CHUNK, :].astype(F32) for f in range(4)]
            terms, far_terms = missing_terms(mine, far, 1.0 if side else -1.0)
            put(ghost_nu, (side,), TOP + k, far[3] * HALF)
            for c in range(3):
                extra[side, c, k : k + CHUNK, :] = far_terms[c]
                for t, width in tiles_of(nz):
                    part = slice(t * LANES, t * LANES + width)
                    window = slice(TOP + k, TOP + k + CHUNK)
                    value = (pad[c, x, t, window, :width] + terms[c][:, part]).astype(BF16)
                    edge[c, side, t, window, :width] = value.astype(F32)
                    edge_bits[c, side, k : k + CHUNK, part] = value
    for row in (0, TOP + ny):
        edge[:, :, :, row : row + TOP, :] = jnp.zeros((3, 2, tiles, TOP, LANES), F32)

    def read(f, x, t, window):
        if f == 3:
            return ghost_nu[0, t, window, :] if x < 0 else ghost_nu[1, t, window, :] if x == nx else nu_pad[x, t, window, :]
        return edge[f, 0, t, window, :] if x == 0 else edge[f, 1, t, window, :] if x == nx - 1 else pad[f, x, t, window, :]

    for side in range(2):
        sign = 1.0 if side else -1.0
        x, beyond = (nx - 1) * side, nx if side else -1
        row, ghost_row = (TOP + ny - 1, TOP + ny) if side else (TOP, TOP - 1)
        for t, width in tiles_of(nz):
            part = pl.ds(t * LANES, width)
            for k in range(0, ny, CHUNK):
                window = slice(TOP + k, TOP + k + CHUNK)
                both = read(3, x, t, window) + read(3, beyond, t, window)
                coef_x[side, k : k + CHUNK, part] = (both - sign * HALF * read(0, x, t, window))[:, :width]
            for y in range(nx):
                window, other = slice(row, row + 1), slice(ghost_row, ghost_row + 1)
                both = read(3, y, t, window) + read(3, y, t, other)
                coef_y[side, y : y + 1, part] = (both - sign * HALF * read(1, y, t, window))[:, :width]

    for side in range(2):
        for j in range(2):
            x = (nx - 1 - j) * side + j * (1 - side)
            for k in range(0, ny, CHUNK):

                def load(f, t, dx, dy):
                    return read(f, x + dx, t, slice(TOP + k + dy, TOP + k + dy + CHUNK))

                def store(c, part, value, rounded):
                    if j:
                        inner[side, c, 0, k : k + CHUNK, part] = rounded
                    else:
                        quasi[side, c, k : k + CHUNK, part] = value

                def put_block(i, c, part, rounded):
                    if j:
                        blocks[i, c, side, :, part] = rounded

                def put_line(i, c, part, value):
                    lines[i, c, 2 * side + j, :, part] = value

                def bits(f, part):
                    if f == 3:
                        return visc[x, k : k + CHUNK, part]
                    return packed[f, x - 1, k : k + CHUNK, part] if j else edge_bits[f, side, k : k + CHUNK, part]

                new = update(load, bits, None if j else side, True, nz)
                strength_row = (2 * side + (1 - j if side else j)) * ny + k
                emit(new, nz, k, ny, store, strength, strength_row, put_block, put_line, j == 1)
    copies = [pltpu.make_async_copy(inner.at[i], s2.at[:, pl.ds(1 + (nx - 3) * i, 1)], sems.at[i]) for i in range(2)]
    for copy in copies:
        copy.start()
    for i in range(2):
        for c in range(3):
            for j in range(4):
                rows[i, c, j : j + 1, :] = lines[i, c, j]
    peaks[...] = jnp.maximum(peaks_in[...], gather(hot_outer[...], [strength[...]], z_of[...]))
    for copy in copies:
        copy.wait()


def second_edges(plo, phi, extra, quasi, coef_x, ylo, yhi, rows_middle, rows_outer, coef_y, blocks_middle, blocks_outer,
                 hot_late, z_of, slot_of, peaks, s2_in, s2, best, layers, strips, late, sems):
    _, _, ny, nz = quasi.shape
    nx = ylo.shape[1]
    copies = []
    added = [[coef_y[i] * g[c].astype(F32) for c in range(3)] for i, g in enumerate((ylo, yhi))]
    line = lax.broadcasted_iota(jnp.int32, (CHUNK, nz), 0)
    for side, ghost in enumerate((plo, phi)):
        x = (nx - 1) * side
        for c in range(3):
            for k in range(0, ny, CHUNK):
                part = slice(k, k + CHUNK)
                far = (ghost[c, part, :].astype(F32) + extra[side, c, part, :]).astype(BF16).astype(F32)
                value = quasi[side, c, part, :] + coef_x[side, part, :] * far
                if k == 0:
                    value = value + jnp.where(line == 0, jnp.broadcast_to(added[0][c][x : x + 1], line.shape), 0.0)
                if k == ny - CHUNK:
                    value = value + jnp.where(line == CHUNK - 1, jnp.broadcast_to(added[1][c][x : x + 1], line.shape), 0.0)
                value = value.astype(BF16)
                layers[side, c, part, :] = value
                late[c, side * ny + k : side * ny + k + CHUNK, :] = value
        copies.append(pltpu.make_async_copy(layers.at[side], s2.at[:, x], sems.at[side]))
        copies[-1].start()
    for c in range(3):
        fixed = []
        for i in range(2):
            outer = rows_outer[i, c]
            base = jnp.concatenate([outer[:2], rows_middle[i, c], outer[3:4], outer[2:3]], axis=0)
            fixed.append(base + added[i][c])
        late[c, 2 * ny : 2 * ny + 2 * nx, :] = jnp.concatenate(fixed, axis=0).astype(BF16)
        for i in range(2):
            for x in range(1, nx - 1):
                fresh = jnp.broadcast_to(fixed[i][x : x + 1], line.shape)
                outer = x == 1 or x == nx - 2
                kept = blocks_outer[i, c, 0 if x == 1 else 1] if outer else blocks_middle[i, c, x - 2]
                strips[i, c, x - 1] = jnp.where(line == (CHUNK - 1) * i, fresh, kept.astype(F32)).astype(BF16)
    for i in range(2):
        place = s2.at[:, 1 : nx - 1, (ny - CHUNK) * i : (ny - CHUNK) * i + CHUNK]
        copies.append(pltpu.make_async_copy(strips.at[i], place, sems.at[2 + i]))
        copies[-1].start()
    last = gather(hot_late[...], [late[c] for c in range(3)], z_of[...])
    peak = jnp.maximum(peaks[...], last)
    slot = lax.broadcasted_iota(jnp.int32, (peak.shape[0], best.shape[0] * best.shape[1]), 1).astype(F32)
    flat = jnp.max(jnp.where(slot == slot_of[...], peak, 0.0), axis=0, keepdims=True)
    owners, each = best.shape
    place = lax.broadcasted_iota(jnp.int32, (owners, owners * each), 1)
    first = each * lax.broadcasted_iota(jnp.int32, (owners, owners * each), 0)
    wide = jnp.broadcast_to(flat, place.shape)
    for j in range(each):
        best[:, j : j + 1] = jnp.max(jnp.where(place == first + j, wide, 0.0), axis=1, keepdims=True)
    for copy in copies:
        copy.wait()


VM = pl.BlockSpec(memory_space=pltpu.VMEM)
HB = pl.BlockSpec(memory_space=pltpu.HBM)


def shape(dims, kind):
    return jax.ShapeDtypeStruct(dims, kind)


FIRST = 10**6
MIDDLE = 8 * 10**9


def call(kernel, ins, outs, scratch, mib, flops, **others):
    return pl.pallas_call(
        kernel,
        out_shape=tuple(o for o, _ in outs),
        in_specs=ins,
        out_specs=[spec for _, spec in outs],
        scratch_shapes=scratch,
        compiler_params=pltpu.CompilerParams(vmem_limit_bytes=mib * 2**20),
        cost_estimate=pl.CostEstimate(flops=flops, bytes_accessed=10**6, transcendentals=0),
        name=kernel.__name__,
        **others,
    )


def body(velocity, viscosity, tap_cell, tap_block, block_slot):
    _, nx, ny, nz = velocity.shape
    taps = tap_cell.shape[1]
    tiles = len(tiles_of(nz))
    tall = TOP + ny + 8
    groups = lax.axis_size(("gx", "gy"))
    each = block_slot.shape[0] // groups
    late_rows = 2 * ny + 2 * nx

    def perms(axis):
        peers = lax.axis_size(axis)
        up = [(i, (i + 1) % peers) for i in range(peers)]
        return up, [(j, i) for i, j in up]

    x_up, x_down = perms("gx")
    y_up, y_down = perms("gy")

    yface = (shape((4, nx, nz), BF16), VM)
    xface = (shape((4, ny, nz), BF16), VM)
    (own_lo,) = call(x_face, [HB] * 2, [xface], [pltpu.SemaphoreType.DMA((2,))], 60, 10**6)(velocity, viscosity)
    ahi = lax.ppermute(own_lo, "gx", x_down)
    own_ylo, own_yhi, own_hi = call(other_faces, [VM] * 2 + [HB], [yface, yface, xface], [], 8, 10**6)(velocity, viscosity, own_lo)
    ylo = lax.ppermute(own_yhi, "gy", y_up)
    yhi = lax.ppermute(own_ylo, "gy", y_down)
    alo = lax.ppermute(own_hi, "gx", x_up)

    face = (shape((3, ny, nz), BF16), VM)
    outs = [
        (shape((3, nx, tiles, tall, LANES), F32), VM),
        (shape((nx, tiles, tall, LANES), F32), VM),
        (shape((3, nx - 2, ny, nz), BF16), VM),
        face,
        face,
        (shape((2, 3, nx, nz), F32), VM),
    ]
    scratch = [pltpu.VMEM((3, nx, tiles, tall, LANES), F32), pltpu.VMEM((2, 3, nx, 1, nz), F32)]
    pad, nu_pad, packed, edge_lo, edge_hi, rows = call(first_step, [VM] * 4, outs, scratch, 28, FIRST)(velocity, viscosity, ylo, yhi)
    plo = lax.ppermute(edge_hi, "gx", x_up)
    phi = lax.ppermute(edge_lo, "gx", x_down)

    whole = (shape((3, nx, ny, nz), BF16), HB)
    column = (shape((taps, 1), F32), VM)
    outs = [
        whole,
        (shape((2, 3, nx - 4, CHUNK, nz), BF16), VM),
        (shape((2, 3, nx - 4, nz), F32), VM),
        (shape((taps, 4 * ny), BF16), VM),
        (shape((taps, late_rows), BF16), VM),
        (shape((taps, 1), jnp.int32), VM),
        column,
        column,
    ]
    scratch = [
        pltpu.VMEM((3, nx - 4, ny, nz), BF16),
        pltpu.VMEM(((nx - 4) * ny, nz), BF16),
        pltpu.VMEM((2, 3, nx - 4, 1, nz), F32),
        pltpu.SemaphoreType.DMA,
    ]
    s2, blocks_middle, rows_middle, hot_outer, hot_late, z_of, slot_of, peaks = call(
        second_middle, [VM] * 4 + [HB] + [VM] * 3, outs, scratch, 28, MIDDLE
    )(pad, nu_pad, packed, viscosity, ahi, tap_cell, tap_block, block_slot[None])

    yface = (shape((3, nx, nz), BF16), VM)
    face_lo, face_hi = call(first_faces, [VM] * 6, [yface, yface], [], 4, 10**6)(rows, own_ylo, own_yhi, alo, ahi, slot_of)
    y2lo = lax.ppermute(face_hi, "gy", y_up)
    y2hi = lax.ppermute(face_lo, "gy", y_down)

    outs = [
        whole,
        (shape((2, 3, ny, nz), F32), VM),
        (shape((2, 3, ny, nz), F32), VM),
        (shape((2, 3, 4, nz), F32), VM),
        (shape((2, 3, 2, CHUNK, nz), BF16), VM),
        (shape((2, ny, nz), F32), VM),
        (shape((2, nx, nz), F32), VM),
        column,
    ]
    scratch = [
        pltpu.VMEM((3, 2, tiles, tall, LANES), F32),
        pltpu.VMEM((3, 2, ny, nz), BF16),
        pltpu.VMEM((2, tiles, tall, LANES), F32),
        pltpu.VMEM((2, 3, 1, ny, nz), BF16),
        pltpu.VMEM((4 * ny, nz), BF16),
        pltpu.VMEM((2, 3, 4, 1, nz), F32),
        pltpu.SemaphoreType.DMA((2,)),
    ]
    s2, quasi, extra, rows_outer, blocks_outer, coef_x, coef_y, peaks = call(
        second_outer, [VM] * 11 + [HB], outs, scratch, 28, 10**6, input_output_aliases={11: 0}
    )(pad, nu_pad, packed, viscosity, own_lo, own_hi, alo, ahi, hot_outer, z_of, peaks, s2)

    scratch = [
        pltpu.VMEM((2, 3, ny, nz), BF16),
        pltpu.VMEM((2, 3, nx - 2, CHUNK, nz), BF16),
        pltpu.VMEM((3, late_rows, nz), BF16),
        pltpu.SemaphoreType.DMA((4,)),
    ]
    new_velocity, best = call(
        second_edges, [VM] * 16 + [HB], [whole, (shape((groups, each), F32), VM)], scratch, 16, 10**6, input_output_aliases={16: 0}
    )(plo, phi, extra, quasi, coef_x, y2lo, y2hi, rows_middle, rows_outer, coef_y, blocks_middle, blocks_outer,
      hot_late, z_of, slot_of, peaks, s2)

    received = lax.all_to_all(best, ("gx", "gy"), split_axis=0, concat_axis=0, tiled=True)
    return new_velocity, jnp.max(received, axis=0)


def solution(mesh):
    placed = (
        P(None, "gx", "gy", None),
        P("gx", "gy", None),
        P(("gx", "gy"), None),
        P(("gx", "gy"), None),
        P(),
    )
    return jax.shard_map(
        body,
        mesh=mesh,
        in_specs=placed,
        out_specs=(P(None, "gx", "gy", None), P(("gx", "gy"))),
        check_vma=False,
    )
```

time: 116 us -> 57.5 us (0.50)
  other arithmetic: 39.1 us -> 0.66 us
  waiting for transfers between devices: 26.6 us -> 3.44 us
  Pallas kernels: 0 us -> 15.5 us
  local copies, waits for them, and re-layouts: 14.7 us -> 1.03 us
  starting transfers between devices: 16.6 us -> 19.7 us
  blocking collectives: 18.2 us -> 16.3 us
    ppermute x8, waiting for transfers between devices: 26.6 us -> 3.44 us  [the longest x1 2.33 us: body(): yhi = lax.ppermute(own_ylo, 'gy', y_down)]
    another operation x7 -> x0, other arithmetic: 19.8 us -> none  [advance(): return jnp.stack(results, 0)]
    pallas_call x0 -> x7, Pallas kernels: none -> 15.5 us  [the longest x1 4.64 us: body(): call(first_step, [VM] * 4, outs, scratch, 28, FIRST)]
    concatenate x3 -> x0, other arithmetic: 7.38 us -> none  [the longest x1 3.83 us: padded_2(): x = jnp.concatenate([before, x, after], axis=dim)]
    gather x2 -> x0, local copies, waits for them, and re-layouts: 6.75 us -> none  [tap_energy(): return energy[cells]]
    convert_element_type x3 -> x0, other arithmetic: 4.32 us -> none  [the longest x2 4.07 us: advance(): flow = flow_pad.astype(jnp.float32)]
    reduce_sum x2 -> x0, other arithmetic: 3.44 us -> none  [tap_energy(): energy = jnp.sum(jnp.square(state.astype(jnp.float32)), axis=0).reshape(-1)]
    reshape x2 -> x0, local copies, waits for them, and re-layouts: 3.31 us -> none  [tap_energy(): energy = jnp.sum(jnp.square(state.astype(jnp.float32)), axis=0).reshape(-1)]
  transfers between devices with their start and end apart: 8 -> 8, of which waited for: 6 -> 2; matrix products, arithmetic and copies ran while one was open for 8% -> 0% of each run, Pallas kernels for 0% -> 21%
where the time goes in v4:
time: 57.5 us; the launch traced here: 57.4 us
  starting transfers between devices  19.7 us (34%)
  blocking collectives  16.3 us (28%)
  Pallas kernels  15.5 us (27%)
  waiting for transfers between devices  3.44 us (6%)
  local copies, waits for them, and re-layouts  1.03 us (2%)
  between operations  0.79 us (1%)
  other arithmetic  0.66 us (1%)
    all_to_all x1, blocking collectives, body(): lax.all_to_all(best, ('gx', 'gy'), split_axis=0, concat_axis=0, tiled=True)  16.3 us
    ppermute x1, starting transfers between devices, body(): ahi = lax.ppermute(own_lo, 'gx', x_down)  7.12 us
    ppermute x1, starting transfers between devices, body(): phi = lax.ppermute(edge_lo, 'gx', x_down)  5.07 us
    pallas_call x1, Pallas kernels, body(): call(first_step, [VM] * 4, outs, scratch, 28, FIRST)  4.64 us
    ppermute x1, starting transfers between devices, body(): y2hi = lax.ppermute(face_lo, 'gy', y_down)  4.6 us
    pallas_call x1, Pallas kernels, body(): call(second_middle, [VM] * 4 + [HB] + [VM] * 3, outs, scratch, 28, MIDDLE)  3.77 us
    pallas_call x1, Pallas kernels, body(): call(second_outer, [VM] * 11 + [HB], outs, scratch, 28, 10 ** 6, input_ou...  3.44 us
    ppermute x1, waiting for transfers between devices, body(): yhi = lax.ppermute(own_ylo, 'gy', y_down)  2.33 us
  transfers between devices with their start and end apart: 8, of which 2 were waited for; matrix products, arithmetic and copies ran while one was open for 0% of the time, Pallas kernels for 21%

profile of v4, /device:TPU:1, one launch (start us, length us, event | category | flops | bytes accessed | tf_op | source)
XLA Modules:
  0.0 57.4 jit_solution(18443384729880759949)
XLA Ops:
  0.6 0.0 copy-start.1
  0.6 0.0 copy-start
  0.6 1.9 %x_face.1.after.own_lo = bf16[4,64,576]{2,1,0:T(8,128)(2,1)} custom-call(bf16[3,8,64,576]{3,2,1,0:T(8,128)(2,1)} %vel.5, bf16[8,64,576]{2,1,0:T(8,128)(2,1)} %visc.9), custom_call_target="tpu_custom_call" | custom-call | flops 1000000 | bytes 1000000 | tf_op jit(solution)/shard_map/x_face/pallas_call | solution.py:493
  2.6 7.1 %collective-permute-start.5 = (bf16[4,64,576]{2,1,0:T(8,128)(2,1)}, bf16[4,64,576]{2,1,0:T(8,128)(2,1)S(1)}, u32[]{:S(2)}, u32[]{:S(2)}) collective-permute-start(bf16[4,64,576]{2,1,0:T(8,128)(2,1)} %x_face.1.after.own_lo), channel_id=1, source_target_pairs={{16,0},{32,16},{48,32},{64,48},{80,64},{96,80},{112,96},{0,112},{1... | collective-permute-start | bytes 884744 | tf_op jit(solution)/shard_map/ppermute | solution.py:494
  9.7 0.0 copy-done.1
  9.7 0.0 copy-done
  9.7 0.0 copy-start.2
  9.7 1.0 %copy-done.2 = bf16[4,64,576]{2,1,0:T(8,128)(2,1)S(1)} copy-done((bf16[4,64,576]{2,1,0:T(8,128)(2,1)S(1)}, bf16[4,64,576]{2,1,0:T(8,128)(2,1)}, u32[]{:S(2)}) %copy-start.2) | copy-done | bytes 294936
  10.7 0.2 other_faces.1
  10.8 0.0 copy-start.4
  10.8 0.0 copy-start.5
  10.9 0.0 copy-start.6
  10.9 2.2 %collective-permute-start = (bf16[4,8,576]{2,1,0:T(8,128)(2,1)S(1)}, bf16[4,8,576]{2,1,0:T(8,128)(2,1)S(1)}, u32[]{:S(2)}, u32[]{:S(2)}) collective-permute-start(bf16[4,8,576]{2,1,0:T(8,128)(2,1)S(1)} %get-tuple-element.31.own_yhi), channel_id=1, source_target_pairs={{0,1},{1,2},{2,3},{3,4},{4,5},{5,6},{6,7},{7,8},{8,9},{9,10},{10,1... | collective-permute-start | bytes 110600 | tf_op jit(solution)/shard_map/ppermute | solution.py:496
  13.1 0.0 collective-permute-start.1
  13.1 0.0 collective-permute-start.4
  13.1 1.1 %collective-permute-done.ylo = bf16[4,8,576]{2,1,0:T(8,128)(2,1)S(1)} collective-permute-done((bf16[4,8,576]{2,1,0:T(8,128)(2,1)S(1)}, bf16[4,8,576]{2,1,0:T(8,128)(2,1)S(1)}, u32[]{:S(2)}, u32[]{:S(2)}) %collective-permute-start) | collective-permute-done | bytes 36896 | tf_op jit(solution)/shard_map/ppermute | solution.py:496
  14.2 2.3 %collective-permute-done.1.yhi = bf16[4,8,576]{2,1,0:T(8,128)(2,1)S(1)} collective-permute-done((bf16[4,8,576]{2,1,0:T(8,128)(2,1)S(1)}, bf16[4,8,576]{2,1,0:T(8,128)(2,1)S(1)}, u32[]{:S(2)}, u32[]{:S(2)}) %collective-permute-start.1) | collective-permute-done | bytes 36896 | tf_op jit(solution)/shard_map/ppermute | solution.py:497
  16.5 4.6 %first_step.1 = (f32[3,8,5,80,128]{4,3,2,1,0:T(8,128)S(1)}, f32[8,5,80,128]{3,2,1,0:T(8,128)S(1)}, bf16[3,6,64,576]{3,2,1,0:T(8,128)(2,1)S(1)}, bf16[3,64,576]{2...) custom-call(bf16[3,8,64,576]{3,2,1,0:T(8,128)(2,1)S(1)} %copy-done, ...), custom_call_target="tpu_custom_call" | custom-call | flops 1000000 | bytes 1000000 | tf_op jit(solution)/shard_map/first_step/pallas_call | solution.py:510
  21.1 0.1 collective-permute-start.2
  21.2 5.1 %collective-permute-start.3 = (bf16[3,64,576]{2,1,0:T(8,128)(2,1)S(1)}, bf16[3,64,576]{2,1,0:T(8,128)(2,1)S(1)}, u32[]{:S(2)}, u32[]{:S(2)}) collective-permute-start(bf16[3,64,576]{2,1,0:T(8,128)(2,1)S(1)} %get-tuple-element.34), channel_id=1, source_target_pairs={{16,0},{32,16},{48,32},{64,48},{80,64},{96,80},{112,96},{0,112},{1... | collective-permute-start | bytes 663560 | tf_op jit(solution)/shard_map/ppermute | solution.py:512
  26.3 0.0 collective-permute-done.5.after.ahi
  26.3 0.0 copy-done.4
  26.3 0.0 copy-done.5
  26.3 0.0 copy-done.6
  26.3 0.0 copy-start.3
  26.3 3.8 %second_middle.1 = (bf16[3,8,64,576]{3,2,1,0:T(8,128)(2,1)}, bf16[2,3,4,16,576]{4,3,2,1,0:T(8,128)(2,1)S(1)}, f32[2,3,4,576]{3,2,1,0:T(4,128)S(1)}, bf16[320,256...) custom-call(f32[3,8,5,80,128]{4,3,2,1,0:T(8,128)S(1)} %get-tuple-ele, ...), custom_call_target="tpu_custom_call" | custom-call | flops 8000000000 | bytes 1000000 | tf_op jit(solution)/shard_map/second_middle/pallas_call | solution.py:532
  30.1 0.0 collective-permute-done.4.alo
  30.1 0.1 first_faces.1
  30.2 0.6 %collective-permute-start.6 = (bf16[3,8,576]{2,1,0:T(8,128)(2,1)S(1)}, bf16[3,8,576]{2,1,0:T(8,128)(2,1)S(1)}, u32[]{:S(2)}, u32[]{:S(2)}) collective-permute-start(bf16[3,8,576]{2,1,0:T(8,128)(2,1)S(1)} %get-tuple-element.48), channel_id=1, source_target_pairs={{0,1},{1,2},{2,3},{3,4},{4,5},{5,6},{6,7},{7,8},{8,9},{9,10},{10,1... | collective-permute-start | bytes 82952 | tf_op jit(solution)/shard_map/ppermute | solution.py:538
  30.8 4.6 %collective-permute-start.7 = (bf16[3,8,576]{2,1,0:T(8,128)(2,1)S(1)}, bf16[3,8,576]{2,1,0:T(8,128)(2,1)S(1)}, u32[]{:S(2)}, u32[]{:S(2)}) collective-permute-start(bf16[3,8,576]{2,1,0:T(8,128)(2,1)S(1)} %get-tuple-element.49), channel_id=1, source_target_pairs={{1,0},{2,1},{3,2},{4,3},{5,4},{6,5},{7,6},{8,7},{9,8},{10,9},{11,1... | collective-permute-start | bytes 82952 | tf_op jit(solution)/shard_map/ppermute | solution.py:539
  35.5 0.0 copy-done.3
  35.5 3.4 %second_outer.1 = (bf16[3,8,64,576]{3,2,1,0:T(8,128)(2,1)}, f32[2,3,64,576]{3,2,1,0:T(8,128)S(1)}, f32[2,3,64,576]{3,2,1,0:T(8,128)S(1)}, f32[2,3,4,576]{3,2,1,0...) custom-call(f32[3,8,5,80,128]{4,3,2,1,0:T(8,128)S(1)} %get-tuple-ele, ...), custom_call_target="tpu_custom_call", output_to_operand_aliasing={{0}: (11, {})} | custom-call | flops 1000000 | bytes 1000000 | tf_op jit(solution)/shard_map/second_outer/pallas_call | solution.py:560
  38.9 0.0 collective-permute-done.2.plo
  38.9 0.0 collective-permute-done.3.phi
  38.9 0.0 collective-permute-done.6.ylo
  38.9 0.0 collective-permute-done.7.yhi
  38.9 1.5 %second_edges.1 = (bf16[3,8,64,576]{3,2,1,0:T(8,128)(2,1)}, f32[128,4]{1,0:T(8,128)S(1)}) custom-call(bf16[3,64,576]{2,1,0:T(8,128)(2,1)S(1)} %collective-permute-done.2.plo, bf16[3,64,576]{2,1,0:T(8,128)(2,1)S(1)} %collective-permute-done.3.phi, f32[2,3,64,576]{3,2,1,0:T(8,128)S(1)} %get-tuple-element.43.extra, ...), custom_call_target="tpu_custom_call", output_to_operand_aliasing={{0}: (16, {})} | custom-call | flops 1000000 | bytes 1000000 | tf_op jit(solution)/shard_map/second_edges/pallas_call | solution.py:570
  40.4 16.3 %all_to_all.9 = f32[128,1,4]{2,1,0:T(1,128)S(1)} all-to-all(f32[128,1,4]{2,1,0:T(1,128)S(1)} %bitcast.4), channel_id=1, replica_groups=mesh['gx'=8,'gy'=16] {'gx','gy'}, dimensions={0} | all-to-all | bytes 4096 | tf_op jit(solution)/shard_map/all_to_all | solution.py:575
  56.7 0.7 %reduce_max.9 = f32[4]{0:T(128)} reduce(f32[128,1,4]{2,1,0:T(1,128)S(1)} %all_to_all.9, f32[]{:T(128)} %constant.0.clone.1), dimensions={0,1}, to_apply=%region_0.0 | reduce | flops 508 | bytes 2068 | tf_op jit(solution)/shard_map/reduce_max | solution.py:576
Async XLA Ops:
  0.6 9.0 %copy-start.1 = (bf16[8,64,576]{2,1,0:T(8,128)(2,1)S(1)}, bf16[8,64,576]{2,1,0:T(8,128)(2,1)}, u32[]{:S(2)}) copy-start(bf16[8,64,576]{2,1,0:T(8,128)(2,1)} %visc.9) | copy-start | bytes 1769476
  0.6 9.0 %copy-start = (bf16[3,8,64,576]{3,2,1,0:T(8,128)(2,1)S(1)}, bf16[3,8,64,576]{3,2,1,0:T(8,128)(2,1)}, u32[]{:S(2)}) copy-start(bf16[3,8,64,576]{3,2,1,0:T(8,128)(2,1)} %vel.5) | copy-start | bytes 5308420
  2.6 23.7 %collective-permute-start.5 = (bf16[4,64,576]{2,1,0:T(8,128)(2,1)}, bf16[4,64,576]{2,1,0:T(8,128)(2,1)S(1)}, u32[]{:S(2)}, u32[]{:S(2)}) collective-permute-start(bf16[4,64,576]{2,1,0:T(8,128)(2,1)} %x_face.1.after.own_lo), channel_id=1, source_target_pairs={{16,0},{32,16},{48,32},{64,48},{80,64},{96,80},{112,96},{0,112},{1... | collective-permute-start | bytes 884744 | tf_op jit(solution)/shard_map/ppermute | solution.py:494
  9.7 1.0 %copy-start.2 = (bf16[4,64,576]{2,1,0:T(8,128)(2,1)S(1)}, bf16[4,64,576]{2,1,0:T(8,128)(2,1)}, u32[]{:S(2)}) copy-start(bf16[4,64,576]{2,1,0:T(8,128)(2,1)} %x_face.1.after.own_lo) | copy-start | bytes 884740
  10.8 15.5 %copy-start.4 = (s32[512]{0:T(512)S(1)}, s32[512]{0:T(512)}, u32[]{:S(2)}) copy-start(s32[512]{0:T(512)} %param.9) | copy-start | bytes 6148
  10.8 15.5 %copy-start.5 = (s32[1,320]{1,0:T(1,128)S(1)}, s32[1,320]{1,0:T(1,128)}, u32[]{:S(2)}) copy-start(s32[1,320]{1,0:T(1,128)} %cells.1) | copy-start | bytes 3844
  10.9 15.5 %copy-start.6 = (s32[1,320]{1,0:T(1,128)S(1)}, s32[1,320]{1,0:T(1,128)}, u32[]{:S(2)}) copy-start(s32[1,320]{1,0:T(1,128)} %tap_blocks.1) | copy-start | bytes 3844
  10.9 3.3 %collective-permute-start = (bf16[4,8,576]{2,1,0:T(8,128)(2,1)S(1)}, bf16[4,8,576]{2,1,0:T(8,128)(2,1)S(1)}, u32[]{:S(2)}, u32[]{:S(2)}) collective-permute-start(bf16[4,8,576]{2,1,0:T(8,128)(2,1)S(1)} %get-tuple-element.31.own_yhi), channel_id=1, source_target_pairs={{0,1},{1,2},{2,3},{3,4},{4,5},{5,6},{6,7},{7,8},{8,9},{9,10},{10,1... | collective-permute-start | bytes 110600 | tf_op jit(solution)/shard_map/ppermute | solution.py:496
  13.1 3.4 %collective-permute-start.1 = (bf16[4,8,576]{2,1,0:T(8,128)(2,1)S(1)}, bf16[4,8,576]{2,1,0:T(8,128)(2,1)S(1)}, u32[]{:S(2)}, u32[]{:S(2)}) collective-permute-start(bf16[4,8,576]{2,1,0:T(8,128)(2,1)S(1)} %get-tuple-element.32.own_ylo), channel_id=1, source_target_pairs={{1,0},{2,1},{3,2},{4,3},{5,4},{6,5},{7,6},{8,7},{9,8},{10,9},{11,1... | collective-permute-start | bytes 110600 | tf_op jit(solution)/shard_map/ppermute | solution.py:497
  13.1 17.0 %collective-permute-start.4 = (bf16[4,64,576]{2,1,0:T(8,128)(2,1)S(1)}, bf16[4,64,576]{2,1,0:T(8,128)(2,1)S(1)}, u32[]{:S(2)}, u32[]{:S(2)}) collective-permute-start(bf16[4,64,576]{2,1,0:T(8,128)(2,1)S(1)} %get-tuple-element.38.own_hi), channel_id=1, source_target_pairs={{0,16},{16,32},{32,48},{48,64},{64,80},{80,96},{96,112},{112,0},{1... | collective-permute-start | bytes 884744 | tf_op jit(solution)/shard_map/ppermute | solution.py:498
  21.1 17.8 %collective-permute-start.2 = (bf16[3,64,576]{2,1,0:T(8,128)(2,1)S(1)}, bf16[3,64,576]{2,1,0:T(8,128)(2,1)S(1)}, u32[]{:S(2)}, u32[]{:S(2)}) collective-permute-start(bf16[3,64,576]{2,1,0:T(8,128)(2,1)S(1)} %get-tuple-element.33), channel_id=1, source_target_pairs={{0,16},{16,32},{32,48},{48,64},{64,80},{80,96},{96,112},{112,0},{1... | collective-permute-start | bytes 663560 | tf_op jit(solution)/shard_map/ppermute | solution.py:511
  21.2 17.7 %collective-permute-start.3 = (bf16[3,64,576]{2,1,0:T(8,128)(2,1)S(1)}, bf16[3,64,576]{2,1,0:T(8,128)(2,1)S(1)}, u32[]{:S(2)}, u32[]{:S(2)}) collective-permute-start(bf16[3,64,576]{2,1,0:T(8,128)(2,1)S(1)} %get-tuple-element.34), channel_id=1, source_target_pairs={{16,0},{32,16},{48,32},{64,48},{80,64},{96,80},{112,96},{0,112},{1... | collective-permute-start | bytes 663560 | tf_op jit(solution)/shard_map/ppermute | solution.py:512
  26.3 9.1 %copy-start.3 = (bf16[4,64,576]{2,1,0:T(8,128)(2,1)S(1)}, bf16[4,64,576]{2,1,0:T(8,128)(2,1)}, u32[]{:S(2)}) copy-start(bf16[4,64,576]{2,1,0:T(8,128)(2,1)} %x_face.1.after.own_lo) | copy-start | bytes 884740
  30.2 8.7 %collective-permute-start.6 = (bf16[3,8,576]{2,1,0:T(8,128)(2,1)S(1)}, bf16[3,8,576]{2,1,0:T(8,128)(2,1)S(1)}, u32[]{:S(2)}, u32[]{:S(2)}) collective-permute-start(bf16[3,8,576]{2,1,0:T(8,128)(2,1)S(1)} %get-tuple-element.48), channel_id=1, source_target_pairs={{0,1},{1,2},{2,3},{3,4},{4,5},{5,6},{6,7},{7,8},{8,9},{9,10},{10,1... | collective-permute-start | bytes 82952 | tf_op jit(solution)/shard_map/ppermute | solution.py:538
  30.8 8.1 %collective-permute-start.7 = (bf16[3,8,576]{2,1,0:T(8,128)(2,1)S(1)}, bf16[3,8,576]{2,1,0:T(8,128)(2,1)S(1)}, u32[]{:S(2)}, u32[]{:S(2)}) collective-permute-start(bf16[3,8,576]{2,1,0:T(8,128)(2,1)S(1)} %get-tuple-element.49), channel_id=1, source_target_pairs={{1,0},{2,1},{3,2},{4,3},{5,4},{6,5},{7,6},{8,7},{9,8},{10,9},{11,1... | collective-permute-start | bytes 82952 | tf_op jit(solution)/shard_map/ppermute | solution.py:539

commit v5 on v4

--- a/solution.py
+++ b/solution.py
@@ -492,7 +492,7 @@
     xface = (shape((4, ny, nz), BF16), VM)
     (own_lo,) = call(x_face, [HB] * 2, [xface], [pltpu.SemaphoreType.DMA((2,))], 60, 10**6)(velocity, viscosity)
     ahi = lax.ppermute(own_lo, "gx", x_down)
-    own_ylo, own_yhi, own_hi = call(other_faces, [VM] * 2 + [HB], [yface, yface, xface], [], 8, 10**6)(velocity, viscosity, own_lo)
+    own_ylo, own_yhi, own_hi = call(other_faces, [VM] * 2 + [HB], [yface, yface, xface], [], 8, 10**6)(velocity, viscosity, tap_cell)
     ylo = lax.ppermute(own_yhi, "gy", y_up)
     yhi = lax.ppermute(own_ylo, "gy", y_down)
     alo = lax.ppermute(own_hi, "gx", x_up)

time: 57.5 us -> 57.2 us (level)
  local copies, waits for them, and re-layouts: 1.03 us -> 0.03 us
  starting transfers between devices: 19.7 us -> 20.6 us
    ppermute x1, starting transfers between devices: 4.6 us -> 5.61 us  [body(): y2hi = lax.ppermute(face_lo, 'gy', y_down)]
    unnamed x14 -> x12, local copies, waits for them, and re-layouts: 1.03 us -> 0.03 us
where the time goes in v5:
time: 57.2 us; the launch traced here: 57.1 us
  starting transfers between devices  20.6 us (36%)
  blocking collectives  16.3 us (28%)
  Pallas kernels  15.2 us (27%)
  waiting for transfers between devices  3.52 us (6%)
  between operations  0.79 us (1%)
  other arithmetic  0.66 us (1%)
    all_to_all x1, blocking collectives, body(): lax.all_to_all(best, ('gx', 'gy'), split_axis=0, concat_axis=0, tiled=True)  16.3 us
    ppermute x1, starting transfers between devices, body(): ahi = lax.ppermute(own_lo, 'gx', x_down)  7.12 us
    ppermute x1, starting transfers between devices, body(): y2hi = lax.ppermute(face_lo, 'gy', y_down)  5.61 us
    ppermute x1, starting transfers between devices, body(): phi = lax.ppermute(edge_lo, 'gx', x_down)  5.07 us
    pallas_call x1, Pallas kernels, body(): call(first_step, [VM] * 4, outs, scratch, 28, FIRST)  4.48 us
    pallas_call x1, Pallas kernels, body(): call(second_middle, [VM] * 4 + [HB] + [VM] * 3, outs, scratch, 28, MIDDLE)  3.7 us
    pallas_call x1, Pallas kernels, body(): call(second_outer, [VM] * 11 + [HB], outs, scratch, 28, 10 ** 6, input_ou...  3.39 us
    ppermute x1, waiting for transfers between devices, body(): yhi = lax.ppermute(own_ylo, 'gy', y_down)  2.41 us
  transfers between devices with their start and end apart: 8, of which 2 were waited for; matrix products, arithmetic and copies ran while one was open for 0% of the time, Pallas kernels for 21%

profile of v5, /device:TPU:1, one launch (start us, length us, event | category | flops | bytes accessed | tf_op | source)
XLA Modules:
  0.0 57.1 jit_solution(2733386031210871081)
XLA Ops:
  0.6 0.0 copy-start.1
  0.6 0.0 copy-start
  0.6 0.0 copy-start.3
  0.7 1.9 %x_face.1.own_lo = bf16[4,64,576]{2,1,0:T(8,128)(2,1)} custom-call(bf16[3,8,64,576]{3,2,1,0:T(8,128)(2,1)} %vel.5, bf16[8,64,576]{2,1,0:T(8,128)(2,1)} %visc.9), custom_call_target="tpu_custom_call" | custom-call | flops 1000000 | bytes 1000000 | tf_op jit(solution)/shard_map/x_face/pallas_call | solution.py:493
  2.6 7.1 %collective-permute-start.5 = (bf16[4,64,576]{2,1,0:T(8,128)(2,1)}, bf16[4,64,576]{2,1,0:T(8,128)(2,1)S(1)}, u32[]{:S(2)}, u32[]{:S(2)}) collective-permute-start(bf16[4,64,576]{2,1,0:T(8,128)(2,1)} %x_face.1.own_lo), channel_id=1, source_target_pairs={{16,0},{32,16},{48,32},{64,48},{80,64},{96,80},{112,96},{0,112},{1... | collective-permute-start | bytes 884744 | tf_op jit(solution)/shard_map/ppermute | solution.py:494
  9.7 0.0 copy-done.1
  9.7 0.0 copy-done
  9.7 0.0 copy-done.3
  9.7 0.2 other_faces.1
  9.8 0.0 copy-start.4
  9.9 0.0 copy-start.5
  9.9 2.2 %collective-permute-start = (bf16[4,8,576]{2,1,0:T(8,128)(2,1)S(1)}, bf16[4,8,576]{2,1,0:T(8,128)(2,1)S(1)}, u32[]{:S(2)}, u32[]{:S(2)}) collective-permute-start(bf16[4,8,576]{2,1,0:T(8,128)(2,1)S(1)} %get-tuple-element.31.own_yhi), channel_id=1, source_target_pairs={{0,1},{1,2},{2,3},{3,4},{4,5},{5,6},{6,7},{7,8},{8,9},{9,10},{10,1... | collective-permute-start | bytes 110600 | tf_op jit(solution)/shard_map/ppermute | solution.py:496
  12.1 0.0 collective-permute-start.1
  12.1 0.0 collective-permute-start.4
  12.1 1.1 %collective-permute-done.ylo = bf16[4,8,576]{2,1,0:T(8,128)(2,1)S(1)} collective-permute-done((bf16[4,8,576]{2,1,0:T(8,128)(2,1)S(1)}, bf16[4,8,576]{2,1,0:T(8,128)(2,1)S(1)}, u32[]{:S(2)}, u32[]{:S(2)}) %collective-permute-start) | collective-permute-done | bytes 36896 | tf_op jit(solution)/shard_map/ppermute | solution.py:496
  13.2 2.4 %collective-permute-done.1.yhi = bf16[4,8,576]{2,1,0:T(8,128)(2,1)S(1)} collective-permute-done((bf16[4,8,576]{2,1,0:T(8,128)(2,1)S(1)}, bf16[4,8,576]{2,1,0:T(8,128)(2,1)S(1)}, u32[]{:S(2)}, u32[]{:S(2)}) %collective-permute-start.1) | collective-permute-done | bytes 36896 | tf_op jit(solution)/shard_map/ppermute | solution.py:497
  15.6 4.5 %first_step.1 = (f32[3,8,5,80,128]{4,3,2,1,0:T(8,128)S(1)}, f32[8,5,80,128]{3,2,1,0:T(8,128)S(1)}, bf16[3,6,64,576]{3,2,1,0:T(8,128)(2,1)S(1)}, bf16[3,64,576]{2...) custom-call(bf16[3,8,64,576]{3,2,1,0:T(8,128)(2,1)S(1)} %copy-done, ...), custom_call_target="tpu_custom_call" | custom-call | flops 1000000 | bytes 1000000 | tf_op jit(solution)/shard_map/first_step/pallas_call | solution.py:510
  20.1 0.1 collective-permute-start.2
  20.1 5.1 %collective-permute-start.3 = (bf16[3,64,576]{2,1,0:T(8,128)(2,1)S(1)}, bf16[3,64,576]{2,1,0:T(8,128)(2,1)S(1)}, u32[]{:S(2)}, u32[]{:S(2)}) collective-permute-start(bf16[3,64,576]{2,1,0:T(8,128)(2,1)S(1)} %get-tuple-element.34), channel_id=1, source_target_pairs={{16,0},{32,16},{48,32},{64,48},{80,64},{96,80},{112,96},{0,112},{1... | collective-permute-start | bytes 663560 | tf_op jit(solution)/shard_map/ppermute | solution.py:512
  25.2 0.0 collective-permute-done.5.after.ahi
  25.2 0.0 copy-done.4
  25.2 0.0 copy-done.5
  25.2 0.0 copy-start.2
  25.2 3.7 %second_middle.1 = (bf16[3,8,64,576]{3,2,1,0:T(8,128)(2,1)}, bf16[2,3,4,16,576]{4,3,2,1,0:T(8,128)(2,1)S(1)}, f32[2,3,4,576]{3,2,1,0:T(4,128)S(1)}, bf16[320,256...) custom-call(f32[3,8,5,80,128]{4,3,2,1,0:T(8,128)S(1)} %get-tuple-ele, ...), custom_call_target="tpu_custom_call" | custom-call | flops 8000000000 | bytes 1000000 | tf_op jit(solution)/shard_map/second_middle/pallas_call | solution.py:532
  28.9 0.0 collective-permute-done.4.alo
  29.0 0.1 first_faces.1
  29.0 0.6 collective-permute-start.6
  29.6 5.6 %collective-permute-start.7 = (bf16[3,8,576]{2,1,0:T(8,128)(2,1)S(1)}, bf16[3,8,576]{2,1,0:T(8,128)(2,1)S(1)}, u32[]{:S(2)}, u32[]{:S(2)}) collective-permute-start(bf16[3,8,576]{2,1,0:T(8,128)(2,1)S(1)} %get-tuple-element.49), channel_id=1, source_target_pairs={{1,0},{2,1},{3,2},{4,3},{5,4},{6,5},{7,6},{8,7},{9,8},{10,9},{11,1... | collective-permute-start | bytes 82952 | tf_op jit(solution)/shard_map/ppermute | solution.py:539
  35.2 0.0 copy-done.2
  35.2 3.4 %second_outer.1 = (bf16[3,8,64,576]{3,2,1,0:T(8,128)(2,1)}, f32[2,3,64,576]{3,2,1,0:T(8,128)S(1)}, f32[2,3,64,576]{3,2,1,0:T(8,128)S(1)}, f32[2,3,4,576]{3,2,1,0...) custom-call(f32[3,8,5,80,128]{4,3,2,1,0:T(8,128)S(1)} %get-tuple-ele, ...), custom_call_target="tpu_custom_call", output_to_operand_aliasing={{0}: (11, {})} | custom-call | flops 1000000 | bytes 1000000 | tf_op jit(solution)/shard_map/second_outer/pallas_call | solution.py:560
  38.6 0.0 collective-permute-done.2.plo
  38.6 0.0 collective-permute-done.3.phi
  38.6 0.0 collective-permute-done.6.ylo
  38.6 0.0 collective-permute-done.7.yhi
  38.7 1.5 %second_edges.1 = (bf16[3,8,64,576]{3,2,1,0:T(8,128)(2,1)}, f32[128,4]{1,0:T(8,128)S(1)}) custom-call(bf16[3,64,576]{2,1,0:T(8,128)(2,1)S(1)} %collective-permute-done.2.plo, bf16[3,64,576]{2,1,0:T(8,128)(2,1)S(1)} %collective-permute-done.3.phi, f32[2,3,64,576]{3,2,1,0:T(8,128)S(1)} %get-tuple-element.43.extra, ...), custom_call_target="tpu_custom_call", output_to_operand_aliasing={{0}: (16, {})} | custom-call | flops 1000000 | bytes 1000000 | tf_op jit(solution)/shard_map/second_edges/pallas_call | solution.py:570
  40.1 16.3 %all_to_all.9 = f32[128,1,4]{2,1,0:T(1,128)S(1)} all-to-all(f32[128,1,4]{2,1,0:T(1,128)S(1)} %bitcast.4), channel_id=1, replica_groups=mesh['gx'=8,'gy'=16] {'gx','gy'}, dimensions={0} | all-to-all | bytes 4096 | tf_op jit(solution)/shard_map/all_to_all | solution.py:575
  56.4 0.7 %reduce_max.9 = f32[4]{0:T(128)} reduce(f32[128,1,4]{2,1,0:T(1,128)S(1)} %all_to_all.9, f32[]{:T(128)} %constant.0.clone.1), dimensions={0,1}, to_apply=%region_0.0 | reduce | flops 508 | bytes 2068 | tf_op jit(solution)/shard_map/reduce_max | solution.py:576
Async XLA Ops:
  0.6 9.0 %copy-start.1 = (bf16[8,64,576]{2,1,0:T(8,128)(2,1)S(1)}, bf16[8,64,576]{2,1,0:T(8,128)(2,1)}, u32[]{:S(2)}) copy-start(bf16[8,64,576]{2,1,0:T(8,128)(2,1)} %visc.9) | copy-start | bytes 1769476
  0.6 9.0 %copy-start = (bf16[3,8,64,576]{3,2,1,0:T(8,128)(2,1)S(1)}, bf16[3,8,64,576]{3,2,1,0:T(8,128)(2,1)}, u32[]{:S(2)}) copy-start(bf16[3,8,64,576]{3,2,1,0:T(8,128)(2,1)} %vel.5) | copy-start | bytes 5308420
  0.6 9.0 %copy-start.3 = (s32[1,320]{1,0:T(1,128)S(1)}, s32[1,320]{1,0:T(1,128)}, u32[]{:S(2)}) copy-start(s32[1,320]{1,0:T(1,128)} %cells.1) | copy-start | bytes 3844
  2.6 22.7 %collective-permute-start.5 = (bf16[4,64,576]{2,1,0:T(8,128)(2,1)}, bf16[4,64,576]{2,1,0:T(8,128)(2,1)S(1)}, u32[]{:S(2)}, u32[]{:S(2)}) collective-permute-start(bf16[4,64,576]{2,1,0:T(8,128)(2,1)} %x_face.1.own_lo), channel_id=1, source_target_pairs={{16,0},{32,16},{48,32},{64,48},{80,64},{96,80},{112,96},{0,112},{1... | collective-permute-start | bytes 884744 | tf_op jit(solution)/shard_map/ppermute | solution.py:494
  9.8 15.4 %copy-start.4 = (s32[512]{0:T(512)S(1)}, s32[512]{0:T(512)}, u32[]{:S(2)}) copy-start(s32[512]{0:T(512)} %param.9) | copy-start | bytes 6148
  9.9 15.4 %copy-start.5 = (s32[1,320]{1,0:T(1,128)S(1)}, s32[1,320]{1,0:T(1,128)}, u32[]{:S(2)}) copy-start(s32[1,320]{1,0:T(1,128)} %tap_blocks.1) | copy-start | bytes 3844
  9.9 3.3 %collective-permute-start = (bf16[4,8,576]{2,1,0:T(8,128)(2,1)S(1)}, bf16[4,8,576]{2,1,0:T(8,128)(2,1)S(1)}, u32[]{:S(2)}, u32[]{:S(2)}) collective-permute-start(bf16[4,8,576]{2,1,0:T(8,128)(2,1)S(1)} %get-tuple-element.31.own_yhi), channel_id=1, source_target_pairs={{0,1},{1,2},{2,3},{3,4},{4,5},{5,6},{6,7},{7,8},{8,9},{9,10},{10,1... | collective-permute-start | bytes 110600 | tf_op jit(solution)/shard_map/ppermute | solution.py:496
  12.1 3.5 %collective-permute-start.1 = (bf16[4,8,576]{2,1,0:T(8,128)(2,1)S(1)}, bf16[4,8,576]{2,1,0:T(8,128)(2,1)S(1)}, u32[]{:S(2)}, u32[]{:S(2)}) collective-permute-start(bf16[4,8,576]{2,1,0:T(8,128)(2,1)S(1)} %get-tuple-element.32.own_ylo), channel_id=1, source_target_pairs={{1,0},{2,1},{3,2},{4,3},{5,4},{6,5},{7,6},{8,7},{9,8},{10,9},{11,1... | collective-permute-start | bytes 110600 | tf_op jit(solution)/shard_map/ppermute | solution.py:497
  12.1 16.9 %collective-permute-start.4 = (bf16[4,64,576]{2,1,0:T(8,128)(2,1)S(1)}, bf16[4,64,576]{2,1,0:T(8,128)(2,1)S(1)}, u32[]{:S(2)}, u32[]{:S(2)}) collective-permute-start(bf16[4,64,576]{2,1,0:T(8,128)(2,1)S(1)} %get-tuple-element.38.own_hi), channel_id=1, source_target_pairs={{0,16},{16,32},{32,48},{48,64},{64,80},{80,96},{96,112},{112,0},{1... | collective-permute-start | bytes 884744 | tf_op jit(solution)/shard_map/ppermute | solution.py:498
  20.1 18.5 %collective-permute-start.2 = (bf16[3,64,576]{2,1,0:T(8,128)(2,1)S(1)}, bf16[3,64,576]{2,1,0:T(8,128)(2,1)S(1)}, u32[]{:S(2)}, u32[]{:S(2)}) collective-permute-start(bf16[3,64,576]{2,1,0:T(8,128)(2,1)S(1)} %get-tuple-element.33), channel_id=1, source_target_pairs={{0,16},{16,32},{32,48},{48,64},{64,80},{80,96},{96,112},{112,0},{1... | collective-permute-start | bytes 663560 | tf_op jit(solution)/shard_map/ppermute | solution.py:511
  20.1 18.5 %collective-permute-start.3 = (bf16[3,64,576]{2,1,0:T(8,128)(2,1)S(1)}, bf16[3,64,576]{2,1,0:T(8,128)(2,1)S(1)}, u32[]{:S(2)}, u32[]{:S(2)}) collective-permute-start(bf16[3,64,576]{2,1,0:T(8,128)(2,1)S(1)} %get-tuple-element.34), channel_id=1, source_target_pairs={{16,0},{32,16},{48,32},{64,48},{80,64},{96,80},{112,96},{0,112},{1... | collective-permute-start | bytes 663560 | tf_op jit(solution)/shard_map/ppermute | solution.py:512
  25.2 10.0 %copy-start.2 = (bf16[4,64,576]{2,1,0:T(8,128)(2,1)S(1)}, bf16[4,64,576]{2,1,0:T(8,128)(2,1)}, u32[]{:S(2)}) copy-start(bf16[4,64,576]{2,1,0:T(8,128)(2,1)} %x_face.1.own_lo) | copy-start | bytes 884740
  29.0 9.6 %collective-permute-start.6 = (bf16[3,8,576]{2,1,0:T(8,128)(2,1)S(1)}, bf16[3,8,576]{2,1,0:T(8,128)(2,1)S(1)}, u32[]{:S(2)}, u32[]{:S(2)}) collective-permute-start(bf16[3,8,576]{2,1,0:T(8,128)(2,1)S(1)} %get-tuple-element.48), channel_id=1, source_target_pairs={{0,1},{1,2},{2,3},{3,4},{4,5},{5,6},{6,7},{7,8},{8,9},{9,10},{10,1... | collective-permute-start | bytes 82952 | tf_op jit(solution)/shard_map/ppermute | solution.py:538
  29.6 9.0 %collective-permute-start.7 = (bf16[3,8,576]{2,1,0:T(8,128)(2,1)S(1)}, bf16[3,8,576]{2,1,0:T(8,128)(2,1)S(1)}, u32[]{:S(2)}, u32[]{:S(2)}) collective-permute-start(bf16[3,8,576]{2,1,0:T(8,128)(2,1)S(1)} %get-tuple-element.49), channel_id=1, source_target_pairs={{1,0},{2,1},{3,2},{4,3},{5,4},{6,5},{7,6},{8,7},{9,8},{10,9},{11,1... | collective-permute-start | bytes 82952 | tf_op jit(solution)/shard_map/ppermute | solution.py:539

commit v6 on v5

--- a/solution.py
+++ b/solution.py
@@ -229,15 +229,10 @@
                 blocks(1, c, part, rounded[c][:, :width])
 
 
-def gather(hot, states, z):
-    total = None
-    for state in states:
-        value = jnp.dot(hot, state, preferred_element_type=F32)
-        if len(states) > 1:
-            value = value * value
-        total = value if total is None else total + value
-    lane = lax.broadcasted_iota(jnp.int32, total.shape, 1)
-    return jnp.max(jnp.where(lane == z, total, 0.0), axis=1, keepdims=True)
+def gather(hot, energy, z):
+    picked = jnp.dot(hot, energy, preferred_element_type=F32)
+    lane = lax.broadcasted_iota(jnp.int32, picked.shape, 1)
+    return jnp.max(jnp.where(lane == z, picked, 0.0), axis=1, keepdims=True)
 
 
 def second_middle(pad, nu_pad, packed, visc, after, cells, tap_blocks, slots,
@@ -299,7 +294,7 @@
     z_of[...] = z
     hot_outer[...] = one_hot(outer, hot_outer.shape[1])
     hot_late[...] = one_hot(column_of(line_late), hot_late.shape[1])
-    peaks[...] = gather(one_hot(middle, (nx - 4) * ny), [strength[...]], z)
+    peaks[...] = gather(one_hot(middle, (nx - 4) * ny), strength[...], z)
     count = slots.shape[1]
     block = lax.broadcasted_iota(jnp.int32, (taps, count), 1)
     wanted = column_of(tap_blocks[...].astype(F32)).astype(jnp.int32)
@@ -386,7 +381,7 @@
         for c in range(3):
             for j in range(4):
                 rows[i, c, j : j + 1, :] = lines[i, c, j]
-    peaks[...] = jnp.maximum(peaks_in[...], gather(hot_outer[...], [strength[...]], z_of[...]))
+    peaks[...] = jnp.maximum(peaks_in[...], gather(hot_outer[...], strength[...], z_of[...]))
     for copy in copies:
         copy.wait()
 
@@ -400,9 +395,10 @@
     line = lax.broadcasted_iota(jnp.int32, (CHUNK, nz), 0)
     for side, ghost in enumerate((plo, phi)):
         x = (nx - 1) * side
-        for c in range(3):
-            for k in range(0, ny, CHUNK):
-                part = slice(k, k + CHUNK)
+        for k in range(0, ny, CHUNK):
+            part = slice(k, k + CHUNK)
+            energy = None
+            for c in range(3):
                 far = (ghost[c, part, :].astype(F32) + extra[side, c, part, :]).astype(BF16).astype(F32)
                 value = quasi[side, c, part, :] + coef_x[side, part, :] * far
                 if k == 0:
@@ -411,16 +407,20 @@
                     value = value + jnp.where(line == CHUNK - 1, jnp.broadcast_to(added[1][c][x : x + 1], line.shape), 0.0)
                 value = value.astype(BF16)
                 layers[side, c, part, :] = value
-                late[c, side * ny + k : side * ny + k + CHUNK, :] = value
+                value = value.astype(F32)
+                energy = value * value if c == 0 else energy + value * value
+            late[side * ny + k : side * ny + k + CHUNK, :] = energy.astype(BF16)
         copies.append(pltpu.make_async_copy(layers.at[side], s2.at[:, x], sems.at[side]))
         copies[-1].start()
+    energy = None
     for c in range(3):
         fixed = []
         for i in range(2):
             outer = rows_outer[i, c]
             base = jnp.concatenate([outer[:2], rows_middle[i, c], outer[3:4], outer[2:3]], axis=0)
             fixed.append(base + added[i][c])
-        late[c, 2 * ny : 2 * ny + 2 * nx, :] = jnp.concatenate(fixed, axis=0).astype(BF16)
+        value = jnp.concatenate(fixed, axis=0).astype(BF16).astype(F32)
+        energy = value * value if c == 0 else energy + value * value
         for i in range(2):
             for x in range(1, nx - 1):
                 fresh = jnp.broadcast_to(fixed[i][x : x + 1], line.shape)
@@ -431,7 +431,8 @@
         place = s2.at[:, 1 : nx - 1, (ny - CHUNK) * i : (ny - CHUNK) * i + CHUNK]
         copies.append(pltpu.make_async_copy(strips.at[i], place, sems.at[2 + i]))
         copies[-1].start()
-    last = gather(hot_late[...], [late[c] for c in range(3)], z_of[...])
+    late[2 * ny : 2 * ny + 2 * nx, :] = energy.astype(BF16)
+    last = gather(hot_late[...], late[...], z_of[...])
     peak = jnp.maximum(peaks[...], last)
     slot = lax.broadcasted_iota(jnp.int32, (peak.shape[0], best.shape[0] * best.shape[1]), 1).astype(F32)
     flat = jnp.max(jnp.where(slot == slot_of[...], peak, 0.0), axis=0, keepdims=True)
@@ -443,6 +444,10 @@
         best[:, j : j + 1] = jnp.max(jnp.where(place == first + j, wide, 0.0), axis=1, keepdims=True)
     for copy in copies:
         copy.wait()
+
+
+def final_max(received, highest):
+    highest[...] = jnp.max(received[...], axis=0, keepdims=True)
 
 
 VM = pl.BlockSpec(memory_space=pltpu.VMEM)
@@ -564,7 +569,7 @@
     scratch = [
         pltpu.VMEM((2, 3, ny, nz), BF16),
         pltpu.VMEM((2, 3, nx - 2, CHUNK, nz), BF16),
-        pltpu.VMEM((3, late_rows, nz), BF16),
+        pltpu.VMEM((late_rows, nz), BF16),
         pltpu.SemaphoreType.DMA((4,)),
     ]
     new_velocity, best = call(
@@ -573,7 +578,8 @@
       hot_late, z_of, slot_of, peaks, s2)
 
     received = lax.all_to_all(best, ("gx", "gy"), split_axis=0, concat_axis=0, tiled=True)
-    return new_velocity, jnp.max(received, axis=0)
+    (highest,) = call(final_max, [VM], [(shape((1, each), F32), VM)], [], 4, 10**6)(received)
+    return new_velocity, highest[0]
 
 
 def solution(mesh):

time: 57.2 us -> 57 us (level)
  other arithmetic: 0.66 us -> 0 us
    reduce_max x1 -> x0, other arithmetic: 0.66 us -> none  [body(): return (new_velocity, jnp.max(received, axis=0))]
where the time goes in v6:
time: 57 us; the launch traced here: 56.9 us
  starting transfers between devices  20.6 us (36%)
  blocking collectives  16.3 us (29%)
  Pallas kernels  15.6 us (27%)
  waiting for transfers between devices  3.52 us (6%)
  between operations  0.79 us (1%)
    all_to_all x1, blocking collectives, body(): lax.all_to_all(best, ('gx', 'gy'), split_axis=0, concat_axis=0, tiled=True)  16.3 us
    ppermute x1, starting transfers between devices, body(): ahi = lax.ppermute(own_lo, 'gx', x_down)  7.12 us
    ppermute x1, starting transfers between devices, body(): y2hi = lax.ppermute(face_lo, 'gy', y_down)  5.61 us
    ppermute x1, starting transfers between devices, body(): phi = lax.ppermute(edge_lo, 'gx', x_down)  5.07 us
    pallas_call x1, Pallas kernels, body(): call(first_step, [VM] * 4, outs, scratch, 28, FIRST)  4.48 us
    pallas_call x1, Pallas kernels, body(): call(second_middle, [VM] * 4 + [HB] + [VM] * 3, outs, scratch, 28, MIDDLE)  3.7 us
    pallas_call x1, Pallas kernels, body(): call(second_outer, [VM] * 11 + [HB], outs, scratch, 28, 10 ** 6, input_ou...  3.39 us
    ppermute x1, waiting for transfers between devices, body(): yhi = lax.ppermute(own_ylo, 'gy', y_down)  2.41 us
  transfers between devices with their start and end apart: 8, of which 2 were waited for; matrix products, arithmetic and copies ran while one was open for 0% of the time, Pallas kernels for 21%

profile of v6, /device:TPU:1, one launch (start us, length us, event | category | flops | bytes accessed | tf_op | source)
XLA Modules:
  0.0 56.9 jit_solution(17855741742762977418)
XLA Ops:
  0.6 0.0 copy-start.1
  0.6 0.0 copy-start
  0.6 0.0 copy-start.3
  0.7 1.9 %x_face.1.own_lo = bf16[4,64,576]{2,1,0:T(8,128)(2,1)} custom-call(bf16[3,8,64,576]{3,2,1,0:T(8,128)(2,1)} %vel.5, bf16[8,64,576]{2,1,0:T(8,128)(2,1)} %visc.9), custom_call_target="tpu_custom_call" | custom-call | flops 1000000 | bytes 1000000 | tf_op jit(solution)/shard_map/x_face/pallas_call | solution.py:498
  2.6 7.1 %collective-permute-start.5 = (bf16[4,64,576]{2,1,0:T(8,128)(2,1)}, bf16[4,64,576]{2,1,0:T(8,128)(2,1)S(1)}, u32[]{:S(2)}, u32[]{:S(2)}) collective-permute-start(bf16[4,64,576]{2,1,0:T(8,128)(2,1)} %x_face.1.own_lo), channel_id=1, source_target_pairs={{16,0},{32,16},{48,32},{64,48},{80,64},{96,80},{112,96},{0,112},{1... | collective-permute-start | bytes 884744 | tf_op jit(solution)/shard_map/ppermute | solution.py:499
  9.7 0.0 copy-done.1
  9.7 0.0 copy-done
  9.7 0.0 copy-done.3
  9.7 0.2 other_faces.1
  9.8 0.0 copy-start.4
  9.9 0.0 copy-start.5
  9.9 2.2 %collective-permute-start = (bf16[4,8,576]{2,1,0:T(8,128)(2,1)S(1)}, bf16[4,8,576]{2,1,0:T(8,128)(2,1)S(1)}, u32[]{:S(2)}, u32[]{:S(2)}) collective-permute-start(bf16[4,8,576]{2,1,0:T(8,128)(2,1)S(1)} %get-tuple-element.31.own_yhi), channel_id=1, source_target_pairs={{0,1},{1,2},{2,3},{3,4},{4,5},{5,6},{6,7},{7,8},{8,9},{9,10},{10,1... | collective-permute-start | bytes 110600 | tf_op jit(solution)/shard_map/ppermute | solution.py:501
  12.1 0.0 collective-permute-start.1
  12.1 0.0 collective-permute-start.4
  12.1 1.1 %collective-permute-done.ylo = bf16[4,8,576]{2,1,0:T(8,128)(2,1)S(1)} collective-permute-done((bf16[4,8,576]{2,1,0:T(8,128)(2,1)S(1)}, bf16[4,8,576]{2,1,0:T(8,128)(2,1)S(1)}, u32[]{:S(2)}, u32[]{:S(2)}) %collective-permute-start) | collective-permute-done | bytes 36896 | tf_op jit(solution)/shard_map/ppermute | solution.py:501
  13.2 2.4 %collective-permute-done.1.yhi = bf16[4,8,576]{2,1,0:T(8,128)(2,1)S(1)} collective-permute-done((bf16[4,8,576]{2,1,0:T(8,128)(2,1)S(1)}, bf16[4,8,576]{2,1,0:T(8,128)(2,1)S(1)}, u32[]{:S(2)}, u32[]{:S(2)}) %collective-permute-start.1) | collective-permute-done | bytes 36896 | tf_op jit(solution)/shard_map/ppermute | solution.py:502
  15.6 4.5 %first_step.1 = (f32[3,8,5,80,128]{4,3,2,1,0:T(8,128)S(1)}, f32[8,5,80,128]{3,2,1,0:T(8,128)S(1)}, bf16[3,6,64,576]{3,2,1,0:T(8,128)(2,1)S(1)}, bf16[3,64,576]{2...) custom-call(bf16[3,8,64,576]{3,2,1,0:T(8,128)(2,1)S(1)} %copy-done, ...), custom_call_target="tpu_custom_call" | custom-call | flops 1000000 | bytes 1000000 | tf_op jit(solution)/shard_map/first_step/pallas_call | solution.py:515
  20.1 0.1 collective-permute-start.2
  20.2 5.1 %collective-permute-start.3 = (bf16[3,64,576]{2,1,0:T(8,128)(2,1)S(1)}, bf16[3,64,576]{2,1,0:T(8,128)(2,1)S(1)}, u32[]{:S(2)}, u32[]{:S(2)}) collective-permute-start(bf16[3,64,576]{2,1,0:T(8,128)(2,1)S(1)} %get-tuple-element.34), channel_id=1, source_target_pairs={{16,0},{32,16},{48,32},{64,48},{80,64},{96,80},{112,96},{0,112},{1... | collective-permute-start | bytes 663560 | tf_op jit(solution)/shard_map/ppermute | solution.py:517
  25.2 0.0 collective-permute-done.5.after.ahi
  25.2 0.0 copy-done.4
  25.2 0.0 copy-done.5
  25.2 0.0 copy-start.2
  25.2 3.7 %second_middle.1 = (bf16[3,8,64,576]{3,2,1,0:T(8,128)(2,1)}, bf16[2,3,4,16,576]{4,3,2,1,0:T(8,128)(2,1)S(1)}, f32[2,3,4,576]{3,2,1,0:T(4,128)S(1)}, bf16[320,256...) custom-call(f32[3,8,5,80,128]{4,3,2,1,0:T(8,128)S(1)} %get-tuple-ele, ...), custom_call_target="tpu_custom_call" | custom-call | flops 8000000000 | bytes 1000000 | tf_op jit(solution)/shard_map/second_middle/pallas_call | solution.py:537
  29.0 0.0 collective-permute-done.4.alo
  29.0 0.1 first_faces.1
  29.1 0.6 collective-permute-start.6
  29.6 5.6 %collective-permute-start.7 = (bf16[3,8,576]{2,1,0:T(8,128)(2,1)S(1)}, bf16[3,8,576]{2,1,0:T(8,128)(2,1)S(1)}, u32[]{:S(2)}, u32[]{:S(2)}) collective-permute-start(bf16[3,8,576]{2,1,0:T(8,128)(2,1)S(1)} %get-tuple-element.49), channel_id=1, source_target_pairs={{1,0},{2,1},{3,2},{4,3},{5,4},{6,5},{7,6},{8,7},{9,8},{10,9},{11,1... | collective-permute-start | bytes 82952 | tf_op jit(solution)/shard_map/ppermute | solution.py:544
  35.2 0.0 copy-done.2
  35.2 3.4 %second_outer.1 = (bf16[3,8,64,576]{3,2,1,0:T(8,128)(2,1)}, f32[2,3,64,576]{3,2,1,0:T(8,128)S(1)}, f32[2,3,64,576]{3,2,1,0:T(8,128)S(1)}, f32[2,3,4,576]{3,2,1,0...) custom-call(f32[3,8,5,80,128]{4,3,2,1,0:T(8,128)S(1)} %get-tuple-ele, ...), custom_call_target="tpu_custom_call", output_to_operand_aliasing={{0}: (11, {})} | custom-call | flops 1000000 | bytes 1000000 | tf_op jit(solution)/shard_map/second_outer/pallas_call | solution.py:565
  38.6 0.0 collective-permute-done.2.plo
  38.6 0.0 collective-permute-done.3.phi
  38.6 0.0 collective-permute-done.6.ylo
  38.7 0.0 collective-permute-done.7.yhi
  38.7 1.4 %second_edges.1 = (bf16[3,8,64,576]{3,2,1,0:T(8,128)(2,1)}, f32[128,4]{1,0:T(8,128)S(1)}) custom-call(bf16[3,64,576]{2,1,0:T(8,128)(2,1)S(1)} %collective-permute-done.2.plo, bf16[3,64,576]{2,1,0:T(8,128)(2,1)S(1)} %collective-permute-done.3.phi, f32[2,3,64,576]{3,2,1,0:T(8,128)S(1)} %get-tuple-element.43.extra, ...), custom_call_target="tpu_custom_call", output_to_operand_aliasing={{0}: (16, {})} | custom-call | flops 1000000 | bytes 1000000 | tf_op jit(solution)/shard_map/second_edges/pallas_call | solution.py:575
  40.0 16.3 %all_to_all.11 = f32[128,1,4]{2,1,0:T(1,128)S(1)} all-to-all(f32[128,1,4]{2,1,0:T(1,128)S(1)} %bitcast.7), channel_id=1, replica_groups=mesh['gx'=8,'gy'=16] {'gx','gy'}, dimensions={0} | all-to-all | bytes 4096 | tf_op jit(solution)/shard_map/all_to_all | solution.py:580
  56.3 0.5 final_max.1
Async XLA Ops:
  0.6 9.1 %copy-start.1 = (bf16[8,64,576]{2,1,0:T(8,128)(2,1)S(1)}, bf16[8,64,576]{2,1,0:T(8,128)(2,1)}, u32[]{:S(2)}) copy-start(bf16[8,64,576]{2,1,0:T(8,128)(2,1)} %visc.9) | copy-start | bytes 1769476
  0.6 9.0 %copy-start = (bf16[3,8,64,576]{3,2,1,0:T(8,128)(2,1)S(1)}, bf16[3,8,64,576]{3,2,1,0:T(8,128)(2,1)}, u32[]{:S(2)}) copy-start(bf16[3,8,64,576]{3,2,1,0:T(8,128)(2,1)} %vel.5) | copy-start | bytes 5308420
  0.6 9.0 %copy-start.3 = (s32[1,320]{1,0:T(1,128)S(1)}, s32[1,320]{1,0:T(1,128)}, u32[]{:S(2)}) copy-start(s32[1,320]{1,0:T(1,128)} %cells.1) | copy-start | bytes 3844
  2.6 22.7 %collective-permute-start.5 = (bf16[4,64,576]{2,1,0:T(8,128)(2,1)}, bf16[4,64,576]{2,1,0:T(8,128)(2,1)S(1)}, u32[]{:S(2)}, u32[]{:S(2)}) collective-permute-start(bf16[4,64,576]{2,1,0:T(8,128)(2,1)} %x_face.1.own_lo), channel_id=1, source_target_pairs={{16,0},{32,16},{48,32},{64,48},{80,64},{96,80},{112,96},{0,112},{1... | collective-permute-start | bytes 884744 | tf_op jit(solution)/shard_map/ppermute | solution.py:499
  9.8 15.4 %copy-start.4 = (s32[512]{0:T(512)S(1)}, s32[512]{0:T(512)}, u32[]{:S(2)}) copy-start(s32[512]{0:T(512)} %param.9) | copy-start | bytes 6148
  9.9 15.4 %copy-start.5 = (s32[1,320]{1,0:T(1,128)S(1)}, s32[1,320]{1,0:T(1,128)}, u32[]{:S(2)}) copy-start(s32[1,320]{1,0:T(1,128)} %tap_blocks.1) | copy-start | bytes 3844
  9.9 3.3 %collective-permute-start = (bf16[4,8,576]{2,1,0:T(8,128)(2,1)S(1)}, bf16[4,8,576]{2,1,0:T(8,128)(2,1)S(1)}, u32[]{:S(2)}, u32[]{:S(2)}) collective-permute-start(bf16[4,8,576]{2,1,0:T(8,128)(2,1)S(1)} %get-tuple-element.31.own_yhi), channel_id=1, source_target_pairs={{0,1},{1,2},{2,3},{3,4},{4,5},{5,6},{6,7},{7,8},{8,9},{9,10},{10,1... | collective-permute-start | bytes 110600 | tf_op jit(solution)/shard_map/ppermute | solution.py:501
  12.1 3.5 %collective-permute-start.1 = (bf16[4,8,576]{2,1,0:T(8,128)(2,1)S(1)}, bf16[4,8,576]{2,1,0:T(8,128)(2,1)S(1)}, u32[]{:S(2)}, u32[]{:S(2)}) collective-permute-start(bf16[4,8,576]{2,1,0:T(8,128)(2,1)S(1)} %get-tuple-element.32.own_ylo), channel_id=1, source_target_pairs={{1,0},{2,1},{3,2},{4,3},{5,4},{6,5},{7,6},{8,7},{9,8},{10,9},{11,1... | collective-permute-start | bytes 110600 | tf_op jit(solution)/shard_map/ppermute | solution.py:502
  12.1 16.9 %collective-permute-start.4 = (bf16[4,64,576]{2,1,0:T(8,128)(2,1)S(1)}, bf16[4,64,576]{2,1,0:T(8,128)(2,1)S(1)}, u32[]{:S(2)}, u32[]{:S(2)}) collective-permute-start(bf16[4,64,576]{2,1,0:T(8,128)(2,1)S(1)} %get-tuple-element.38.own_hi), channel_id=1, source_target_pairs={{0,16},{16,32},{32,48},{48,64},{64,80},{80,96},{96,112},{112,0},{1... | collective-permute-start | bytes 884744 | tf_op jit(solution)/shard_map/ppermute | solution.py:503
  20.1 18.5 %collective-permute-start.2 = (bf16[3,64,576]{2,1,0:T(8,128)(2,1)S(1)}, bf16[3,64,576]{2,1,0:T(8,128)(2,1)S(1)}, u32[]{:S(2)}, u32[]{:S(2)}) collective-permute-start(bf16[3,64,576]{2,1,0:T(8,128)(2,1)S(1)} %get-tuple-element.33), channel_id=1, source_target_pairs={{0,16},{16,32},{32,48},{48,64},{64,80},{80,96},{96,112},{112,0},{1... | collective-permute-start | bytes 663560 | tf_op jit(solution)/shard_map/ppermute | solution.py:516
  20.2 18.5 %collective-permute-start.3 = (bf16[3,64,576]{2,1,0:T(8,128)(2,1)S(1)}, bf16[3,64,576]{2,1,0:T(8,128)(2,1)S(1)}, u32[]{:S(2)}, u32[]{:S(2)}) collective-permute-start(bf16[3,64,576]{2,1,0:T(8,128)(2,1)S(1)} %get-tuple-element.34), channel_id=1, source_target_pairs={{16,0},{32,16},{48,32},{64,48},{80,64},{96,80},{112,96},{0,112},{1... | collective-permute-start | bytes 663560 | tf_op jit(solution)/shard_map/ppermute | solution.py:517
  25.2 10.0 %copy-start.2 = (bf16[4,64,576]{2,1,0:T(8,128)(2,1)S(1)}, bf16[4,64,576]{2,1,0:T(8,128)(2,1)}, u32[]{:S(2)}) copy-start(bf16[4,64,576]{2,1,0:T(8,128)(2,1)} %x_face.1.own_lo) | copy-start | bytes 884740
  29.1 9.6 %collective-permute-start.6 = (bf16[3,8,576]{2,1,0:T(8,128)(2,1)S(1)}, bf16[3,8,576]{2,1,0:T(8,128)(2,1)S(1)}, u32[]{:S(2)}, u32[]{:S(2)}) collective-permute-start(bf16[3,8,576]{2,1,0:T(8,128)(2,1)S(1)} %get-tuple-element.48), channel_id=1, source_target_pairs={{0,1},{1,2},{2,3},{3,4},{4,5},{5,6},{6,7},{7,8},{8,9},{9,10},{10,1... | collective-permute-start | bytes 82952 | tf_op jit(solution)/shard_map/ppermute | solution.py:543
  29.6 9.0 %collective-permute-start.7 = (bf16[3,8,576]{2,1,0:T(8,128)(2,1)S(1)}, bf16[3,8,576]{2,1,0:T(8,128)(2,1)S(1)}, u32[]{:S(2)}, u32[]{:S(2)}) collective-permute-start(bf16[3,8,576]{2,1,0:T(8,128)(2,1)S(1)} %get-tuple-element.49), channel_id=1, source_target_pairs={{1,0},{2,1},{3,2},{4,3},{5,4},{6,5},{7,6},{8,7},{9,8},{10,9},{11,1... | collective-permute-start | bytes 82952 | tf_op jit(solution)/shard_map/ppermute | solution.py:544
